TPU v7x, 512 devices: a whole 4x4x16 slice. The times are simulated.
512 devices in a mesh: feat: 32 (over z, core), tok: 16 (over y, x).
Axes of the slice: x: 4, y: 4, z: 16, core: 2. Of those that a mesh axis runs over, the one named last changes fastest.
Arguments:
- enc_rows: bfloat16 [8192, 16384], P('feat', 'tok'), may hold values from -0.75 to 0.75
- dec_rows: bfloat16 [8192, 16384], P('feat', 'tok'), may hold values from -0.046875 to 0.046875
- inputs: bfloat16 [4096, 16384], P('feat', 'tok'), may hold values from -6 to 6
- out_grad: bfloat16 [4096, 16384], P('feat', 'tok'), may hold values from -6 to 6
- destinations: int32 [4096, 2], P('feat'), may hold values from 0 to 31, all different within a row; in each aligned block of 128 rows (0 to 127, 128 to 255, ...) at most 16 rows name the same one
- local_ids: int32 [4096, 2, 32], P('feat'), may hold values from 0 to 255, as said below
- code_values: float32 [4096, 2, 32], P('feat'), may hold values from 0.05 to 2
Outputs:
- enc_grad: bfloat16 [8192, 16384], P('feat', 'tok')
- dec_grad: bfloat16 [8192, 16384], P('feat', 'tok')
- in_grad: bfloat16 [4096, 16384], P('feat', 'tok')
Inputs may be any that keep to these rules, and one draw needn't show every extreme that they name: `destinations`: each row names 2 different feat indices; in each aligned block of 128 rows (the tokens of one feat index) no index is named by more than 16 rows, and one index is named by exactly 16 rows. `local_ids`: the 32 numbers of one token and one h are different.
All inputs are finite; a program needn't handle non-finite values.
Results may differ from a plain program's by a relative error of at most 0.0058.
Values may be sent and summed in bfloat16 or wider, within the bound.
No kernel may reach another device: no remote copies, remote signals or barrier semaphores. Data moves between devices by JAX's collectives and lax.ppermute only.
A program may use at most 64 MiB of HBM per device.

v0:
```python
import jax
import jax.numpy as jnp
from jax import lax
from jax.sharding import PartitionSpec as P


def route_slots(destinations, groups, capacity):
    pair_count = destinations.shape[0] * destinations.shape[1]
    flat_dest = destinations.reshape(pair_count)
    matches = (flat_dest[:, None] == jnp.arange(groups, dtype=jnp.int32)[None, :]).astype(jnp.int32)
    before = jnp.cumsum(matches, axis=0) - matches
    position = jnp.sum(before * matches, axis=1)
    return flat_dest * capacity + position


def decoder_side(recv_grads, recv_ids, recv_codes, dec_rows):
    feat_rows = dec_rows.shape[0]
    feature_line = jnp.arange(feat_rows, dtype=jnp.int32)
    hits = recv_ids[:, :, None] == feature_line[None, None, :]
    partial_value = jnp.einsum(
        "rd,fd->rf", recv_grads, dec_rows, preferred_element_type=jnp.float32
    )
    summed = lax.psum(partial_value, "tok")
    code_grad = jnp.sum(jnp.where(hits, summed[:, None, :], 0.0), axis=2)
    pre_b = code_grad.astype(jnp.bfloat16).astype(jnp.float32)
    code_mat = jnp.sum(
        jnp.where(hits, recv_codes.astype(jnp.float32)[:, :, None], 0.0), axis=1
    ).astype(jnp.bfloat16)
    pre_mat = jnp.sum(jnp.where(hits, pre_b[:, :, None], 0.0), axis=1).astype(jnp.bfloat16)
    dec_grad = jnp.einsum("rf,rd->fd", code_mat, recv_grads, preferred_element_type=jnp.float32)
    return (dec_grad.astype(jnp.bfloat16), pre_mat)


def shards(enc_rows, dec_rows, inputs, out_grad, destinations, local_ids, code_values):
    groups = lax.axis_size("feat")
    tok_rows, hop_count = destinations.shape
    per_hop = local_ids.shape[2]
    width = dec_rows.shape[1]
    capacity = max(2, 2 * tok_rows * hop_count // groups)
    slot_count = groups * capacity
    pair_count = tok_rows * hop_count
    slot_index = route_slots(destinations, groups, capacity)
    pair_token = jnp.arange(pair_count, dtype=jnp.int32) // hop_count
    token_table = jnp.full((slot_count,), tok_rows, jnp.int32).at[slot_index].set(pair_token)
    send_ids = (
        jnp.zeros((slot_count, per_hop), jnp.int32)
        .at[slot_index]
        .set(local_ids.reshape(pair_count, per_hop))
        .reshape(groups, capacity, per_hop)
    )
    send_codes = (
        jnp.zeros((slot_count, per_hop), jnp.bfloat16)
        .at[slot_index]
        .set(code_values.reshape(pair_count, per_hop).astype(jnp.bfloat16))
        .reshape(groups, capacity, per_hop)
    )
    send_grads = jnp.take(out_grad, token_table, axis=0, mode="fill", fill_value=0).reshape(
        groups, capacity, width
    )
    send_inputs = jnp.take(inputs, token_table, axis=0, mode="fill", fill_value=0).reshape(
        groups, capacity, width
    )
    recv_inputs, recv_grads, recv_ids, recv_codes = (
        lax.all_to_all(send_inputs, "feat", split_axis=0, concat_axis=0, tiled=True),
        lax.all_to_all(send_grads, "feat", split_axis=0, concat_axis=0, tiled=True),
        lax.all_to_all(send_ids, "feat", split_axis=0, concat_axis=0, tiled=True),
        lax.all_to_all(send_codes, "feat", split_axis=0, concat_axis=0, tiled=True),
    )
    recv_inputs = recv_inputs.reshape(slot_count, width)
    dec_grad, pre_mat = decoder_side(
        recv_grads.reshape(slot_count, width),
        recv_ids.reshape(slot_count, per_hop),
        recv_codes.reshape(slot_count, per_hop),
        dec_rows,
    )
    enc_grad = jnp.einsum(
        "rf,rd->fd", pre_mat, recv_inputs, preferred_element_type=jnp.float32
    ).astype(jnp.bfloat16)
    back_terms = jnp.dot(pre_mat, enc_rows, preferred_element_type=jnp.float32).astype(jnp.bfloat16)
    returned = lax.all_to_all(
        back_terms.reshape(groups, capacity, width), "feat", split_axis=0, concat_axis=0, tiled=True
    )
    returned = returned.reshape(slot_count, width)
    hop_terms = (
        jnp.take(returned, slot_index, axis=0)
        .astype(jnp.float32)
        .reshape(tok_rows, hop_count, width)
    )
    in_grad = jnp.sum(hop_terms, axis=1).astype(jnp.bfloat16)
    return (enc_grad, dec_grad, in_grad)


def solution(mesh):
    placed = (
        P("feat", "tok"),
        P("feat", "tok"),
        P("feat", "tok"),
        P("feat", "tok"),
        P("feat", None),
        P("feat", None, None),
        P("feat", None, None),
    )
    return jax.shard_map(
        shards,
        mesh=mesh,
        in_specs=placed,
        out_specs=(P("feat", "tok"), P("feat", "tok"), P("feat", "tok")),
        check_vma=False,
    )
```

profile of v0, /device:TPU:1, one launch (start us, length us, event | category | flops | bytes accessed | tf_op | source)
XLA Modules:
  0.0 346.5 jit_solution(5370515748201928644)
XLA Ops:
  7.2 0.9 copy.24
  8.3 0.7 broadcast_multiply_fusion
  9.0 0.6 reduce-window.6
  10.1 0.8 convert_element_type.61
  11.1 1.2 scatter_custom_fusion.2
  12.3 0.8 reshape.186
  13.1 16.7 %all-to-all-start.3 = ((bf16[32,2,256]{2,1,0:T(2,128)(2,1)}), bf16[32,2,256]{2,1,0:T(2,128)(2,1)S(1)}, u32[]{:S(2)}, u32[]{:S(2)}) async-start(bf16[32,2,256]{2,1,0:T(2,128)(2,1)} %reshape.186), calls=%async_computation.3 | async-start | bytes 65536 | tf_op jit(solution)/shard_map/all_to_all | solution.py:67
  29.8 1.4 scatter_custom_fusion.1
  31.3 2.1 gather_fusion.1
  33.4 2.1 gather_fusion.2
  35.6 1.2 scatter_custom_fusion
  36.8 0.8 reshape.188
  37.6 4.3 %all-to-all-done.3 = bf16[32,2,256]{2,1,0:T(2,128)(2,1)S(1)} async-done(((bf16[32,2,256]{2,1,0:T(2,128)(2,1)}), bf16[32,2,256]{2,1,0:T(2,128)(2,1)S(1)}, u32[]{:S(2)}, u32[]{:S(2)}) %all-to-all-start.3) | async-done | bytes 32800 | tf_op jit(solution)/shard_map/all_to_all | solution.py:67
  41.9 7.8 %all-to-all-start = ((s32[32,1,512]{2,1,0:T(1,128)}), s32[32,1,512]{2,1,0:T(1,128)S(1)}, u32[]{:S(2)}, u32[]{:S(2)}) async-start(s32[32,1,512]{2,1,0:T(1,128)} %reshape.188), calls=%async_computation | async-start | bytes 131072 | tf_op jit(solution)/shard_map/all_to_all | solution.py:66
  49.8 1.6 broadcast_select_fusion.1
  51.4 11.5 %all-to-all-done = s32[32,1,512]{2,1,0:T(1,128)S(1)} async-done(((s32[32,1,512]{2,1,0:T(1,128)}), s32[32,1,512]{2,1,0:T(1,128)S(1)}, u32[]{:S(2)}, u32[]{:S(2)}) %all-to-all-start) | async-done | bytes 65568 | tf_op jit(solution)/shard_map/all_to_all | solution.py:66
  62.9 61.0 %all_to_all.25 = bf16[32,16,1024]{2,1,0:T(8,128)(2,1)S(1)} all-to-all(bf16[32,16,1024]{2,1,0:T(8,128)(2,1)} %bitcast.46), channel_id=1, replica_groups=mesh['feat'=32,'tok'=16] {'feat'}, dimensions={0} | all-to-all | bytes 2097152 | tf_op jit(solution)/shard_map/all_to_all | solution.py:65
  123.8 4.8 %all-to-all-start.2 = ((bf16[32,16,1024]{2,1,0:T(8,128)(2,1)}), bf16[32,16,1024]{2,1,0:T(8,128)(2,1)S(1)}, u32[]{:S(2)}, u32[]{:S(2)}) async-start(bf16[32,16,1024]{2,1,0:T(8,128)(2,1)} %bitcast.8), calls=%async_computation.2 | async-start | bytes 2097152 | tf_op jit(solution)/shard_map/all_to_all | solution.py:64
  128.7 1.3 fusion.14
  130.1 0.7 bitcast_convert_fusion
  131.3 0.8 reduce.3
  132.3 116.4 %all-reduce.2.cloned.1.call-done = f32[512,256]{1,0:T(8,128)} async-done(((f32[512,256]{1,0:T(8,128)}), f32[512,256]{1,0:T(8,128)}) %all-reduce.2.cloned.1.call-update) | async-done | bytes 524304 | tf_op jit(solution)/shard_map/psum | solution.py:23
  248.7 6.6 %select_reduce_fusion.2 = bf16[512,32]{1,0:T(8,128)(2,1)S(1)} fusion(f32[512,256]{1,0:T(8,128)} %all-reduce.2.cloned.1.call-done, s32[512,32]{1,0:T(8,128)S(1)} %bitcast.49), kind=kLoop, calls=%fused_computation.8 | loop fusion | flops 12566528 | bytes 622592 | tf_op jit(solution)/shard_map/reduce_sum | solution.py:24
  255.3 8.6 %select_reduce_fusion = (bf16[512,256]{1,0:T(8,128)(2,1)S(1)}, bf16[512,256]{1,0:T(8,128)(2,1)S(1)}) fusion(f32[512,32]{1,0:T(8,128)S(1)} %copy-done.5, s32[512,32]{1,0:T(8,128)S(1)} %bitcast.50, f32[512,32]{1,0:T(8,128)S(1)} %convert_element_type.82), kind=kLoop, calls=%fused_computation.6 | loop fusion | flops 20709376 | bytes 720896 | tf_op jit(solution)/shard_map/reduce_sum | solution.py:26
  263.9 1.5 convolution_convert_fusion
  265.4 1.0 copy-done.3
  266.4 14.3 %all-to-all-start.4 = ((bf16[32,16,1024]{2,1,0:T(8,128)(2,1)}), bf16[32,16,1024]{2,1,0:T(8,128)(2,1)S(1)}, u32[]{:S(2)}, u32[]{:S(2)}) async-start(bf16[32,16,1024]{2,1,0:T(8,128)(2,1)} %bitcast.48), calls=%async_computation.4 | async-start | bytes 2097152 | tf_op jit(solution)/shard_map/all_to_all | solution.py:80
  281.1 1.3 convolution_convert_fusion.1
  282.4 1.3 convolution_convert_fusion.2
  283.7 52.8 %all-to-all-done.4 = bf16[32,16,1024]{2,1,0:T(8,128)(2,1)S(1)} async-done(((bf16[32,16,1024]{2,1,0:T(8,128)(2,1)}), bf16[32,16,1024]{2,1,0:T(8,128)(2,1)S(1)}, u32[]{:S(2)}, u32[]{:S(2)}) %all-to-all-start.4) | async-done | bytes 1048608 | tf_op jit(solution)/shard_map/all_to_all | solution.py:80
  336.5 1.2 gather_fusion
  337.8 1.9 fusion
  (46 shorter events, 2.6 us)
Async XLA Ops:
  7.2 256.8 %copy-start = (bf16[256,1024]{1,0:T(8,128)(2,1)S(1)}, bf16[256,1024]{1,0:T(8,128)(2,1)}, u32[]{:S(2)}) copy-start(bf16[256,1024]{1,0:T(8,128)(2,1)} %param.9) | copy-start | bytes 1572868
  7.2 24.1 %copy-start.1 = (bf16[128,1024]{1,0:T(8,128)(2,1)S(1)}, bf16[128,1024]{1,0:T(8,128)(2,1)}, u32[]{:S(2)}) copy-start(bf16[128,1024]{1,0:T(8,128)(2,1)} %param.12) | copy-start | bytes 786436
  13.1 28.9 %all-to-all-start.3 = ((bf16[32,2,256]{2,1,0:T(2,128)(2,1)}), bf16[32,2,256]{2,1,0:T(2,128)(2,1)S(1)}, u32[]{:S(2)}, u32[]{:S(2)}) async-start(bf16[32,2,256]{2,1,0:T(2,128)(2,1)} %reshape.186), calls=%async_computation.3 | async-start | bytes 65536 | tf_op jit(solution)/shard_map/all_to_all | solution.py:67
  31.3 2.1 copy-start.2
  33.4 2.1 copy-start.7
  41.9 20.9 %all-to-all-start = ((s32[32,1,512]{2,1,0:T(1,128)}), s32[32,1,512]{2,1,0:T(1,128)S(1)}, u32[]{:S(2)}, u32[]{:S(2)}) async-start(s32[32,1,512]{2,1,0:T(1,128)} %reshape.188), calls=%async_computation | async-start | bytes 131072 | tf_op jit(solution)/shard_map/all_to_all | solution.py:66
  123.8 4.8 %copy-start.6 = (bf16[256,1024]{1,0:T(8,128)(2,1)S(1)}, bf16[256,1024]{1,0:T(8,128)(2,1)}, u32[]{:S(2)}) copy-start(bf16[256,1024]{1,0:T(8,128)(2,1)} %param.10) | copy-start | bytes 1572868
  123.8 141.6 %all-to-all-start.2 = ((bf16[32,16,1024]{2,1,0:T(8,128)(2,1)}), bf16[32,16,1024]{2,1,0:T(8,128)(2,1)S(1)}, u32[]{:S(2)}, u32[]{:S(2)}) async-start(bf16[32,16,1024]{2,1,0:T(8,128)(2,1)} %bitcast.8), calls=%async_computation.2 | async-start | bytes 2097152 | tf_op jit(solution)/shard_map/all_to_all | solution.py:64
  128.6 120.1 %all-reduce.2.cloned.1.call-start = ((), (), s32[]{:S(2)}) async-start(), calls=%async_computation.5 | async-start | bytes 1048576 | tf_op jit(solution)/shard_map/psum | solution.py:23
  248.7 6.7 %copy-start.5 = (f32[512,32]{1,0:T(8,128)S(1)}, f32[512,32]{1,0:T(8,128)}, u32[]{:S(2)}) copy-start(f32[512,32]{1,0:T(8,128)} %bitcast_convert_fusion) | copy-start | bytes 196612
  265.4 1.0 copy-start.3
  265.4 15.5 %copy-start.8 = (s32[128,2]{0,1:T(2,128)S(1)}, s32[128,2]{0,1:T(2,128)}, u32[]{:S(2)}) copy-start(s32[128,2]{0,1:T(2,128)} %param.13) | copy-start | bytes 3076
  266.4 70.0 %all-to-all-start.4 = ((bf16[32,16,1024]{2,1,0:T(8,128)(2,1)}), bf16[32,16,1024]{2,1,0:T(8,128)(2,1)S(1)}, u32[]{:S(2)}, u32[]{:S(2)}) async-start(bf16[32,16,1024]{2,1,0:T(8,128)(2,1)} %bitcast.48), calls=%async_computation.4 | async-start | bytes 2097152 | tf_op jit(solution)/shard_map/all_to_all | solution.py:80
  281.1 1.3 copy-start.4
Sparse Core Ops, SparseCore 0:
  133.2 115.3 all-reduce.1
where the time goes:
time: 347 us
  waiting for transfers between devices  185 us (53%)
  blocking collectives  61 us (18%)
  starting transfers between devices  43.7 us (13%)
  other arithmetic  22.4 us (6%)
  local copies, waits for them, and re-layouts  14.8 us (4%)
  between operations  14.3 us (4%)
  matrix products  5.28 us (2%)
    psum x1, waiting for transfers between devices, decoder_side(): summed = lax.psum(partial_value, 'tok')  116 us
    all_to_all x1, blocking collectives, shards(): lax.all_to_all(send_grads, 'feat', split_axis=0, concat_axis=0, tiled=True)  61 us
    all_to_all x1, waiting for transfers between devices, shards(): lax.all_to_all(back_terms.reshape(groups, capacity, width), 'feat', split...  52.8 us
    all_to_all x1, starting transfers between devices, shards(): lax.all_to_all(send_codes, 'feat', split_axis=0, concat_axis=0, tiled=True)  16.7 us
    all_to_all x1, starting transfers between devices, shards(): lax.all_to_all(back_terms.reshape(groups, capacity, width), 'feat', split...  14.3 us
    all_to_all x1, waiting for transfers between devices, shards(): lax.all_to_all(send_ids, 'feat', split_axis=0, concat_axis=0, tiled=True)  11.5 us
    reduce_sum x1, other arithmetic, decoder_side(): jnp.sum(jnp.where(hits, recv_codes.astype(jnp.float32)[:, :, None], 0.0),...  8.6 us
    all_to_all x1, starting transfers between devices, shards(): lax.all_to_all(send_ids, 'feat', split_axis=0, concat_axis=0, tiled=True)  7.85 us
  transfers between devices with their start and end apart: 5, of which 4 were waited for; matrix products, arithmetic and copies ran while one was open for 9% of the time, Pallas kernels for 0%

commit v1 on v0

v1 whole, which is shorter than its diff:
```python
import functools

import jax
import jax.numpy as jnp
from jax import lax
from jax.experimental import pallas as pl
from jax.experimental.pallas import tpu as pltpu
from jax.sharding import PartitionSpec as P

F32 = jnp.float32
BF16 = jnp.bfloat16
LANES = 128
VMEM_BYTES = 48 * 1024 * 1024
ROWS_ROWS = (((1,), (1,)), ((), ()))
DEPTH_FIRST = (((0,), (0,)), ((), ()))


def call(kernel, outs, flops, moved):
    return pl.pallas_call(
        kernel,
        out_shape=outs,
        compiler_params=pltpu.CompilerParams(vmem_limit_bytes=VMEM_BYTES),
        cost_estimate=pl.CostEstimate(flops=flops, bytes_accessed=moved, transcendentals=0),
    )


def pick_matrices(dest_ref, groups, capacity, slot_count):
    tokens = dest_ref.shape[1]
    group_line = lax.broadcasted_iota(jnp.int32, (groups, tokens), 0)
    earlier = (
        lax.broadcasted_iota(jnp.int32, (tokens, tokens), 0)
        < lax.broadcasted_iota(jnp.int32, (tokens, tokens), 1)
    ).astype(F32).astype(BF16)
    slot_line = lax.broadcasted_iota(jnp.int32, (slot_count, tokens), 0)
    taken = jnp.zeros((groups, 1), F32)
    out = []
    for hop in range(dest_ref.shape[0]):
        dest = dest_ref[hop : hop + 1, :]
        match = (group_line == dest).astype(F32)
        before = jnp.dot(match.astype(BF16), earlier, preferred_element_type=F32) + taken
        place = jnp.sum(before * match, axis=0, keepdims=True).astype(jnp.int32)
        out.append((slot_line == dest * capacity + place).astype(F32).astype(BF16))
        taken = taken + jnp.sum(match, axis=1, keepdims=True)
    return out


def pack_kernel(groups, capacity, dest_ref, ids_ref, codes_ref, grads_ref, inputs_ref, row_ref, input_ref):
    slot_count, width = input_ref.shape
    tokens = grads_ref.shape[0]
    picks = pick_matrices(dest_ref, groups, capacity, slot_count)
    pick = functools.reduce(jnp.add, picks)
    row_ref[:, :width] = jnp.dot(pick, grads_ref[...], preferred_element_type=F32).astype(BF16)
    per = ids_ref.shape[1]
    notes = jnp.zeros((slot_count, LANES), F32)
    for hop, hop_pick in enumerate(picks):
        lines = jnp.concatenate(
            [
                ids_ref[hop].astype(F32),
                codes_ref[hop],
                jnp.zeros((LANES - 2 * per, tokens), F32),
            ],
            axis=0,
        ).astype(BF16)
        notes = notes + lax.dot_general(hop_pick, lines, ROWS_ROWS, preferred_element_type=F32)
    row_ref[:, width:] = notes.astype(BF16)
    input_ref[...] = jnp.dot(pick, inputs_ref[...], preferred_element_type=F32).astype(BF16)


def fold(values, per):
    parts = LANES // per
    height = values.shape[0] // parts
    lane = lax.broadcasted_iota(jnp.int32, (height, LANES), 1)
    out = values[:height]
    for q in range(1, parts):
        turned = pltpu.roll(values[q * height : (q + 1) * height], q * per, 1)
        out = jnp.where(lane >= q * per, turned, out)
    return out


def score_kernel(per, row_ref, dec_ref, score_ref, ids_ref, codes_ref):
    width = dec_ref.shape[1]
    scores = lax.dot_general(row_ref[:, :width], dec_ref[...], ROWS_ROWS, preferred_element_type=F32)
    notes = row_ref[:, width:].astype(F32)
    ids = notes.astype(jnp.int32)
    low = ids & (LANES - 1)
    chosen = jnp.take_along_axis(scores[:, :LANES], low, axis=1)
    for part in range(1, dec_ref.shape[0] // LANES):
        here = jnp.take_along_axis(scores[:, part * LANES : (part + 1) * LANES], low, axis=1)
        chosen = jnp.where(ids >= part * LANES, here, chosen)
    folded = fold(chosen, per)
    for copy in range(score_ref.shape[0]):
        score_ref[copy] = folded
    ids_ref[...] = fold(notes, per).T
    codes_ref[...] = fold(pltpu.roll(notes, LANES - per, 1), per).T


def spread(ids, values, features, per):
    held = ids.shape[1]
    feature_line = lax.broadcasted_iota(jnp.int32, (features, held), 0).astype(F32)
    blocks = []
    for q in range(LANES // per):
        block = jnp.zeros((features, held), F32)
        for j in range(q * per, (q + 1) * per):
            block = jnp.where(feature_line == ids[j : j + 1, :], values[j : j + 1, :], block)
        blocks.append(block)
    return jnp.concatenate(blocks, axis=1).astype(BF16)


def back_kernel(per, score_ref, ids_ref, enc_ref, pre_ref, back_ref):
    total = score_ref[0]
    for copy in range(1, score_ref.shape[0]):
        total = total + score_ref[copy]
    rounded = total.astype(BF16).astype(F32).T
    pre = spread(ids_ref[...], rounded, enc_ref.shape[0], per)
    pre_ref[...] = pre
    back_ref[...] = lax.dot_general(pre, enc_ref[...], DEPTH_FIRST, preferred_element_type=F32).astype(BF16)


def dec_kernel(per, ids_ref, codes_ref, row_ref, out_ref):
    features, width = out_ref.shape
    code = spread(ids_ref[...], codes_ref[...], features, per)
    out_ref[...] = jnp.dot(code, row_ref[:, :width], preferred_element_type=F32).astype(BF16)


def enc_kernel(pre_ref, input_ref, out_ref):
    out_ref[...] = jnp.dot(pre_ref[...], input_ref[...], preferred_element_type=F32).astype(BF16)


def merge_kernel(groups, capacity, dest_ref, back_ref, out_ref):
    picks = pick_matrices(dest_ref, groups, capacity, back_ref.shape[0])
    pick = functools.reduce(jnp.add, picks)
    out_ref[...] = lax.dot_general(pick, back_ref[...], DEPTH_FIRST, preferred_element_type=F32).astype(BF16)


def shards(enc_rows, dec_rows, inputs, out_grad, destinations, local_ids, code_values):
    groups = lax.axis_size("feat")
    slices = lax.axis_size("tok")
    tokens, hops = destinations.shape
    per = local_ids.shape[2]
    features, width = dec_rows.shape
    capacity = max(2, 2 * tokens * hops // groups)
    slots = groups * capacity
    dest = destinations.T
    shape = jax.ShapeDtypeStruct
    mac = 2 * slots * width

    send_rows, send_inputs = call(
        functools.partial(pack_kernel, groups, capacity),
        (shape((slots, width + LANES), BF16), shape((slots, width), BF16)),
        2 * mac * tokens,
        4 * slots * width + 4 * tokens * width,
    )(dest, jnp.transpose(local_ids, (1, 2, 0)), jnp.transpose(code_values, (1, 2, 0)), out_grad, inputs)

    rows = lax.all_to_all(
        send_rows.reshape(groups, capacity, width + LANES), "feat", split_axis=0, concat_axis=0, tiled=True
    ).reshape(slots, width + LANES)
    held = slots * per // LANES
    score, ids, codes = call(
        functools.partial(score_kernel, per),
        (shape((slices, held, LANES), F32), shape((LANES, held), F32), shape((LANES, held), F32)),
        mac * features,
        2 * slots * width,
    )(rows, dec_rows)
    score = lax.all_to_all(score, "tok", split_axis=0, concat_axis=0, tiled=True)
    pre, back = call(
        functools.partial(back_kernel, per),
        (shape((features, slots), BF16), shape((slots, width), BF16)),
        mac * features,
        2 * slots * width,
    )(score, ids, enc_rows)
    returned = lax.all_to_all(
        back.reshape(groups, capacity, width), "feat", split_axis=0, concat_axis=0, tiled=True
    ).reshape(slots, width)
    dec_grad = call(
        functools.partial(dec_kernel, per), shape((features, width), BF16), mac * features, 4 * slots * width
    )(ids, codes, rows)
    given = lax.all_to_all(
        send_inputs.reshape(groups, capacity, width), "feat", split_axis=0, concat_axis=0, tiled=True
    ).reshape(slots, width)
    enc_grad = call(enc_kernel, shape((features, width), BF16), mac * features, 4 * slots * width)(pre, given)
    in_grad = call(
        functools.partial(merge_kernel, groups, capacity),
        shape((tokens, width), BF16),
        mac * tokens,
        4 * slots * width,
    )(dest, returned)
    return (enc_grad, dec_grad, in_grad)


def solution(mesh):
    split = P("feat", "tok")
    return jax.shard_map(
        shards,
        mesh=mesh,
        in_specs=(split, split, split, split, P("feat", None), P("feat", None, None), P("feat", None, None)),
        out_specs=(split, split, split),
        check_vma=False,
    )
```

time: 347 us -> 232 us (0.67)
  waiting for transfers between devices: 185 us -> 102 us
  blocking collectives: 61 us -> 101 us
  starting transfers between devices: 43.7 us -> 10.2 us
  other arithmetic: 22.4 us -> 0 us
  between operations: 14.3 us -> 0.74 us
  Pallas kernels: 0 us -> 8.11 us
  matrix products: 5.28 us -> 0 us
  local copies, waits for them, and re-layouts: 14.8 us -> 9.6 us
    psum x1 -> x0, waiting for transfers between devices: 116 us -> none  [decoder_side(): summed = lax.psum(partial_value, 'tok')]
    all_to_all x1 -> x2, blocking collectives: 61 us -> 101 us  [the longest x1 78.2 us: shards(): lax.all_to_all(send_rows.reshape(groups, capacity, width + LANES), 'feat'...]
    all_to_all x4 -> x2, starting transfers between devices: 43.7 us -> 10.2 us  [the longest x1 5.59 us: shards(): lax.all_to_all(send_inputs.reshape(groups, capacity, width), 'feat', spli...]
    all_to_all x4 -> x2, waiting for transfers between devices: 68.6 us -> 102 us  [the longest x1 51.3 us: shards(): lax.all_to_all(send_inputs.reshape(groups, capacity, width), 'feat', spli...]
    reduce_sum x4 -> x0, other arithmetic: 17.2 us -> none  [the longest x1 8.6 us: decoder_side(): jnp.sum(jnp.where(hits, recv_codes.astype(jnp.float32)[:, :, None], 0.0),...]
    pallas_call x0 -> x6, Pallas kernels: none -> 8.11 us  [the longest x1 2.24 us: shards(): call(functools.partial(dec_kernel, per), shape((features, width), BF16),...]
    unnamed x24 -> x30, local copies, waits for them, and re-layouts: 3.79 us -> 9.6 us
    gather x4 -> x0, local copies, waits for them, and re-layouts: 5.48 us -> none  [the longest x1 2.06 us: shards(): jnp.take(out_grad, token_table, axis=0, mode='fill', fill_value=0)]
  transfers between devices with their start and end apart: 5 -> 2, of which waited for: 4 -> 2; matrix products, arithmetic and copies ran while one was open for 9% -> 0% of each run, Pallas kernels for 0% -> 2%
where the time goes in v1:
time: 232 us; the launch traced here: 231 us
  waiting for transfers between devices  102 us (44%)
  blocking collectives  101 us (44%)
  starting transfers between devices  10.2 us (4%)
  local copies, waits for them, and re-layouts  9.6 us (4%)
  Pallas kernels  8.11 us (3%)
    all_to_all x1, blocking collectives, shards(): lax.all_to_all(send_rows.reshape(groups, capacity, width + LANES), 'feat'...  78.2 us
    all_to_all x1, waiting for transfers between devices, shards(): lax.all_to_all(send_inputs.reshape(groups, capacity, width), 'feat', spli...  51.3 us
    all_to_all x1, waiting for transfers between devices, shards(): lax.all_to_all(back.reshape(groups, capacity, width), 'feat', split_axis=...  50.7 us
    all_to_all x1, blocking collectives, shards(): lax.all_to_all(score, 'tok', split_axis=0, concat_axis=0, tiled=True)  22.7 us
    unnamed x30, local copies, waits for them, and re-layouts  9.6 us
    all_to_all x1, starting transfers between devices, shards(): lax.all_to_all(send_inputs.reshape(groups, capacity, width), 'feat', spli...  5.59 us
  transfers between devices with their start and end apart: 2, of which 2 were waited for; matrix products, arithmetic and copies ran while one was open for 0% of the time, Pallas kernels for 2%

profile of v1, /device:TPU:1, one launch (start us, length us, event | category | flops | bytes accessed | tf_op | source)
XLA Modules:
  0.0 231.5 jit_solution(9800546924297143152)
XLA Ops:
  0.6 0.0 copy-start.9
  0.6 0.7 copy-done.9
  1.3 0.9 copy-done.11
  2.3 0.9 copy-done.12
  3.2 0.8 copy-done.13
  4.0 0.8 copy-done.14
  4.7 0.9 shard_map.94
  5.7 0.0 copy-start.1
  5.7 1.0 copy-done.1
  6.7 78.2 %all_to_all.20 = bf16[32,16,1152]{2,1,0:T(8,128)(2,1)S(1)} all-to-all(bf16[32,16,1152]{2,1,0:T(8,128)(2,1)S(1)} %bitcast.13), channel_id=1, replica_groups=mesh['feat'=32,'tok'=16] {'feat'}, dimensions={0} | all-to-all | bytes 2359296 | tf_op jit(solution)/shard_map/all_to_all | solution.py:154
  84.8 0.0 copy-done.3
  84.8 0.9 shard_map.95
  85.7 0.0 copy-start.4
  85.7 0.0 copy-start.7
  85.7 22.7 %all_to_all.21.score_ref = f32[16,128,128]{2,1,0:T(8,128)S(1)} all-to-all(f32[16,128,128]{2,1,0:T(8,128)S(1)} %get-tuple-element.11), channel_id=1, replica_groups=mesh['feat'=32,'tok'=16] {'tok'}, dimensions={0} | all-to-all | bytes 2097152 | tf_op jit(solution)/shard_map/all_to_all | solution.py:164
  108.4 0.0 copy-done.4
  108.4 5.6 %all-to-all-start.2 = ((bf16[32,16,1024]{2,1,0:T(8,128)(2,1)}), bf16[32,16,1024]{2,1,0:T(8,128)(2,1)S(1)}, u32[]{:S(2)}, u32[]{:S(2)}) async-start(bf16[32,16,1024]{2,1,0:T(8,128)(2,1)} %bitcast.15), calls=%async_computation.2 | async-start | bytes 2097152 | tf_op jit(solution)/shard_map/all_to_all | solution.py:177
  114.0 0.0 copy-start.2
  114.0 1.0 copy-done.2
  115.0 0.8 copy-done.5
  115.9 1.6 shard_map.96
  117.5 0.0 copy-start
  117.5 1.0 copy-done
  118.5 51.3 %all-to-all-done.2 = bf16[32,16,1024]{2,1,0:T(8,128)(2,1)S(1)} async-done(((bf16[32,16,1024]{2,1,0:T(8,128)(2,1)}), bf16[32,16,1024]{2,1,0:T(8,128)(2,1)S(1)}, u32[]{:S(2)}, u32[]{:S(2)}) %all-to-all-start.2) | async-done | bytes 1048608 | tf_op jit(solution)/shard_map/all_to_all | solution.py:177
  169.8 4.6 %all-to-all-start.3 = ((bf16[32,16,1024]{2,1,0:T(8,128)(2,1)}), bf16[32,16,1024]{2,1,0:T(8,128)(2,1)S(1)}, u32[]{:S(2)}, u32[]{:S(2)}) async-start(bf16[32,16,1024]{2,1,0:T(8,128)(2,1)} %bitcast.14), calls=%async_computation.3 | async-start | bytes 2097152 | tf_op jit(solution)/shard_map/all_to_all | solution.py:171
  174.4 0.0 copy-start.6
  174.5 0.8 copy-done.6
  175.3 0.8 copy-done.8
  176.1 2.2 shard_map.98
  178.4 1.2 shard_map.97
  179.6 50.7 %all-to-all-done.3 = bf16[32,16,1024]{2,1,0:T(8,128)(2,1)S(1)} async-done(((bf16[32,16,1024]{2,1,0:T(8,128)(2,1)}), bf16[32,16,1024]{2,1,0:T(8,128)(2,1)S(1)}, u32[]{:S(2)}, u32[]{:S(2)}) %all-to-all-start.3) | async-done | bytes 1048608 | tf_op jit(solution)/shard_map/all_to_all | solution.py:171
  230.3 1.2 shard_map.99
  (10 shorter events, 0.0 us)
Async XLA Ops:
  0.6 0.7 copy-start.9
  1.3 0.9 copy-start.11
  2.3 0.9 copy-start.12
  3.2 0.8 copy-start.13
  4.0 0.8 copy-start.14
  5.7 1.0 copy-start.1
  6.7 78.2 %copy-start.3 = (bf16[256,1024]{1,0:T(8,128)(2,1)S(1)}, bf16[256,1024]{1,0:T(8,128)(2,1)}, u32[]{:S(2)}) copy-start(bf16[256,1024]{1,0:T(8,128)(2,1)} %dec_ref.1) | copy-start | bytes 1572868
  85.7 22.7 %copy-start.4 = (f32[128,128]{1,0:T(8,128)}, f32[128,128]{1,0:T(8,128)S(1)}, u32[]{:S(2)}) copy-start(f32[128,128]{1,0:T(8,128)S(1)} %get-tuple-element.12.ids_ref) | copy-start | bytes 196612
  85.7 22.7 %copy-start.7 = (f32[128,128]{1,0:T(8,128)}, f32[128,128]{1,0:T(8,128)S(1)}, u32[]{:S(2)}) copy-start(f32[128,128]{1,0:T(8,128)S(1)} %get-tuple-element.15.codes_ref) | copy-start | bytes 196612
  108.4 61.4 %all-to-all-start.2 = ((bf16[32,16,1024]{2,1,0:T(8,128)(2,1)}), bf16[32,16,1024]{2,1,0:T(8,128)(2,1)S(1)}, u32[]{:S(2)}, u32[]{:S(2)}) async-start(bf16[32,16,1024]{2,1,0:T(8,128)(2,1)} %bitcast.15), calls=%async_computation.2 | async-start | bytes 2097152 | tf_op jit(solution)/shard_map/all_to_all | solution.py:177
  114.0 1.0 copy-start.2
  115.0 0.8 copy-start.5
  117.5 1.0 copy-start
  169.8 60.4 %all-to-all-start.3 = ((bf16[32,16,1024]{2,1,0:T(8,128)(2,1)}), bf16[32,16,1024]{2,1,0:T(8,128)(2,1)S(1)}, u32[]{:S(2)}, u32[]{:S(2)}) async-start(bf16[32,16,1024]{2,1,0:T(8,128)(2,1)} %bitcast.14), calls=%async_computation.3 | async-start | bytes 2097152 | tf_op jit(solution)/shard_map/all_to_all | solution.py:171
  174.4 0.8 copy-start.6
  175.3 0.8 copy-start.8
  178.4 51.9 %copy-start.10 = (s32[128,2]{0,1:T(2,128)S(1)}, s32[128,2]{0,1:T(2,128)}, u32[]{:S(2)}) copy-start(s32[128,2]{0,1:T(2,128)} %param.11) | copy-start | bytes 3076

commit v2 on v1

--- a/solution.py
+++ b/solution.py
@@ -10,44 +10,71 @@
 F32 = jnp.float32
 BF16 = jnp.bfloat16
 LANES = 128
+EARLY = (8, 7)
 VMEM_BYTES = 48 * 1024 * 1024
 ROWS_ROWS = (((1,), (1,)), ((), ()))
 DEPTH_FIRST = (((0,), (0,)), ((), ()))
 
 
-def call(kernel, outs, flops, moved):
+def call(kernel, outs, flops, moved, scratch=(), plain=0, order_only=0):
+    specs = {}
+    if order_only:
+        specs["in_specs"] = [pl.BlockSpec(memory_space=pltpu.VMEM)] * plain
+        specs["in_specs"] += [pl.BlockSpec(memory_space=pl.ANY)] * order_only
     return pl.pallas_call(
         kernel,
+        **specs,
         out_shape=outs,
+        scratch_shapes=scratch,
         compiler_params=pltpu.CompilerParams(vmem_limit_bytes=VMEM_BYTES),
         cost_estimate=pl.CostEstimate(flops=flops, bytes_accessed=moved, transcendentals=0),
     )
 
 
-def pick_matrices(dest_ref, groups, capacity, slot_count):
+def places(dest_ref, groups):
     tokens = dest_ref.shape[1]
     group_line = lax.broadcasted_iota(jnp.int32, (groups, tokens), 0)
     earlier = (
         lax.broadcasted_iota(jnp.int32, (tokens, tokens), 0)
         < lax.broadcasted_iota(jnp.int32, (tokens, tokens), 1)
     ).astype(F32).astype(BF16)
-    slot_line = lax.broadcasted_iota(jnp.int32, (slot_count, tokens), 0)
     taken = jnp.zeros((groups, 1), F32)
     out = []
     for hop in range(dest_ref.shape[0]):
-        dest = dest_ref[hop : hop + 1, :]
-        match = (group_line == dest).astype(F32)
+        match = (group_line == dest_ref[hop : hop + 1, :]).astype(F32)
         before = jnp.dot(match.astype(BF16), earlier, preferred_element_type=F32) + taken
-        place = jnp.sum(before * match, axis=0, keepdims=True).astype(jnp.int32)
-        out.append((slot_line == dest * capacity + place).astype(F32).astype(BF16))
+        out.append(jnp.sum(before * match, axis=0, keepdims=True).astype(jnp.int32))
         taken = taken + jnp.sum(match, axis=1, keepdims=True)
     return out
 
 
-def pack_kernel(groups, capacity, dest_ref, ids_ref, codes_ref, grads_ref, inputs_ref, row_ref, input_ref):
-    slot_count, width = input_ref.shape
-    tokens = grads_ref.shape[0]
-    picks = pick_matrices(dest_ref, groups, capacity, slot_count)
+def one_hot(numbers, count):
+    line = lax.broadcasted_iota(jnp.int32, (count, numbers.shape[1]), 0)
+    return (line == numbers).astype(F32).astype(BF16)
+
+
+def pick_matrices(dest_ref, groups, capacity):
+    return [
+        one_hot(dest_ref[hop : hop + 1, :] * capacity + place, groups * capacity)
+        for hop, place in enumerate(places(dest_ref, groups))
+    ]
+
+
+def relative_slots(dest, place, groups, capacity):
+    me = lax.axis_index("feat")
+    chips = groups // 2
+    core = me & 1
+    away = ((dest >> 1) - (me >> 1)) & (chips - 1)
+    away = jnp.where(core == 1, (chips - away) & (chips - 1), away)
+    far = capacity + (away - 1) * 2 * capacity + (dest & 1) * capacity
+    here = jnp.where((dest & 1) == core, 0, (groups - 1) * capacity)
+    return jnp.where(away == 0, here, far) + place
+
+
+def pack_rows_kernel(groups, capacity, dest_ref, ids_ref, codes_ref, grads_ref, row_ref):
+    slot_count = row_ref.shape[0]
+    tokens, width = grads_ref.shape
+    picks = pick_matrices(dest_ref, groups, capacity)
     pick = functools.reduce(jnp.add, picks)
     row_ref[:, :width] = jnp.dot(pick, grads_ref[...], preferred_element_type=F32).astype(BF16)
     per = ids_ref.shape[1]
@@ -63,7 +90,69 @@
         ).astype(BF16)
         notes = notes + lax.dot_general(hop_pick, lines, ROWS_ROWS, preferred_element_type=F32)
     row_ref[:, width:] = notes.astype(BF16)
-    input_ref[...] = jnp.dot(pick, inputs_ref[...], preferred_element_type=F32).astype(BF16)
+
+
+def pack_inputs_kernel(groups, capacity, dest_ref, inputs_ref, keep_ref, give_ref):
+    kept = keep_ref.shape[0]
+    numbers = [
+        relative_slots(dest_ref[hop : hop + 1, :], place, groups, capacity)
+        for hop, place in enumerate(places(dest_ref, groups))
+    ]
+    pick = functools.reduce(jnp.add, [one_hot(number, groups * capacity) for number in numbers])
+    chosen = jnp.dot(pick, inputs_ref[...], preferred_element_type=F32).astype(BF16)
+    keep_ref[...] = chosen[:kept]
+    give_ref[...] = chosen[kept:]
+
+
+def join_kernel(capacity, reach, picked, keep_ref, got_ref, after_ref, *out_refs):
+    del after_ref
+    for k, out_ref in zip(picked, out_refs, strict=True):
+        if k > reach:
+            mine = capacity + reach * 2 * capacity
+            out_ref[...] = keep_ref[mine : mine + 2 * capacity, :]
+            continue
+        for core in range(2):
+            mine = capacity + ((k - 1) * 2 + core) * capacity
+            theirs = ((reach - k) * 2 + core) * capacity
+            out_ref[2 * core * capacity : (2 * core + 1) * capacity, :] = keep_ref[mine : mine + capacity, :]
+            out_ref[(2 * core + 1) * capacity : (2 * core + 2) * capacity, :] = got_ref[theirs : theirs + capacity, :]
+
+
+def cross_kernel(capacity, far_ref, *refs):
+    message_refs, out_ref = refs[:-1], refs[-1]
+    other = 1 - (lax.axis_index("feat") & 1)
+    for k, ref in enumerate(message_refs):
+        start = pl.multiple_of(other * 2 * capacity, 2 * capacity)
+        out_ref[k * 2 * capacity : (k + 1) * 2 * capacity, :] = ref[pl.ds(start, 2 * capacity), :]
+    start = pl.multiple_of(other * capacity, capacity)
+    out_ref[len(message_refs) * 2 * capacity :, :] = far_ref[pl.ds(start, capacity), :]
+
+
+def enc_kernel(groups, capacity, pre_ref, keep_ref, got_ref, far_ref, crossed_ref, *refs):
+    message_refs, out_ref, line_ref = refs[:-2], refs[-2], refs[-1]
+    me = lax.axis_index("feat")
+    chips = groups // 2
+    chip, core = me >> 1, me & 1
+    other = 1 - core
+    reach = len(message_refs)
+
+    def put(away, owner, rows):
+        source = ((chip + away) & (chips - 1)) * 2 + owner
+        line_ref[pl.ds(pl.multiple_of(source * capacity, capacity), capacity), :] = rows
+
+    put(0, core, keep_ref[:capacity, :])
+    put(0, other, got_ref[got_ref.shape[0] - capacity :, :])
+    put(chips // 2, core, far_ref[pl.ds(pl.multiple_of(core * capacity, capacity), capacity), :])
+    put(chips // 2, other, crossed_ref[reach * 2 * capacity :, :])
+    for k in range(1, reach + 1):
+        away = jnp.where(core == 0, chips - k, k)
+        base = pl.multiple_of(core * 2 * capacity, 2 * capacity)
+        put(away, core, message_refs[k - 1][pl.ds(base, capacity), :])
+        put(away, other, message_refs[k - 1][pl.ds(base + capacity, capacity), :])
+        base = (k - 1) * 2 * capacity
+        put(chips - away, other, crossed_ref[base : base + capacity, :])
+        put(chips - away, core, crossed_ref[base + capacity : base + 2 * capacity, :])
+    out_ref[...] = jnp.dot(pre_ref[...], line_ref[...], preferred_element_type=F32).astype(BF16)
 
 
 def fold(values, per):
@@ -106,7 +195,8 @@
     return jnp.concatenate(blocks, axis=1).astype(BF16)
 
 
-def back_kernel(per, score_ref, ids_ref, enc_ref, pre_ref, back_ref):
+def back_kernel(per, score_ref, ids_ref, enc_ref, *refs):
+    pre_ref, back_ref = refs[-2:]
     total = score_ref[0]
     for copy in range(1, score_ref.shape[0]):
         total = total + score_ref[copy]
@@ -122,12 +212,8 @@
     out_ref[...] = jnp.dot(code, row_ref[:, :width], preferred_element_type=F32).astype(BF16)
 
 
-def enc_kernel(pre_ref, input_ref, out_ref):
-    out_ref[...] = jnp.dot(pre_ref[...], input_ref[...], preferred_element_type=F32).astype(BF16)
-
-
 def merge_kernel(groups, capacity, dest_ref, back_ref, out_ref):
-    picks = pick_matrices(dest_ref, groups, capacity, back_ref.shape[0])
+    picks = pick_matrices(dest_ref, groups, capacity)
     pick = functools.reduce(jnp.add, picks)
     out_ref[...] = lax.dot_general(pick, back_ref[...], DEPTH_FIRST, preferred_element_type=F32).astype(BF16)
 
@@ -144,16 +230,43 @@
     shape = jax.ShapeDtypeStruct
     mac = 2 * slots * width
 
-    send_rows, send_inputs = call(
-        functools.partial(pack_kernel, groups, capacity),
-        (shape((slots, width + LANES), BF16), shape((slots, width), BF16)),
-        2 * mac * tokens,
-        4 * slots * width + 4 * tokens * width,
-    )(dest, jnp.transpose(local_ids, (1, 2, 0)), jnp.transpose(code_values, (1, 2, 0)), out_grad, inputs)
-
+    send_rows = call(
+        functools.partial(pack_rows_kernel, groups, capacity),
+        shape((slots, width + LANES), BF16),
+        mac * tokens,
+        2 * slots * width + 2 * tokens * width,
+    )(dest, jnp.transpose(local_ids, (1, 2, 0)), jnp.transpose(code_values, (1, 2, 0)), out_grad)
     rows = lax.all_to_all(
         send_rows.reshape(groups, capacity, width + LANES), "feat", split_axis=0, concat_axis=0, tiled=True
     ).reshape(slots, width + LANES)
+
+    chips = groups // 2
+    reach = chips // 2 - 1
+    given = (reach * 2 + 1) * capacity
+    keep, give = call(
+        functools.partial(pack_inputs_kernel, groups, capacity),
+        (shape((slots - given, width), BF16), shape((given, width), BF16)),
+        mac * tokens,
+        2 * slots * width + 2 * tokens * width,
+    )(dest, inputs)
+    swap = [(i, i ^ 1) for i in range(groups)]
+    got = lax.ppermute(give, "feat", swap)
+
+    def away(k):
+        return [(i, ((i // 2 + (chips - k if i % 2 else k)) % chips) * 2 + i % 2) for i in range(groups)]
+
+    def send(picked, after):
+        messages = call(
+            functools.partial(join_kernel, capacity, reach, picked),
+            tuple(shape(((4 if k <= reach else 2) * capacity, width), BF16) for k in picked),
+            0,
+            4 * len(picked) * 4 * capacity * width,
+            plain=2,
+            order_only=1,
+        )(keep, got, after)
+        return {k: lax.ppermute(m, "feat", away(k)) for k, m in zip(picked, messages, strict=True)}
+
+    arrived = send(EARLY, rows)
     held = slots * per // LANES
     score, ids, codes = call(
         functools.partial(score_kernel, per),
@@ -167,17 +280,32 @@
         (shape((features, slots), BF16), shape((slots, width), BF16)),
         mac * features,
         2 * slots * width,
-    )(score, ids, enc_rows)
+        plain=3,
+        order_only=len(EARLY),
+    )(score, ids, enc_rows, *[arrived[k] for k in EARLY])
     returned = lax.all_to_all(
         back.reshape(groups, capacity, width), "feat", split_axis=0, concat_axis=0, tiled=True
     ).reshape(slots, width)
+    arrived |= send(tuple(k for k in range(reach, 0, -1) if k not in EARLY), back)
+    far = arrived[reach + 1]
+    arrived = [arrived[k] for k in range(1, reach + 1)]
+    crossed = lax.ppermute(
+        call(functools.partial(cross_kernel, capacity), shape((given, width), BF16), 0, 4 * given * width)(
+            far, *arrived
+        ),
+        "feat",
+        swap,
+    )
     dec_grad = call(
         functools.partial(dec_kernel, per), shape((features, width), BF16), mac * features, 4 * slots * width
     )(ids, codes, rows)
-    given = lax.all_to_all(
-        send_inputs.reshape(groups, capacity, width), "feat", split_axis=0, concat_axis=0, tiled=True
-    ).reshape(slots, width)
-    enc_grad = call(enc_kernel, shape((features, width), BF16), mac * features, 4 * slots * width)(pre, given)
+    enc_grad = call(
+        functools.partial(enc_kernel, groups, capacity),
+        shape((features, width), BF16),
+        mac * features,
+        4 * slots * width,
+        (pltpu.VMEM((slots, width), BF16),),
+    )(pre, keep, got, far, crossed, *arrived)
     in_grad = call(
         functools.partial(merge_kernel, groups, capacity),
         shape((tokens, width), BF16),

time: 232 us -> 224 us (0.966); the launches traced: 231 us -> 221 us
  starting transfers between devices: 10.2 us -> 68.4 us
  waiting for transfers between devices: 102 us -> 55.9 us
  blocking collectives: 101 us -> 78.2 us
    ppermute x0 -> x10, waiting for transfers between devices: none -> 55.8 us  [the longest x8 54.4 us: send(): lax.ppermute(m, 'feat', away(k))]
    ppermute x0 -> x10, starting transfers between devices: none -> 52.9 us  [the longest x8 45.1 us: send(): lax.ppermute(m, 'feat', away(k))]
    all_to_all x1, waiting for transfers between devices: 51.3 us -> 0.01 us  [shards(): lax.all_to_all(score, 'tok', split_axis=0, concat_axis=0, tiled=True)]
    all_to_all x1, waiting for transfers between devices: 50.7 us -> 0.01 us  [shards(): lax.all_to_all(back.reshape(groups, capacity, width), 'feat', split_axis=...]
    all_to_all x1 -> x0, blocking collectives: 22.7 us -> none  [shards(): lax.all_to_all(score, 'tok', split_axis=0, concat_axis=0, tiled=True)]
    all_to_all x1, starting transfers between devices: 4.62 us -> 8.6 us  [shards(): lax.all_to_all(back.reshape(groups, capacity, width), 'feat', split_axis=...]
    unnamed x30 -> x28, local copies, waits for them, and re-layouts: 9.6 us -> 7.75 us
  transfers between devices with their start and end apart: 2 -> 12, of which waited for: 2 -> 6; matrix products, arithmetic and copies ran while one was open for 0% -> 0% of each run, Pallas kernels for 2% -> 2%
where the time goes in v2:
time: 224 us; the launch traced here: 221 us
  blocking collectives  78.2 us (35%)
  starting transfers between devices  68.4 us (31%)
  waiting for transfers between devices  55.9 us (25%)
  Pallas kernels  9.51 us (4%)
  local copies, waits for them, and re-layouts  7.75 us (3%)
    all_to_all x1, blocking collectives, shards(): lax.all_to_all(send_rows.reshape(groups, capacity, width + LANES), 'feat'...  78.2 us
    ppermute x8, waiting for transfers between devices, send(): lax.ppermute(m, 'feat', away(k))  54.4 us
    ppermute x8, starting transfers between devices, send(): lax.ppermute(m, 'feat', away(k))  45.1 us
    all_to_all x1, starting transfers between devices, shards(): lax.all_to_all(back.reshape(groups, capacity, width), 'feat', split_axis=...  8.6 us
    unnamed x28, local copies, waits for them, and re-layouts  7.75 us
    all_to_all x1, starting transfers between devices, shards(): lax.all_to_all(score, 'tok', split_axis=0, concat_axis=0, tiled=True)  6.9 us
    ppermute x1, starting transfers between devices, shards(): lax.ppermute(call(functools.partial(cross_kernel, capacity), shape((given...  4.75 us
  transfers between devices with their start and end apart: 12, of which 6 were waited for; matrix products, arithmetic and copies ran while one was open for 0% of the time, Pallas kernels for 2%

profile of v2, /device:TPU:1, one launch (start us, length us, event | category | flops | bytes accessed | tf_op | source)
XLA Modules:
  0.0 220.5 jit_solution(4580612781385714172)
XLA Ops:
  0.6 0.9 copy-done.4
  1.6 0.8 copy-done.9
  2.3 0.8 copy-done.10
  3.1 0.7 copy-done.11
  4.4 78.2 %all_to_all.15 = bf16[32,16,1152]{2,1,0:T(8,128)(2,1)S(1)} all-to-all(bf16[32,16,1152]{2,1,0:T(8,128)(2,1)S(1)} %bitcast.10), channel_id=1, replica_groups=mesh['feat'=32,'tok'=16] {'feat'}, dimensions={0} | all-to-all | bytes 2359296 | tf_op jit(solution)/shard_map/all_to_all | solution.py:239
  82.6 1.8 shard_map.95
  85.1 6.9 %all-to-all-start.1 = ((f32[16,128,128]{2,1,0:T(8,128)}), f32[16,128,128]{2,1,0:T(8,128)S(1)}, u32[]{:S(2)}, u32[]{:S(2)}) async-start(f32[16,128,128]{2,1,0:T(8,128)} %get-tuple-element.18), calls=%async_computation.1 | async-start | bytes 2097152 | tf_op jit(solution)/shard_map/all_to_all | solution.py:277
  92.6 3.0 %collective-permute-start = (bf16[240,1024]{1,0:T(8,128)(2,1)S(1)}, bf16[240,1024]{1,0:T(8,128)(2,1)S(1)}, u32[]{:S(2)}, u32[]{:S(2)}) collective-permute-start(bf16[240,1024]{1,0:T(8,128)(2,1)S(1)} %get-tuple-element.21), channel_id=1, source_target_pairs={{0,16},{16,0},{32,48},{48,32},{64,80},{80,64},{96,112},{112,96},{1... | collective-permute-start | bytes 1474568 | tf_op jit(solution)/shard_map/ppermute | solution.py:253
  95.6 1.5 collective-permute-done.got_ref
  97.1 1.9 collective-permute-start.2
  99.0 11.2 %collective-permute-start.1 = (bf16[32,1024]{1,0:T(8,128)(2,1)S(1)}, bf16[32,1024]{1,0:T(8,128)(2,1)S(1)}, u32[]{:S(2)}, u32[]{:S(2)}) collective-permute-start(bf16[32,1024]{1,0:T(8,128)(2,1)S(1)} %get-tuple-element.22), channel_id=1, source_target_pairs={{0,256},{16,272},{32,288},{48,304},{64,320},{80,336},{96,352},{112... | collective-permute-start | bytes 196616 | tf_op jit(solution)/shard_map/ppermute | solution.py:267
  110.3 10.5 %collective-permute-done.1.refs_0_.far_ref = bf16[32,1024]{1,0:T(8,128)(2,1)S(1)} collective-permute-done((bf16[32,1024]{1,0:T(8,128)(2,1)S(1)}, bf16[32,1024]{1,0:T(8,128)(2,1)S(1)}, u32[]{:S(2)}, u32[]{:S(2)}) %collective-permute-start.1) | collective-permute-done | bytes 65568 | tf_op jit(solution)/shard_map/ppermute | solution.py:267
  120.8 1.0 copy-done.2
  121.9 1.6 shard_map.98
  123.5 1.0 copy-done
  124.5 0.7 copy-done.5
  125.2 8.6 %all-to-all-start.2 = ((bf16[32,16,1024]{2,1,0:T(8,128)(2,1)}), bf16[32,16,1024]{2,1,0:T(8,128)(2,1)S(1)}, u32[]{:S(2)}, u32[]{:S(2)}) async-start(bf16[32,16,1024]{2,1,0:T(8,128)(2,1)} %bitcast.12), calls=%async_computation.2 | async-start | bytes 2097152 | tf_op jit(solution)/shard_map/all_to_all | solution.py:286
  133.8 1.2 copy-done.1
  135.1 4.7 %collective-permute-start.3 = (bf16[64,1024]{1,0:T(8,128)(2,1)S(1)}, bf16[64,1024]{1,0:T(8,128)(2,1)S(1)}, u32[]{:S(2)}, u32[]{:S(2)}) collective-permute-start(bf16[64,1024]{1,0:T(8,128)(2,1)S(1)} %get-tuple-element.26), channel_id=1, source_target_pairs={{0,32},{16,496},{32,64},{48,16},{64,96},{80,48},{96,128},{112,80},... | collective-permute-start | bytes 393224 | tf_op jit(solution)/shard_map/ppermute | solution.py:267
  139.8 4.0 %collective-permute-start.4 = (bf16[64,1024]{1,0:T(8,128)(2,1)S(1)}, bf16[64,1024]{1,0:T(8,128)(2,1)S(1)}, u32[]{:S(2)}, u32[]{:S(2)}) collective-permute-start(bf16[64,1024]{1,0:T(8,128)(2,1)S(1)} %get-tuple-element.27), channel_id=1, source_target_pairs={{0,64},{16,464},{32,96},{48,496},{64,128},{80,16},{96,160},{112,48... | collective-permute-start | bytes 393224 | tf_op jit(solution)/shard_map/ppermute | solution.py:267
  143.8 6.1 %collective-permute-start.5 = (bf16[64,1024]{1,0:T(8,128)(2,1)S(1)}, bf16[64,1024]{1,0:T(8,128)(2,1)S(1)}, u32[]{:S(2)}, u32[]{:S(2)}) collective-permute-start(bf16[64,1024]{1,0:T(8,128)(2,1)S(1)} %get-tuple-element.28), channel_id=1, source_target_pairs={{0,96},{16,432},{32,128},{48,464},{64,160},{80,496},{96,192},{112,... | collective-permute-start | bytes 393224 | tf_op jit(solution)/shard_map/ppermute | solution.py:267
  149.9 4.0 %collective-permute-start.6 = (bf16[64,1024]{1,0:T(8,128)(2,1)S(1)}, bf16[64,1024]{1,0:T(8,128)(2,1)S(1)}, u32[]{:S(2)}, u32[]{:S(2)}) collective-permute-start(bf16[64,1024]{1,0:T(8,128)(2,1)S(1)} %get-tuple-element.29), channel_id=1, source_target_pairs={{0,128},{16,400},{32,160},{48,432},{64,192},{80,464},{96,224},{112... | collective-permute-start | bytes 393224 | tf_op jit(solution)/shard_map/ppermute | solution.py:267
  153.8 2.2 collective-permute-start.7
  156.0 24.9 %collective-permute-done.3.refs_0_ = bf16[64,1024]{1,0:T(8,128)(2,1)S(1)} collective-permute-done((bf16[64,1024]{1,0:T(8,128)(2,1)S(1)}, bf16[64,1024]{1,0:T(8,128)(2,1)S(1)}, u32[]{:S(2)}, u32[]{:S(2)}) %collective-permute-start.3) | collective-permute-done | bytes 131104 | tf_op jit(solution)/shard_map/ppermute | solution.py:267
  180.9 11.0 %collective-permute-start.8 = (bf16[64,1024]{1,0:T(8,128)(2,1)S(1)}, bf16[64,1024]{1,0:T(8,128)(2,1)S(1)}, u32[]{:S(2)}, u32[]{:S(2)}) collective-permute-start(bf16[64,1024]{1,0:T(8,128)(2,1)S(1)} %get-tuple-element.31), channel_id=1, source_target_pairs={{0,192},{16,336},{32,224},{48,368},{64,256},{80,400},{96,288},{112... | collective-permute-start | bytes 393224 | tf_op jit(solution)/shard_map/ppermute | solution.py:267
  192.0 7.2 %collective-permute-done.6.refs_3_ = bf16[64,1024]{1,0:T(8,128)(2,1)S(1)} collective-permute-done((bf16[64,1024]{1,0:T(8,128)(2,1)S(1)}, bf16[64,1024]{1,0:T(8,128)(2,1)S(1)}, u32[]{:S(2)}, u32[]{:S(2)}) %collective-permute-start.6) | collective-permute-done | bytes 131104 | tf_op jit(solution)/shard_map/ppermute | solution.py:267
  199.2 10.7 %collective-permute-done.7.refs_4_ = bf16[64,1024]{1,0:T(8,128)(2,1)S(1)} collective-permute-done((bf16[64,1024]{1,0:T(8,128)(2,1)S(1)}, bf16[64,1024]{1,0:T(8,128)(2,1)S(1)}, u32[]{:S(2)}, u32[]{:S(2)}) %collective-permute-start.7) | collective-permute-done | bytes 131104 | tf_op jit(solution)/shard_map/ppermute | solution.py:267
  209.9 1.0 collective-permute-done.8.refs_5_
  211.0 4.7 %collective-permute-start.9 = (bf16[240,1024]{1,0:T(8,128)(2,1)S(1)}, bf16[240,1024]{1,0:T(8,128)(2,1)S(1)}, u32[]{:S(2)}, u32[]{:S(2)}) collective-permute-start(bf16[240,1024]{1,0:T(8,128)(2,1)S(1)} %shard_map.100), channel_id=1, source_target_pairs={{0,16},{16,0},{32,48},{48,32},{64,80},{80,64},{96,112},{112,96},{1... | collective-permute-start | bytes 1474568 | tf_op jit(solution)/shard_map/ppermute | solution.py:292
  215.7 2.2 %shard_map.102 = bf16[256,1024]{1,0:T(8,128)(2,1)} custom-call(f32[128,128]{1,0:T(8,128)S(1)} %get-tuple-element.19.ids_ref, f32[128,128]{1,0:T(8,128)S(1)} %copy-done.8, bf16[512,1152]{1,0:T(8,128)(2,1)S(1)} %bitcast.9), custom_call_target="tpu_custom_call" | custom-call | flops 268435456 | bytes 2097152 | tf_op jit(solution)/shard_map/pallas_call | solution.py:299
  218.0 1.3 shard_map.101
  219.3 1.2 shard_map.103
  (31 shorter events, 2.0 us)
Async XLA Ops:
  0.6 1.0 copy-start.4
  1.6 0.8 copy-start.9
  2.3 0.8 copy-start.10
  3.1 0.7 copy-start.11
  4.4 78.2 %copy-start.3 = (bf16[256,1024]{1,0:T(8,128)(2,1)S(1)}, bf16[256,1024]{1,0:T(8,128)(2,1)}, u32[]{:S(2)}) copy-start(bf16[256,1024]{1,0:T(8,128)(2,1)} %dec_ref.1) | copy-start | bytes 1572868
  84.4 0.6 copy-start.7
  85.1 6.9 %copy-start.12 = (s32[128,2]{0,1:T(2,128)S(1)}, s32[128,2]{0,1:T(2,128)}, u32[]{:S(2)}) copy-start(s32[128,2]{0,1:T(2,128)} %param.11) | copy-start | bytes 3076
  85.1 6.9 %copy-start.13 = (bf16[128,1024]{1,0:T(8,128)(2,1)S(1)}, bf16[128,1024]{1,0:T(8,128)(2,1)}, u32[]{:S(2)}) copy-start(bf16[128,1024]{1,0:T(8,128)(2,1)} %inputs_ref.1) | copy-start | bytes 786436
  85.1 35.7 %all-to-all-start.1 = ((f32[16,128,128]{2,1,0:T(8,128)}), f32[16,128,128]{2,1,0:T(8,128)S(1)}, u32[]{:S(2)}, u32[]{:S(2)}) async-start(f32[16,128,128]{2,1,0:T(8,128)} %get-tuple-element.18), calls=%async_computation.1 | async-start | bytes 2097152 | tf_op jit(solution)/shard_map/all_to_all | solution.py:277
  92.6 4.5 %collective-permute-start = (bf16[240,1024]{1,0:T(8,128)(2,1)S(1)}, bf16[240,1024]{1,0:T(8,128)(2,1)S(1)}, u32[]{:S(2)}, u32[]{:S(2)}) collective-permute-start(bf16[240,1024]{1,0:T(8,128)(2,1)S(1)} %get-tuple-element.21), channel_id=1, source_target_pairs={{0,16},{16,0},{32,48},{48,32},{64,80},{80,64},{96,112},{112,96},{1... | collective-permute-start | bytes 1474568 | tf_op jit(solution)/shard_map/ppermute | solution.py:253
  97.1 23.7 %collective-permute-start.2 = (bf16[64,1024]{1,0:T(8,128)(2,1)S(1)}, bf16[64,1024]{1,0:T(8,128)(2,1)S(1)}, u32[]{:S(2)}, u32[]{:S(2)}) collective-permute-start(bf16[64,1024]{1,0:T(8,128)(2,1)S(1)} %get-tuple-element.23), channel_id=1, source_target_pairs={{0,224},{16,304},{32,256},{48,336},{64,288},{80,368},{96,320},{112... | collective-permute-start | bytes 393224 | tf_op jit(solution)/shard_map/ppermute | solution.py:267
  99.0 21.8 %collective-permute-start.1 = (bf16[32,1024]{1,0:T(8,128)(2,1)S(1)}, bf16[32,1024]{1,0:T(8,128)(2,1)S(1)}, u32[]{:S(2)}, u32[]{:S(2)}) collective-permute-start(bf16[32,1024]{1,0:T(8,128)(2,1)S(1)} %get-tuple-element.22), channel_id=1, source_target_pairs={{0,256},{16,272},{32,288},{48,304},{64,320},{80,336},{96,352},{112... | collective-permute-start | bytes 196616 | tf_op jit(solution)/shard_map/ppermute | solution.py:267
  120.8 1.0 copy-start.2
  123.5 1.0 copy-start
  124.5 0.7 copy-start.5
  125.2 94.1 %all-to-all-start.2 = ((bf16[32,16,1024]{2,1,0:T(8,128)(2,1)}), bf16[32,16,1024]{2,1,0:T(8,128)(2,1)S(1)}, u32[]{:S(2)}, u32[]{:S(2)}) async-start(bf16[32,16,1024]{2,1,0:T(8,128)(2,1)} %bitcast.12), calls=%async_computation.2 | async-start | bytes 2097152 | tf_op jit(solution)/shard_map/all_to_all | solution.py:286
  133.8 1.3 copy-start.1
  135.1 80.7 %copy-start.8 = (f32[128,128]{1,0:T(8,128)S(1)}, f32[128,128]{1,0:T(8,128)}, u32[]{:S(2)}) copy-start(f32[128,128]{1,0:T(8,128)} %copy-done.7) | copy-start | bytes 196612
  135.1 45.9 %collective-permute-start.3 = (bf16[64,1024]{1,0:T(8,128)(2,1)S(1)}, bf16[64,1024]{1,0:T(8,128)(2,1)S(1)}, u32[]{:S(2)}, u32[]{:S(2)}) collective-permute-start(bf16[64,1024]{1,0:T(8,128)(2,1)S(1)} %get-tuple-element.26), channel_id=1, source_target_pairs={{0,32},{16,496},{32,64},{48,16},{64,96},{80,48},{96,128},{112,80},... | collective-permute-start | bytes 393224 | tf_op jit(solution)/shard_map/ppermute | solution.py:267
  139.8 52.2 %collective-permute-start.4 = (bf16[64,1024]{1,0:T(8,128)(2,1)S(1)}, bf16[64,1024]{1,0:T(8,128)(2,1)S(1)}, u32[]{:S(2)}, u32[]{:S(2)}) collective-permute-start(bf16[64,1024]{1,0:T(8,128)(2,1)S(1)} %get-tuple-element.27), channel_id=1, source_target_pairs={{0,64},{16,464},{32,96},{48,496},{64,128},{80,16},{96,160},{112,48... | collective-permute-start | bytes 393224 | tf_op jit(solution)/shard_map/ppermute | solution.py:267
  143.8 48.2 %collective-permute-start.5 = (bf16[64,1024]{1,0:T(8,128)(2,1)S(1)}, bf16[64,1024]{1,0:T(8,128)(2,1)S(1)}, u32[]{:S(2)}, u32[]{:S(2)}) collective-permute-start(bf16[64,1024]{1,0:T(8,128)(2,1)S(1)} %get-tuple-element.28), channel_id=1, source_target_pairs={{0,96},{16,432},{32,128},{48,464},{64,160},{80,496},{96,192},{112,... | collective-permute-start | bytes 393224 | tf_op jit(solution)/shard_map/ppermute | solution.py:267
  149.9 49.3 %collective-permute-start.6 = (bf16[64,1024]{1,0:T(8,128)(2,1)S(1)}, bf16[64,1024]{1,0:T(8,128)(2,1)S(1)}, u32[]{:S(2)}, u32[]{:S(2)}) collective-permute-start(bf16[64,1024]{1,0:T(8,128)(2,1)S(1)} %get-tuple-element.29), channel_id=1, source_target_pairs={{0,128},{16,400},{32,160},{48,432},{64,192},{80,464},{96,224},{112... | collective-permute-start | bytes 393224 | tf_op jit(solution)/shard_map/ppermute | solution.py:267
  153.8 56.1 %collective-permute-start.7 = (bf16[64,1024]{1,0:T(8,128)(2,1)S(1)}, bf16[64,1024]{1,0:T(8,128)(2,1)S(1)}, u32[]{:S(2)}, u32[]{:S(2)}) collective-permute-start(bf16[64,1024]{1,0:T(8,128)(2,1)S(1)} %get-tuple-element.30), channel_id=1, source_target_pairs={{0,160},{16,368},{32,192},{48,400},{64,224},{80,432},{96,256},{112... | collective-permute-start | bytes 393224 | tf_op jit(solution)/shard_map/ppermute | solution.py:267
  180.9 30.0 %collective-permute-start.8 = (bf16[64,1024]{1,0:T(8,128)(2,1)S(1)}, bf16[64,1024]{1,0:T(8,128)(2,1)S(1)}, u32[]{:S(2)}, u32[]{:S(2)}) collective-permute-start(bf16[64,1024]{1,0:T(8,128)(2,1)S(1)} %get-tuple-element.31), channel_id=1, source_target_pairs={{0,192},{16,336},{32,224},{48,368},{64,256},{80,400},{96,288},{112... | collective-permute-start | bytes 393224 | tf_op jit(solution)/shard_map/ppermute | solution.py:267
  211.0 7.0 %copy-start.6 = (bf16[256,512]{1,0:T(8,128)(2,1)S(1)}, bf16[256,512]{1,0:T(8,128)(2,1)}, u32[]{:S(2)}) copy-start(bf16[256,512]{1,0:T(8,128)(2,1)} %copy-done.5) | copy-start | bytes 786436
  211.0 7.0 %collective-permute-start.9 = (bf16[240,1024]{1,0:T(8,128)(2,1)S(1)}, bf16[240,1024]{1,0:T(8,128)(2,1)S(1)}, u32[]{:S(2)}, u32[]{:S(2)}) collective-permute-start(bf16[240,1024]{1,0:T(8,128)(2,1)S(1)} %shard_map.100), channel_id=1, source_target_pairs={{0,16},{16,0},{32,48},{48,32},{64,80},{80,64},{96,112},{112,96},{1... | collective-permute-start | bytes 1474568 | tf_op jit(solution)/shard_map/ppermute | solution.py:292

commit v3 on v1

--- a/solution.py
+++ b/solution.py
@@ -10,15 +10,17 @@
 F32 = jnp.float32
 BF16 = jnp.bfloat16
 LANES = 128
+DEVICES_A_STEP = 4
 VMEM_BYTES = 48 * 1024 * 1024
 ROWS_ROWS = (((1,), (1,)), ((), ()))
 DEPTH_FIRST = (((0,), (0,)), ((), ()))
 
 
-def call(kernel, outs, flops, moved):
+def call(kernel, outs, flops, moved, **how):
     return pl.pallas_call(
         kernel,
         out_shape=outs,
+        **how,
         compiler_params=pltpu.CompilerParams(vmem_limit_bytes=VMEM_BYTES),
         cost_estimate=pl.CostEstimate(flops=flops, bytes_accessed=moved, transcendentals=0),
     )
@@ -44,26 +46,19 @@
     return out
 
 
-def pack_kernel(groups, capacity, dest_ref, ids_ref, codes_ref, grads_ref, inputs_ref, row_ref, input_ref):
-    slot_count, width = input_ref.shape
-    tokens = grads_ref.shape[0]
+def pack_kernel(groups, capacity, dest_ref, ids_ref, codes_ref, grads_ref, row_ref):
+    slot_count = row_ref.shape[0]
+    tokens, width = grads_ref.shape
     picks = pick_matrices(dest_ref, groups, capacity, slot_count)
     pick = functools.reduce(jnp.add, picks)
     row_ref[:, :width] = jnp.dot(pick, grads_ref[...], preferred_element_type=F32).astype(BF16)
     per = ids_ref.shape[1]
     notes = jnp.zeros((slot_count, LANES), F32)
+    number = lax.broadcasted_iota(jnp.int32, (LANES - 2 * per, tokens), 1).astype(F32) + 1.0
     for hop, hop_pick in enumerate(picks):
-        lines = jnp.concatenate(
-            [
-                ids_ref[hop].astype(F32),
-                codes_ref[hop],
-                jnp.zeros((LANES - 2 * per, tokens), F32),
-            ],
-            axis=0,
-        ).astype(BF16)
+        lines = jnp.concatenate([ids_ref[hop].astype(F32), codes_ref[hop], number], axis=0).astype(BF16)
         notes = notes + lax.dot_general(hop_pick, lines, ROWS_ROWS, preferred_element_type=F32)
     row_ref[:, width:] = notes.astype(BF16)
-    input_ref[...] = jnp.dot(pick, inputs_ref[...], preferred_element_type=F32).astype(BF16)
 
 
 def fold(values, per):
@@ -122,8 +117,27 @@
     out_ref[...] = jnp.dot(code, row_ref[:, :width], preferred_element_type=F32).astype(BF16)
 
 
-def enc_kernel(pre_ref, input_ref, out_ref):
-    out_ref[...] = jnp.dot(pre_ref[...], input_ref[...], preferred_element_type=F32).astype(BF16)
+def enc_kernel(per, capacity, tokens, pre_ref, note_ref, input_ref, out_ref, turned_ref, total_ref):
+    step = pl.program_id(0)
+
+    @pl.when(step == 0)
+    def _():
+        turned_ref[...] = pre_ref[...].T
+        total_ref[...] = jnp.zeros_like(total_ref)
+
+    slots = note_ref.shape[0]
+    number = note_ref[:, 2 * per : 2 * per + 1].astype(F32).astype(jnp.int32)
+    device = lax.broadcasted_iota(jnp.int32, (slots, 1), 0) // capacity
+    place = jnp.where(number > 0, device * tokens + number - 1, -1)
+    line = lax.broadcasted_iota(jnp.int32, (slots, input_ref.shape[0]), 1)
+    hot = (line == place).astype(F32).astype(BF16)
+    here = turned_ref[pl.ds(pl.multiple_of(step * slots, slots), slots), :]
+    wide = lax.dot_general(here, hot, DEPTH_FIRST, preferred_element_type=F32).astype(BF16)
+    total_ref[...] += jnp.dot(wide, input_ref[...], preferred_element_type=F32)
+
+    @pl.when(step == pl.num_programs(0) - 1)
+    def _():
+        out_ref[...] = total_ref[...].astype(BF16)
 
 
 def merge_kernel(groups, capacity, dest_ref, back_ref, out_ref):
@@ -144,13 +158,13 @@
     shape = jax.ShapeDtypeStruct
     mac = 2 * slots * width
 
-    send_rows, send_inputs = call(
+    every = lax.all_gather(inputs, "feat", axis=0, tiled=True)
+    send_rows = call(
         functools.partial(pack_kernel, groups, capacity),
-        (shape((slots, width + LANES), BF16), shape((slots, width), BF16)),
-        2 * mac * tokens,
-        4 * slots * width + 4 * tokens * width,
-    )(dest, jnp.transpose(local_ids, (1, 2, 0)), jnp.transpose(code_values, (1, 2, 0)), out_grad, inputs)
-
+        shape((slots, width + LANES), BF16),
+        mac * tokens,
+        2 * slots * width + 2 * tokens * width,
+    )(dest, jnp.transpose(local_ids, (1, 2, 0)), jnp.transpose(code_values, (1, 2, 0)), out_grad)
     rows = lax.all_to_all(
         send_rows.reshape(groups, capacity, width + LANES), "feat", split_axis=0, concat_axis=0, tiled=True
     ).reshape(slots, width + LANES)
@@ -174,10 +188,21 @@
     dec_grad = call(
         functools.partial(dec_kernel, per), shape((features, width), BF16), mac * features, 4 * slots * width
     )(ids, codes, rows)
-    given = lax.all_to_all(
-        send_inputs.reshape(groups, capacity, width), "feat", split_axis=0, concat_axis=0, tiled=True
-    ).reshape(slots, width)
-    enc_grad = call(enc_kernel, shape((features, width), BF16), mac * features, 4 * slots * width)(pre, given)
+    steps = groups // DEVICES_A_STEP
+    enc_grad = call(
+        functools.partial(enc_kernel, per, capacity, tokens),
+        shape((features, width), BF16),
+        2 * groups * tokens * features * width,
+        2 * groups * tokens * width,
+        grid=(steps,),
+        in_specs=[
+            pl.BlockSpec((features, slots), lambda i: (0, 0)),
+            pl.BlockSpec((slots // steps, LANES), lambda i: (i, width // LANES)),
+            pl.BlockSpec((groups * tokens // steps, width), lambda i: (i, 0)),
+        ],
+        out_specs=pl.BlockSpec((features, width), lambda i: (0, 0)),
+        scratch_shapes=[pltpu.VMEM((slots, features), BF16), pltpu.VMEM((features, width), F32)],
+    )(pre, rows, every)
     in_grad = call(
         functools.partial(merge_kernel, groups, capacity),
         shape((tokens, width), BF16),

time: 232 us -> 208 us (0.90)
  waiting for transfers between devices: 102 us -> 54.3 us
  between operations: 0.74 us -> 14.1 us
  blocking collectives: 101 us -> 113 us
  Pallas kernels: 8.11 us -> 17 us
  local copies, waits for them, and re-layouts: 9.6 us -> 3.16 us
  starting transfers between devices: 10.2 us -> 5.71 us
    all_to_all x1 -> x0, waiting for transfers between devices: 51.3 us -> none  [shards(): lax.all_to_all(send_inputs.reshape(groups, capacity, width), 'feat', spli...]
    all_to_all x1, blocking collectives: 78.2 us -> 90 us  [shards(): lax.all_to_all(send_rows.reshape(groups, capacity, width + LANES), 'feat'...]
    pallas_call x2, Pallas kernels: 2.16 us -> 10 us  [the longest x1 9.35 us: shards(): call(functools.partial(enc_kernel, per, capacity, tokens), shape((feature...]
    unnamed x30 -> x14, local copies, waits for them, and re-layouts: 9.6 us -> 3.16 us
    all_to_all x1 -> x0, starting transfers between devices: 5.59 us -> none  [shards(): lax.all_to_all(send_inputs.reshape(groups, capacity, width), 'feat', spli...]
    all_to_all x1, waiting for transfers between devices: 50.7 us -> 53.7 us  [shards(): lax.all_to_all(back.reshape(groups, capacity, width), 'feat', split_axis=...]
  transfers between devices with their start and end apart: 2 -> 2, of which waited for: 2 -> 1; matrix products, arithmetic and copies ran while one was open for 0% -> 0% of each run, Pallas kernels for 2% -> 4%
where the time goes in v3:
time: 208 us; the launch traced here: 207 us
  blocking collectives  113 us (54%)
  waiting for transfers between devices  54.3 us (26%)
  Pallas kernels  17 us (8%)
  between operations  14.1 us (7%)
  starting transfers between devices  5.71 us (3%)
  local copies, waits for them, and re-layouts  3.16 us (2%)
    all_to_all x1, blocking collectives, shards(): lax.all_to_all(send_rows.reshape(groups, capacity, width + LANES), 'feat'...  90 us
    all_to_all x1, waiting for transfers between devices, shards(): lax.all_to_all(back.reshape(groups, capacity, width), 'feat', split_axis=...  53.7 us
    all_to_all x1, blocking collectives, shards(): lax.all_to_all(score, 'tok', split_axis=0, concat_axis=0, tiled=True)  22.8 us
    pallas_call x1, Pallas kernels, shards(): call(functools.partial(enc_kernel, per, capacity, tokens), shape((feature...  9.35 us
    all_to_all x1, starting transfers between devices, shards(): lax.all_to_all(back.reshape(groups, capacity, width), 'feat', split_axis=...  5.67 us
  transfers between devices with their start and end apart: 2, of which 1 were waited for; matrix products, arithmetic and copies ran while one was open for 0% of the time, Pallas kernels for 4%

profile of v3, /device:TPU:1, one launch (start us, length us, event | category | flops | bytes accessed | tf_op | source)
XLA Modules:
  0.0 207.1 jit_solution(4429350992690285907)
XLA Ops:
  7.2 0.0 all-gather.2.cloned.1.call-start
  7.2 0.7 all-gather.2.cloned.1.call-update
  7.9 0.0 copy-start.2
  7.9 0.9 copy-done.2
  8.9 0.0 copy-start.3
  8.9 0.8 copy-done.3
  9.6 0.0 copy-start.4
  9.6 0.8 copy-done.4
  10.4 0.0 copy-start.5
  10.4 0.7 copy-done.5
  11.0 0.6 shard_map.94
  11.7 0.0 copy-start.1
  11.7 90.0 %all_to_all.15 = bf16[32,16,1152]{2,1,0:T(8,128)(2,1)S(1)} all-to-all(bf16[32,16,1152]{2,1,0:T(8,128)(2,1)S(1)} %bitcast.10), channel_id=1, replica_groups=mesh['feat'=32,'tok'=16] {'feat'}, dimensions={0} | all-to-all | bytes 2359296 | tf_op jit(solution)/shard_map/all_to_all | solution.py:168
  101.7 0.0 copy-done.1
  101.7 0.9 shard_map.95
  102.6 0.0 copy-start
  102.6 22.8 %all_to_all.16.score_ref = f32[16,128,128]{2,1,0:T(8,128)S(1)} all-to-all(f32[16,128,128]{2,1,0:T(8,128)S(1)} %get-tuple-element.8), channel_id=1, replica_groups=mesh['feat'=32,'tok'=16] {'tok'}, dimensions={0} | all-to-all | bytes 2097152 | tf_op jit(solution)/shard_map/all_to_all | solution.py:178
  125.4 0.0 copy-done
  125.4 2.7 %shard_map.96 = (bf16[256,512]{1,0:T(8,128)(2,1)S(1)}, bf16[512,1024]{1,0:T(8,128)(2,1)}) custom-call(f32[16,128,128]{2,1,0:T(8,128)S(1)} %all_to_all.16.score_ref, f32[128,128]{1,0:T(8,128)S(1)} %get-tuple-element.9.ids_ref, bf16[256,1024]{1,0:T(8,128)(2,1)S(1)} %copy-done), custom_call_target="tpu_custom_call" | custom-call | flops 268435456 | bytes 1048576 | tf_op jit(solution)/shard_map/pallas_call | solution.py:179
  128.1 5.7 %all-to-all-start.2 = ((bf16[32,16,1024]{2,1,0:T(8,128)(2,1)}), bf16[32,16,1024]{2,1,0:T(8,128)(2,1)S(1)}, u32[]{:S(2)}, u32[]{:S(2)}) async-start(bf16[32,16,1024]{2,1,0:T(8,128)(2,1)} %bitcast.5), calls=%async_computation.2 | async-start | bytes 2097152 | tf_op jit(solution)/shard_map/all_to_all | solution.py:185
  133.7 0.0 copy-start.6
  133.8 2.2 %shard_map.98 = bf16[256,1024]{1,0:T(8,128)(2,1)} custom-call(f32[128,128]{1,0:T(8,128)S(1)} %get-tuple-element.9.ids_ref, f32[128,128]{1,0:T(8,128)S(1)} %get-tuple-element.11.codes_ref, bf16[512,1152]{1,0:T(8,128)(2,1)S(1)} %bitcast.8), custom_call_target="tpu_custom_call" | custom-call | flops 268435456 | bytes 2097152 | tf_op jit(solution)/shard_map/pallas_call | solution.py:188
  136.0 53.7 %all-to-all-done.2 = bf16[32,16,1024]{2,1,0:T(8,128)(2,1)S(1)} async-done(((bf16[32,16,1024]{2,1,0:T(8,128)(2,1)}), bf16[32,16,1024]{2,1,0:T(8,128)(2,1)S(1)}, u32[]{:S(2)}, u32[]{:S(2)}) %all-to-all-start.2) | async-done | bytes 1048608 | tf_op jit(solution)/shard_map/all_to_all | solution.py:185
  189.7 0.0 copy-done.6
  189.7 1.2 shard_map.99
  190.9 0.0 all-gather.2.cloned.1.call-done.input_ref
  190.9 9.3 %shard_map.97 = bf16[256,1024]{1,0:T(8,128)(2,1)} custom-call(bf16[256,512]{1,0:T(8,128)(2,1)S(1)} %get-tuple-element.10.pre_ref, bf16[512,1152]{1,0:T(8,128)(2,1)S(1)} %bitcast.9, bf16[4096,1024]{1,0:T(8,128)(2,1)} %all-gather.2.cloned.1.call-done.input_ref), custom_call_target="tpu_custom_call" | custom-call | flops 2147483648 | bytes 8388608 | tf_op jit(solution)/shard_map/pallas_call | solution.py:192
Async XLA Ops:
  7.2 183.7 %all-gather.2.cloned.1.call-start = ((), (), s32[]{:S(2)}) async-start(), calls=%async_computation.3 | async-start | bytes 8650752 | tf_op jit(solution)/shard_map/all_gather | solution.py:161
  7.9 1.0 copy-start.2
  8.9 0.8 copy-start.3
  9.6 0.8 copy-start.4
  10.4 0.7 copy-start.5
  11.7 90.0 %copy-start.1 = (bf16[256,1024]{1,0:T(8,128)(2,1)S(1)}, bf16[256,1024]{1,0:T(8,128)(2,1)}, u32[]{:S(2)}) copy-start(bf16[256,1024]{1,0:T(8,128)(2,1)} %dec_ref.1) | copy-start | bytes 1572868
  102.6 22.8 %copy-start = (bf16[256,1024]{1,0:T(8,128)(2,1)S(1)}, bf16[256,1024]{1,0:T(8,128)(2,1)}, u32[]{:S(2)}) copy-start(bf16[256,1024]{1,0:T(8,128)(2,1)} %enc_ref.1) | copy-start | bytes 1572868
  128.1 61.6 %all-to-all-start.2 = ((bf16[32,16,1024]{2,1,0:T(8,128)(2,1)}), bf16[32,16,1024]{2,1,0:T(8,128)(2,1)S(1)}, u32[]{:S(2)}, u32[]{:S(2)}) async-start(bf16[32,16,1024]{2,1,0:T(8,128)(2,1)} %bitcast.5), calls=%async_computation.2 | async-start | bytes 2097152 | tf_op jit(solution)/shard_map/all_to_all | solution.py:185
  133.7 55.9 %copy-start.6 = (s32[128,2]{0,1:T(2,128)S(1)}, s32[128,2]{0,1:T(2,128)}, u32[]{:S(2)}) copy-start(s32[128,2]{0,1:T(2,128)} %param.11) | copy-start | bytes 3076
Sparse Core Ops, SparseCore 0:
  10.1 128.0 all-gather.1

commit v4 on v3

--- a/solution.py
+++ b/solution.py
@@ -11,19 +11,27 @@
 BF16 = jnp.bfloat16
 LANES = 128
 DEVICES_A_STEP = 4
+PARTS = 4
 VMEM_BYTES = 48 * 1024 * 1024
 ROWS_ROWS = (((1,), (1,)), ((), ()))
 DEPTH_FIRST = (((0,), (0,)), ((), ()))
 
 
-def call(kernel, outs, flops, moved, **how):
+def call(kernel, outs, flops, moved, operands, after=(), limit=VMEM_BYTES, **how):
+    count = len(operands)
+
+    def body(*refs):
+        kernel(*refs[:count], *refs[count + len(after) :])
+
+    specs = how.pop("in_specs", [pl.BlockSpec(memory_space=pltpu.VMEM)] * count)
     return pl.pallas_call(
-        kernel,
+        body,
         out_shape=outs,
+        in_specs=list(specs) + [pl.BlockSpec(memory_space=pl.ANY)] * len(after),
+        compiler_params=pltpu.CompilerParams(vmem_limit_bytes=limit),
+        cost_estimate=pl.CostEstimate(flops=flops, bytes_accessed=moved, transcendentals=0),
         **how,
-        compiler_params=pltpu.CompilerParams(vmem_limit_bytes=VMEM_BYTES),
-        cost_estimate=pl.CostEstimate(flops=flops, bytes_accessed=moved, transcendentals=0),
-    )
+    )(*operands, *after)
 
 
 def pick_matrices(dest_ref, groups, capacity, slot_count):
@@ -46,19 +54,36 @@
     return out
 
 
-def pack_kernel(groups, capacity, dest_ref, ids_ref, codes_ref, grads_ref, row_ref):
+def pack_kernel(groups, capacity, dest_hbm, ids_hbm, codes_hbm, grads_hbm, row_hbm, *scratch):
+    dest_ref, ids_ref, codes_ref, grads_ref, row_ref, sems = scratch
+    pairs = ((dest_hbm, dest_ref), (ids_hbm, ids_ref), (codes_hbm, codes_ref), (grads_hbm, grads_ref))
+    copies = [pltpu.make_async_copy(a, b, sems.at[i]) for i, (a, b) in enumerate(pairs)]
+    for copy in copies:
+        copy.start()
     slot_count = row_ref.shape[0]
     tokens, width = grads_ref.shape
+    copies[0].wait()
     picks = pick_matrices(dest_ref, groups, capacity, slot_count)
     pick = functools.reduce(jnp.add, picks)
-    row_ref[:, :width] = jnp.dot(pick, grads_ref[...], preferred_element_type=F32).astype(BF16)
     per = ids_ref.shape[1]
     notes = jnp.zeros((slot_count, LANES), F32)
     number = lax.broadcasted_iota(jnp.int32, (LANES - 2 * per, tokens), 1).astype(F32) + 1.0
+    copies[1].wait()
+    copies[2].wait()
     for hop, hop_pick in enumerate(picks):
         lines = jnp.concatenate([ids_ref[hop].astype(F32), codes_ref[hop], number], axis=0).astype(BF16)
         notes = notes + lax.dot_general(hop_pick, lines, ROWS_ROWS, preferred_element_type=F32)
     row_ref[:, width:] = notes.astype(BF16)
+    copies[3].wait()
+    height = slot_count // PARTS
+    sends = []
+    for part in range(PARTS):
+        lines = slice(part * height, (part + 1) * height)
+        row_ref[lines, :width] = jnp.dot(pick[lines], grads_ref[...], preferred_element_type=F32).astype(BF16)
+        sends.append(pltpu.make_async_copy(row_ref.at[lines], row_hbm.at[lines], sems.at[len(copies) + part]))
+        sends[-1].start()
+    for send in sends:
+        send.wait()
 
 
 def fold(values, per):
@@ -164,7 +189,19 @@
         shape((slots, width + LANES), BF16),
         mac * tokens,
         2 * slots * width + 2 * tokens * width,
-    )(dest, jnp.transpose(local_ids, (1, 2, 0)), jnp.transpose(code_values, (1, 2, 0)), out_grad)
+        (dest, jnp.transpose(local_ids, (1, 2, 0)), jnp.transpose(code_values, (1, 2, 0)), out_grad),
+        limit=None,
+        in_specs=[pl.BlockSpec(memory_space=pl.ANY)] * 4,
+        out_specs=pl.BlockSpec(memory_space=pl.ANY),
+        scratch_shapes=[
+            pltpu.VMEM((hops, tokens), jnp.int32),
+            pltpu.VMEM((hops, per, tokens), jnp.int32),
+            pltpu.VMEM((hops, per, tokens), F32),
+            pltpu.VMEM((tokens, width), BF16),
+            pltpu.VMEM((slots, width + LANES), BF16),
+            pltpu.SemaphoreType.DMA((4 + PARTS,)),
+        ],
+    )
     rows = lax.all_to_all(
         send_rows.reshape(groups, capacity, width + LANES), "feat", split_axis=0, concat_axis=0, tiled=True
     ).reshape(slots, width + LANES)
@@ -174,26 +211,33 @@
         (shape((slices, held, LANES), F32), shape((LANES, held), F32), shape((LANES, held), F32)),
         mac * features,
         2 * slots * width,
-    )(rows, dec_rows)
+        (rows, dec_rows),
+    )
     score = lax.all_to_all(score, "tok", split_axis=0, concat_axis=0, tiled=True)
     pre, back = call(
         functools.partial(back_kernel, per),
         (shape((features, slots), BF16), shape((slots, width), BF16)),
         mac * features,
         2 * slots * width,
-    )(score, ids, enc_rows)
+        (score, ids, enc_rows),
+    )
     returned = lax.all_to_all(
         back.reshape(groups, capacity, width), "feat", split_axis=0, concat_axis=0, tiled=True
     ).reshape(slots, width)
     dec_grad = call(
-        functools.partial(dec_kernel, per), shape((features, width), BF16), mac * features, 4 * slots * width
-    )(ids, codes, rows)
+        functools.partial(dec_kernel, per),
+        shape((features, width), BF16),
+        mac * features,
+        4 * slots * width,
+        (ids, codes, rows),
+    )
     steps = groups // DEVICES_A_STEP
     enc_grad = call(
         functools.partial(enc_kernel, per, capacity, tokens),
         shape((features, width), BF16),
         2 * groups * tokens * features * width,
         2 * groups * tokens * width,
+        (pre, rows, every),
         grid=(steps,),
         in_specs=[
             pl.BlockSpec((features, slots), lambda i: (0, 0)),
@@ -202,13 +246,16 @@
         ],
         out_specs=pl.BlockSpec((features, width), lambda i: (0, 0)),
         scratch_shapes=[pltpu.VMEM((slots, features), BF16), pltpu.VMEM((features, width), F32)],
-    )(pre, rows, every)
+    )
     in_grad = call(
         functools.partial(merge_kernel, groups, capacity),
         shape((tokens, width), BF16),
         mac * tokens,
         4 * slots * width,
-    )(dest, returned)
+        (dest, returned),
+        (enc_grad, dec_grad),
+        limit=None,
+    )
     return (enc_grad, dec_grad, in_grad)
 
 

time: 208 us -> 199 us (0.957)
  waiting for transfers between devices: 54.3 us -> 44.5 us
  Pallas kernels: 17 us -> 20.3 us
  local copies, waits for them, and re-layouts: 3.16 us -> 0.97 us
    all_to_all x1, waiting for transfers between devices: 53.7 us -> 41.7 us  [shards(): lax.all_to_all(back.reshape(groups, capacity, width), 'feat', split_axis=...]
    pallas_call x6, Pallas kernels: 17 us -> 20.3 us  [call(): pl.pallas_call(body, out_shape=outs, in_specs=list(specs) + [pl.BlockSpec...]
    unnamed x14 -> x6, local copies, waits for them, and re-layouts: 3.16 us -> 0.97 us
    all_gather x1, waiting for transfers between devices: 0.01 us -> 2.1 us  [shards(): every = lax.all_gather(inputs, 'feat', axis=0, tiled=True)]
  transfers between devices with their start and end apart: 2 -> 2, of which waited for: 1 -> 2; matrix products, arithmetic and copies ran while one was open for 0% -> 0% of each run, Pallas kernels for 4% -> 9%
where the time goes in v4:
time: 199 us; the launch traced here: 198 us
  blocking collectives  113 us (57%)
  waiting for transfers between devices  44.5 us (22%)
  Pallas kernels  20.3 us (10%)
  between operations  14.1 us (7%)
  starting transfers between devices  5.79 us (3%)
    all_to_all x1, blocking collectives, shards(): lax.all_to_all(send_rows.reshape(groups, capacity, width + LANES), 'feat'...  90.3 us
    all_to_all x1, waiting for transfers between devices, shards(): lax.all_to_all(back.reshape(groups, capacity, width), 'feat', split_axis=...  41.7 us
    all_to_all x1, blocking collectives, shards(): lax.all_to_all(score, 'tok', split_axis=0, concat_axis=0, tiled=True)  22.5 us
    pallas_call x6, Pallas kernels, call(): pl.pallas_call(body, out_shape=outs, in_specs=list(specs) + [pl.BlockSpec...  20.3 us
    all_to_all x1, starting transfers between devices, shards(): lax.all_to_all(back.reshape(groups, capacity, width), 'feat', split_axis=...  5.75 us
  transfers between devices with their start and end apart: 2, of which 2 were waited for; matrix products, arithmetic and copies ran while one was open for 0% of the time, Pallas kernels for 9%

profile of v4, /device:TPU:1, one launch (start us, length us, event | category | flops | bytes accessed | tf_op | source)
XLA Modules:
  0.0 198.4 jit_solution(10812981950141164642)
XLA Ops:
  7.2 0.0 all-gather.2.cloned.1.call-start
  7.2 0.7 all-gather.2.cloned.1.call-update
  7.9 2.7 %shard_map.94 = bf16[512,1152]{1,0:T(8,128)(2,1)} custom-call(s32[2,128]{1,0:T(2,128)} %bitcast.14, s32[2,32,128]{2,1,0:T(8,128)} %bitcast.12, f32[2,32,128]{2,1,0:T(8,128)} %bitcast.13, bf16[128,1024]{1,0:T(8,128)(2,1)} %refs_3_.1), custom_call_target="tpu_custom_call" | custom-call | flops 134217728 | bytes 1310720 | tf_op jit(solution)/shard_map/pallas_call | solution.py:27
  10.6 0.0 copy-start.1
  10.6 90.3 %all_to_all.15 = bf16[32,16,1152]{2,1,0:T(8,128)(2,1)S(1)} all-to-all(bf16[32,16,1152]{2,1,0:T(8,128)(2,1)} %bitcast.10), channel_id=1, replica_groups=mesh['feat'=32,'tok'=16] {'feat'}, dimensions={0} | all-to-all | bytes 2359296 | tf_op jit(solution)/shard_map/all_to_all | solution.py:205
  100.9 0.0 copy-done.1
  100.9 0.9 shard_map.95
  101.8 0.0 copy-start
  101.8 22.5 %all_to_all.16.refs_0_ = f32[16,128,128]{2,1,0:T(8,128)S(1)} all-to-all(f32[16,128,128]{2,1,0:T(8,128)S(1)} %get-tuple-element.8), channel_id=1, replica_groups=mesh['feat'=32,'tok'=16] {'tok'}, dimensions={0} | all-to-all | bytes 2097152 | tf_op jit(solution)/shard_map/all_to_all | solution.py:216
  124.3 0.0 copy-done
  124.3 2.7 %shard_map.96 = (bf16[256,512]{1,0:T(8,128)(2,1)S(1)}, bf16[512,1024]{1,0:T(8,128)(2,1)}) custom-call(f32[16,128,128]{2,1,0:T(8,128)S(1)} %all_to_all.16.refs_0_, f32[128,128]{1,0:T(8,128)S(1)} %get-tuple-element.9.refs_1_.refs_0_, bf16[256,1024]{1,0:T(8,128)(2,1)S(1)} %copy-done), custom_call_target="tpu_custom_call" | custom-call | flops 268435456 | bytes 1048576 | tf_op jit(solution)/shard_map/pallas_call | solution.py:27
  127.0 5.8 %all-to-all-start.2 = ((bf16[32,16,1024]{2,1,0:T(8,128)(2,1)}), bf16[32,16,1024]{2,1,0:T(8,128)(2,1)S(1)}, u32[]{:S(2)}, u32[]{:S(2)}) async-start(bf16[32,16,1024]{2,1,0:T(8,128)(2,1)} %bitcast.5), calls=%async_computation.2 | async-start | bytes 2097152 | tf_op jit(solution)/shard_map/all_to_all | solution.py:224
  132.8 2.2 %shard_map.98.refs_3_ = bf16[256,1024]{1,0:T(8,128)(2,1)} custom-call(f32[128,128]{1,0:T(8,128)S(1)} %get-tuple-element.9.refs_1_.refs_0_, f32[128,128]{1,0:T(8,128)S(1)} %get-tuple-element.11.refs_1_, bf16[512,1152]{1,0:T(8,128)(2,1)S(1)} %bitcast.8), custom_call_target="tpu_custom_call" | custom-call | flops 268435456 | bytes 2097152 | tf_op jit(solution)/shard_map/pallas_call | solution.py:27
  135.0 2.1 %all-gather.2.cloned.1.call-done.refs_2_ = bf16[4096,1024]{1,0:T(8,128)(2,1)} async-done(((bf16[128,1024]{1,0:T(8,128)(2,1)}), bf16[4096,1024]{1,0:T(8,128)(2,1)}) %all-gather.2.cloned.1.call-update) | async-done | bytes 8388624 | tf_op jit(solution)/shard_map/all_gather | solution.py:186
  137.1 9.4 %shard_map.97.refs_2_ = bf16[256,1024]{1,0:T(8,128)(2,1)} custom-call(bf16[256,512]{1,0:T(8,128)(2,1)S(1)} %get-tuple-element.10.refs_0_, bf16[512,1152]{1,0:T(8,128)(2,1)S(1)} %bitcast.9, bf16[4096,1024]{1,0:T(8,128)(2,1)} %all-gather.2.cloned.1.call-done.refs_2_), custom_call_target="tpu_custom_call" | custom-call | flops 2147483648 | bytes 8388608 | tf_op jit(solution)/shard_map/pallas_call | solution.py:27
  146.5 41.7 %all-to-all-done.2 = bf16[32,16,1024]{2,1,0:T(8,128)(2,1)S(1)} async-done(((bf16[32,16,1024]{2,1,0:T(8,128)(2,1)}), bf16[32,16,1024]{2,1,0:T(8,128)(2,1)S(1)}, u32[]{:S(2)}, u32[]{:S(2)}) %all-to-all-start.2) | async-done | bytes 1048608 | tf_op jit(solution)/shard_map/all_to_all | solution.py:224
  188.2 0.0 copy-start.2
  188.2 1.0 copy-done.2
  189.2 2.4 %shard_map.99 = bf16[128,1024]{1,0:T(8,128)(2,1)} custom-call(s32[2,128]{1,0:T(2,128)} %bitcast.15, bf16[512,1024]{1,0:T(8,128)(2,1)} %bitcast.11, bf16[256,1024]{1,0:T(8,128)(2,1)} %shard_map.97.refs_2_, bf16[256,1024]{1,0:T(8,128)(2,1)} %shard_map.98.refs_3_), custom_call_target="tpu_custom_call" | custom-call | flops 134217728 | bytes 2097152 | tf_op jit(solution)/shard_map/pallas_call | solution.py:27
Async XLA Ops:
  7.2 129.9 %all-gather.2.cloned.1.call-start = ((), (), s32[]{:S(2)}) async-start(), calls=%async_computation.3 | async-start | bytes 8650752 | tf_op jit(solution)/shard_map/all_gather | solution.py:186
  10.6 90.3 %copy-start.1 = (bf16[256,1024]{1,0:T(8,128)(2,1)S(1)}, bf16[256,1024]{1,0:T(8,128)(2,1)}, u32[]{:S(2)}) copy-start(bf16[256,1024]{1,0:T(8,128)(2,1)} %refs_1_.1) | copy-start | bytes 1572868
  101.8 22.5 %copy-start = (bf16[256,1024]{1,0:T(8,128)(2,1)S(1)}, bf16[256,1024]{1,0:T(8,128)(2,1)}, u32[]{:S(2)}) copy-start(bf16[256,1024]{1,0:T(8,128)(2,1)} %refs_2_.1) | copy-start | bytes 1572868
  127.0 61.2 %all-to-all-start.2 = ((bf16[32,16,1024]{2,1,0:T(8,128)(2,1)}), bf16[32,16,1024]{2,1,0:T(8,128)(2,1)S(1)}, u32[]{:S(2)}, u32[]{:S(2)}) async-start(bf16[32,16,1024]{2,1,0:T(8,128)(2,1)} %bitcast.5), calls=%async_computation.2 | async-start | bytes 2097152 | tf_op jit(solution)/shard_map/all_to_all | solution.py:224
  188.2 1.0 copy-start.2
Sparse Core Ops, SparseCore 0:
  10.1 126.9 all-gather.1

commit v5 on v4

--- a/solution.py
+++ b/solution.py
@@ -142,13 +142,14 @@
     out_ref[...] = jnp.dot(code, row_ref[:, :width], preferred_element_type=F32).astype(BF16)
 
 
-def enc_kernel(per, capacity, tokens, pre_ref, note_ref, input_ref, out_ref, turned_ref, total_ref):
+def enc_kernel(per, capacity, tokens, pre_ref, note_ref, input_ref, out_ref, mark_ref, turned_ref, total_ref):
     step = pl.program_id(0)
 
     @pl.when(step == 0)
     def _():
         turned_ref[...] = pre_ref[...].T
         total_ref[...] = jnp.zeros_like(total_ref)
+        mark_ref[...] = jnp.zeros_like(mark_ref)
 
     slots = note_ref.shape[0]
     number = note_ref[:, 2 * per : 2 * per + 1].astype(F32).astype(jnp.int32)
@@ -232,9 +233,9 @@
         (ids, codes, rows),
     )
     steps = groups // DEVICES_A_STEP
-    enc_grad = call(
+    enc_grad, mark = call(
         functools.partial(enc_kernel, per, capacity, tokens),
-        shape((features, width), BF16),
+        (shape((features, width), BF16), shape((8, LANES), F32)),
         2 * groups * tokens * features * width,
         2 * groups * tokens * width,
         (pre, rows, every),
@@ -244,7 +245,10 @@
             pl.BlockSpec((slots // steps, LANES), lambda i: (i, width // LANES)),
             pl.BlockSpec((groups * tokens // steps, width), lambda i: (i, 0)),
         ],
-        out_specs=pl.BlockSpec((features, width), lambda i: (0, 0)),
+        out_specs=(
+            pl.BlockSpec((features, width), lambda i: (0, 0)),
+            pl.BlockSpec((8, LANES), lambda i: (0, 0)),
+        ),
         scratch_shapes=[pltpu.VMEM((slots, features), BF16), pltpu.VMEM((features, width), F32)],
     )
     in_grad = call(
@@ -253,8 +257,7 @@
         mac * tokens,
         4 * slots * width,
         (dest, returned),
-        (enc_grad, dec_grad),
-        limit=None,
+        (mark,),
     )
     return (enc_grad, dec_grad, in_grad)
 

time: 199 us -> 197 us (0.990)
  no operation moved by 1% of the time
where the time goes in v5:
time: 197 us
  blocking collectives  113 us (57%)
  waiting for transfers between devices  44.9 us (23%)
  Pallas kernels  19.1 us (10%)
  between operations  14.1 us (7%)
  starting transfers between devices  5.78 us (3%)
    all_to_all x1, blocking collectives, shards(): lax.all_to_all(send_rows.reshape(groups, capacity, width + LANES), 'feat'...  90.3 us
    all_to_all x1, waiting for transfers between devices, shards(): lax.all_to_all(back.reshape(groups, capacity, width), 'feat', split_axis=...  41.9 us
    all_to_all x1, blocking collectives, shards(): lax.all_to_all(score, 'tok', split_axis=0, concat_axis=0, tiled=True)  22.5 us
    pallas_call x6, Pallas kernels, call(): pl.pallas_call(body, out_shape=outs, in_specs=list(specs) + [pl.BlockSpec...  19.1 us
    all_to_all x1, starting transfers between devices, shards(): lax.all_to_all(back.reshape(groups, capacity, width), 'feat', split_axis=...  5.74 us
  transfers between devices with their start and end apart: 2, of which 2 were waited for; matrix products, arithmetic and copies ran while one was open for 0% of the time, Pallas kernels for 9%

profile of v5, /device:TPU:1, one launch (start us, length us, event | category | flops | bytes accessed | tf_op | source)
XLA Modules:
  0.0 196.6 jit_solution(11747368017419176760)
XLA Ops:
  7.2 0.0 all-gather.2.cloned.1.call-start
  7.2 0.7 all-gather.2.cloned.1.call-update
  7.9 2.7 %shard_map.94 = bf16[512,1152]{1,0:T(8,128)(2,1)} custom-call(s32[2,128]{1,0:T(2,128)} %bitcast.11, s32[2,32,128]{2,1,0:T(8,128)} %bitcast.14, f32[2,32,128]{2,1,0:T(8,128)} %bitcast.15, bf16[128,1024]{1,0:T(8,128)(2,1)} %refs_3_.1), custom_call_target="tpu_custom_call" | custom-call | flops 134217728 | bytes 1310720 | tf_op jit(solution)/shard_map/pallas_call | solution.py:27
  10.6 0.0 copy-start.1
  10.6 90.3 %all_to_all.15 = bf16[32,16,1152]{2,1,0:T(8,128)(2,1)S(1)} all-to-all(bf16[32,16,1152]{2,1,0:T(8,128)(2,1)} %bitcast.13), channel_id=1, replica_groups=mesh['feat'=32,'tok'=16] {'feat'}, dimensions={0} | all-to-all | bytes 2359296 | tf_op jit(solution)/shard_map/all_to_all | solution.py:206
  100.9 0.0 copy-done.1
  100.9 0.9 shard_map.95
  101.8 0.0 copy-start
  101.8 22.5 %all_to_all.16.refs_0_ = f32[16,128,128]{2,1,0:T(8,128)S(1)} all-to-all(f32[16,128,128]{2,1,0:T(8,128)S(1)} %get-tuple-element.10), channel_id=1, replica_groups=mesh['feat'=32,'tok'=16] {'tok'}, dimensions={0} | all-to-all | bytes 2097152 | tf_op jit(solution)/shard_map/all_to_all | solution.py:217
  124.3 0.0 copy-done
  124.3 2.7 %shard_map.96 = (bf16[256,512]{1,0:T(8,128)(2,1)S(1)}, bf16[512,1024]{1,0:T(8,128)(2,1)}) custom-call(f32[16,128,128]{2,1,0:T(8,128)S(1)} %all_to_all.16.refs_0_, f32[128,128]{1,0:T(8,128)S(1)} %get-tuple-element.11.refs_1_.refs_0_, bf16[256,1024]{1,0:T(8,128)(2,1)S(1)} %copy-done), custom_call_target="tpu_custom_call" | custom-call | flops 268435456 | bytes 1048576 | tf_op jit(solution)/shard_map/pallas_call | solution.py:27
  127.0 5.7 %all-to-all-start.2 = ((bf16[32,16,1024]{2,1,0:T(8,128)(2,1)}), bf16[32,16,1024]{2,1,0:T(8,128)(2,1)S(1)}, u32[]{:S(2)}, u32[]{:S(2)}) async-start(bf16[32,16,1024]{2,1,0:T(8,128)(2,1)} %bitcast.5), calls=%async_computation.2 | async-start | bytes 2097152 | tf_op jit(solution)/shard_map/all_to_all | solution.py:225
  132.8 2.2 %shard_map.98 = bf16[256,1024]{1,0:T(8,128)(2,1)} custom-call(f32[128,128]{1,0:T(8,128)S(1)} %get-tuple-element.11.refs_1_.refs_0_, f32[128,128]{1,0:T(8,128)S(1)} %get-tuple-element.14.refs_1_, bf16[512,1152]{1,0:T(8,128)(2,1)S(1)} %bitcast.8), custom_call_target="tpu_custom_call" | custom-call | flops 268435456 | bytes 2097152 | tf_op jit(solution)/shard_map/pallas_call | solution.py:27
  135.0 2.3 %all-gather.2.cloned.1.call-done.refs_2_ = bf16[4096,1024]{1,0:T(8,128)(2,1)} async-done(((bf16[128,1024]{1,0:T(8,128)(2,1)}), bf16[4096,1024]{1,0:T(8,128)(2,1)}) %all-gather.2.cloned.1.call-update) | async-done | bytes 8388624 | tf_op jit(solution)/shard_map/all_gather | solution.py:187
  137.3 0.0 copy-start.2
  137.3 9.4 %shard_map.97 = (bf16[256,1024]{1,0:T(8,128)(2,1)}, f32[8,128]{1,0:T(8,128)S(1)}) custom-call(bf16[256,512]{1,0:T(8,128)(2,1)S(1)} %get-tuple-element.12.refs_0_, bf16[512,1152]{1,0:T(8,128)(2,1)S(1)} %bitcast.9, bf16[4096,1024]{1,0:T(8,128)(2,1)} %all-gather.2.cloned.1.call-done.refs_2_), custom_call_target="tpu_custom_call" | custom-call | flops 2147483648 | bytes 8388608 | tf_op jit(solution)/shard_map/pallas_call | solution.py:27
  146.7 41.9 %all-to-all-done.2 = bf16[32,16,1024]{2,1,0:T(8,128)(2,1)S(1)} async-done(((bf16[32,16,1024]{2,1,0:T(8,128)(2,1)}), bf16[32,16,1024]{2,1,0:T(8,128)(2,1)S(1)}, u32[]{:S(2)}, u32[]{:S(2)}) %all-to-all-start.2) | async-done | bytes 1048608 | tf_op jit(solution)/shard_map/all_to_all | solution.py:225
  188.6 0.0 copy-done.2
  188.6 1.2 shard_map.99
Async XLA Ops:
  7.2 130.2 %all-gather.2.cloned.1.call-start = ((), (), s32[]{:S(2)}) async-start(), calls=%async_computation.3 | async-start | bytes 8650752 | tf_op jit(solution)/shard_map/all_gather | solution.py:187
  10.6 90.3 %copy-start.1 = (bf16[256,1024]{1,0:T(8,128)(2,1)S(1)}, bf16[256,1024]{1,0:T(8,128)(2,1)}, u32[]{:S(2)}) copy-start(bf16[256,1024]{1,0:T(8,128)(2,1)} %refs_1_.1) | copy-start | bytes 1572868
  101.8 22.5 %copy-start = (bf16[256,1024]{1,0:T(8,128)(2,1)S(1)}, bf16[256,1024]{1,0:T(8,128)(2,1)}, u32[]{:S(2)}) copy-start(bf16[256,1024]{1,0:T(8,128)(2,1)} %refs_2_.1) | copy-start | bytes 1572868
  127.0 61.5 %all-to-all-start.2 = ((bf16[32,16,1024]{2,1,0:T(8,128)(2,1)}), bf16[32,16,1024]{2,1,0:T(8,128)(2,1)S(1)}, u32[]{:S(2)}, u32[]{:S(2)}) async-start(bf16[32,16,1024]{2,1,0:T(8,128)(2,1)} %bitcast.5), calls=%async_computation.2 | async-start | bytes 2097152 | tf_op jit(solution)/shard_map/all_to_all | solution.py:225
  137.3 51.3 %copy-start.2 = (s32[128,2]{0,1:T(2,128)S(1)}, s32[128,2]{0,1:T(2,128)}, u32[]{:S(2)}) copy-start(s32[128,2]{0,1:T(2,128)} %param.11) | copy-start | bytes 3076
Sparse Core Ops, SparseCore 0:
  10.1 127.1 all-gather.1

commit v6 on v5

--- a/solution.py
+++ b/solution.py
@@ -12,6 +12,7 @@
 LANES = 128
 DEVICES_A_STEP = 4
 PARTS = 4
+SCALE = 128.0
 VMEM_BYTES = 48 * 1024 * 1024
 ROWS_ROWS = (((1,), (1,)), ((), ()))
 DEPTH_FIRST = (((0,), (0,)), ((), ()))
@@ -107,9 +108,7 @@
     for part in range(1, dec_ref.shape[0] // LANES):
         here = jnp.take_along_axis(scores[:, part * LANES : (part + 1) * LANES], low, axis=1)
         chosen = jnp.where(ids >= part * LANES, here, chosen)
-    folded = fold(chosen, per)
-    for copy in range(score_ref.shape[0]):
-        score_ref[copy] = folded
+    score_ref[...] = fold(chosen, per)
     ids_ref[...] = fold(notes, per).T
     codes_ref[...] = fold(pltpu.roll(notes, LANES - per, 1), per).T
 
@@ -127,10 +126,7 @@
 
 
 def back_kernel(per, score_ref, ids_ref, enc_ref, pre_ref, back_ref):
-    total = score_ref[0]
-    for copy in range(1, score_ref.shape[0]):
-        total = total + score_ref[copy]
-    rounded = total.astype(BF16).astype(F32).T
+    rounded = score_ref[...].astype(BF16).astype(F32).T
     pre = spread(ids_ref[...], rounded, enc_ref.shape[0], per)
     pre_ref[...] = pre
     back_ref[...] = lax.dot_general(pre, enc_ref[...], DEPTH_FIRST, preferred_element_type=F32).astype(BF16)
@@ -209,12 +205,14 @@
     held = slots * per // LANES
     score, ids, codes = call(
         functools.partial(score_kernel, per),
-        (shape((slices, held, LANES), F32), shape((LANES, held), F32), shape((LANES, held), F32)),
+        (shape((held, LANES), F32), shape((LANES, held), F32), shape((LANES, held), F32)),
         mac * features,
         2 * slots * width,
         (rows, dec_rows),
     )
-    score = lax.all_to_all(score, "tok", split_axis=0, concat_axis=0, tiled=True)
+    parts = jnp.broadcast_to((score * SCALE).astype(jnp.float16), (slices, held, LANES))
+    parts = lax.all_to_all(parts, "tok", split_axis=0, concat_axis=0, tiled=True)
+    score = jnp.sum(parts.astype(F32), axis=0) * (1.0 / SCALE)
     pre, back = call(
         functools.partial(back_kernel, per),
         (shape((features, slots), BF16), shape((slots, width), BF16)),

time: 197 us -> 191 us (0.970); the launches traced: 197 us -> 188 us
  blocking collectives: 113 us -> 107 us
  waiting for transfers between devices: 44.9 us -> 42.1 us
    all_to_all x1, waiting for transfers between devices: 41.9 us -> 12.9 us  [shards(): lax.all_to_all(back.reshape(groups, capacity, width), 'feat', split_axis=...]
    all_gather x1, waiting for transfers between devices: 2.31 us -> 28.4 us  [shards(): every = lax.all_gather(inputs, 'feat', axis=0, tiled=True)]
    all_to_all x1, blocking collectives: 22.5 us -> 16.9 us  [shards(): lax.all_to_all(parts, 'tok', split_axis=0, concat_axis=0, tiled=True)]
where the time goes in v6:
time: 191 us; the launch traced here: 188 us
  blocking collectives  107 us (56%)
  waiting for transfers between devices  42.1 us (22%)
  Pallas kernels  19 us (10%)
  between operations  14.1 us (7%)
  starting transfers between devices  5.77 us (3%)
    all_to_all x1, blocking collectives, shards(): lax.all_to_all(send_rows.reshape(groups, capacity, width + LANES), 'feat'...  90.3 us
    all_gather x1, waiting for transfers between devices, shards(): every = lax.all_gather(inputs, 'feat', axis=0, tiled=True)  28.4 us
    pallas_call x6, Pallas kernels, call(): pl.pallas_call(body, out_shape=outs, in_specs=list(specs) + [pl.BlockSpec...  19 us
    all_to_all x1, blocking collectives, shards(): lax.all_to_all(parts, 'tok', split_axis=0, concat_axis=0, tiled=True)  16.9 us
    all_to_all x1, waiting for transfers between devices, shards(): lax.all_to_all(back.reshape(groups, capacity, width), 'feat', split_axis=...  12.9 us
    all_to_all x1, starting transfers between devices, shards(): lax.all_to_all(back.reshape(groups, capacity, width), 'feat', split_axis=...  5.73 us
  transfers between devices with their start and end apart: 2, of which 2 were waited for; matrix products, arithmetic and copies ran while one was open for 0% of the time, Pallas kernels for 9%

profile of v6, /device:TPU:1, one launch (start us, length us, event | category | flops | bytes accessed | tf_op | source)
XLA Modules:
  0.0 188.4 jit_solution(14460240941444679438)
XLA Ops:
  7.2 0.0 all-gather.2.cloned.1.call-start
  7.2 0.7 all-gather.2.cloned.1.call-update
  7.9 2.7 %shard_map.94 = bf16[512,1152]{1,0:T(8,128)(2,1)} custom-call(s32[2,128]{1,0:T(2,128)} %bitcast.11, s32[2,32,128]{2,1,0:T(8,128)} %bitcast.14, f32[2,32,128]{2,1,0:T(8,128)} %bitcast.15, bf16[128,1024]{1,0:T(8,128)(2,1)} %refs_3_.1), custom_call_target="tpu_custom_call" | custom-call | flops 134217728 | bytes 1310720 | tf_op jit(solution)/shard_map/pallas_call | solution.py:28
  10.6 0.0 copy-start
  10.6 90.3 %all_to_all.15 = bf16[32,16,1152]{2,1,0:T(8,128)(2,1)S(1)} all-to-all(bf16[32,16,1152]{2,1,0:T(8,128)(2,1)} %bitcast.13), channel_id=1, replica_groups=mesh['feat'=32,'tok'=16] {'feat'}, dimensions={0} | all-to-all | bytes 2359296 | tf_op jit(solution)/shard_map/all_to_all | solution.py:202
  100.9 0.0 copy-done
  100.9 0.9 shard_map.95
  101.8 0.0 copy-start.2
  101.8 0.1 broadcast_in_dim.3
  101.9 16.9 %all_to_all.16 = f16[16,128,128]{2,1,0:T(8,128)(2,1)S(1)} all-to-all(f16[16,128,128]{2,1,0:T(8,128)(2,1)S(1)} %broadcast_in_dim.3), channel_id=1, replica_groups=mesh['feat'=32,'tok'=16] {'tok'}, dimensions={0} | all-to-all | bytes 1048576 | tf_op jit(solution)/shard_map/all_to_all | solution.py:214
  118.8 0.1 convert_reduce_fusion
  118.9 0.0 copy-done.2
  118.9 2.7 %shard_map.96 = (bf16[256,512]{1,0:T(8,128)(2,1)S(1)}, bf16[512,1024]{1,0:T(8,128)(2,1)}) custom-call(f32[128,128]{1,0:T(8,128)S(1)} %broadcast_multiply_fusion.refs_0_, f32[128,128]{1,0:T(8,128)S(1)} %get-tuple-element.11.refs_1_.refs_0_, bf16[256,1024]{1,0:T(8,128)(2,1)S(1)} %copy-done.2), custom_call_target="tpu_custom_call" | custom-call | flops 268435456 | bytes 1048576 | tf_op jit(solution)/shard_map/pallas_call | solution.py:28
  121.6 5.7 %all-to-all-start.2 = ((bf16[32,16,1024]{2,1,0:T(8,128)(2,1)}), bf16[32,16,1024]{2,1,0:T(8,128)(2,1)S(1)}, u32[]{:S(2)}, u32[]{:S(2)}) async-start(bf16[32,16,1024]{2,1,0:T(8,128)(2,1)} %bitcast.5), calls=%async_computation.2 | async-start | bytes 2097152 | tf_op jit(solution)/shard_map/all_to_all | solution.py:223
  127.3 2.2 %shard_map.98 = bf16[256,1024]{1,0:T(8,128)(2,1)} custom-call(f32[128,128]{1,0:T(8,128)S(1)} %get-tuple-element.11.refs_1_.refs_0_, f32[128,128]{1,0:T(8,128)S(1)} %get-tuple-element.14.refs_1_, bf16[512,1152]{1,0:T(8,128)(2,1)S(1)} %bitcast.8), custom_call_target="tpu_custom_call" | custom-call | flops 268435456 | bytes 2097152 | tf_op jit(solution)/shard_map/pallas_call | solution.py:28
  129.6 28.4 %all-gather.2.cloned.1.call-done.refs_2_ = bf16[4096,1024]{1,0:T(8,128)(2,1)} async-done(((bf16[128,1024]{1,0:T(8,128)(2,1)}), bf16[4096,1024]{1,0:T(8,128)(2,1)}) %all-gather.2.cloned.1.call-update) | async-done | bytes 8388624 | tf_op jit(solution)/shard_map/all_gather | solution.py:183
  158.0 0.0 copy-start.1
  158.0 9.4 %shard_map.97 = (bf16[256,1024]{1,0:T(8,128)(2,1)}, f32[8,128]{1,0:T(8,128)S(1)}) custom-call(bf16[256,512]{1,0:T(8,128)(2,1)S(1)} %get-tuple-element.12.refs_0_, bf16[512,1152]{1,0:T(8,128)(2,1)S(1)} %bitcast.9, bf16[4096,1024]{1,0:T(8,128)(2,1)} %all-gather.2.cloned.1.call-done.refs_2_), custom_call_target="tpu_custom_call" | custom-call | flops 2147483648 | bytes 8388608 | tf_op jit(solution)/shard_map/pallas_call | solution.py:28
  167.4 12.9 %all-to-all-done.2 = bf16[32,16,1024]{2,1,0:T(8,128)(2,1)S(1)} async-done(((bf16[32,16,1024]{2,1,0:T(8,128)(2,1)}), bf16[32,16,1024]{2,1,0:T(8,128)(2,1)S(1)}, u32[]{:S(2)}, u32[]{:S(2)}) %all-to-all-start.2) | async-done | bytes 1048608 | tf_op jit(solution)/shard_map/all_to_all | solution.py:223
  180.3 0.0 copy-done.1
  180.3 1.2 shard_map.99
  (2 shorter events, 0.0 us)
Async XLA Ops:
  7.2 150.9 %all-gather.2.cloned.1.call-start = ((), (), s32[]{:S(2)}) async-start(), calls=%async_computation.3 | async-start | bytes 8650752 | tf_op jit(solution)/shard_map/all_gather | solution.py:183
  10.6 90.3 %copy-start = (bf16[256,1024]{1,0:T(8,128)(2,1)S(1)}, bf16[256,1024]{1,0:T(8,128)(2,1)}, u32[]{:S(2)}) copy-start(bf16[256,1024]{1,0:T(8,128)(2,1)} %refs_1_.1) | copy-start | bytes 1572868
  101.8 17.1 %copy-start.2 = (bf16[256,1024]{1,0:T(8,128)(2,1)S(1)}, bf16[256,1024]{1,0:T(8,128)(2,1)}, u32[]{:S(2)}) copy-start(bf16[256,1024]{1,0:T(8,128)(2,1)} %refs_2_.1) | copy-start | bytes 1572868
  121.6 58.7 %all-to-all-start.2 = ((bf16[32,16,1024]{2,1,0:T(8,128)(2,1)}), bf16[32,16,1024]{2,1,0:T(8,128)(2,1)S(1)}, u32[]{:S(2)}, u32[]{:S(2)}) async-start(bf16[32,16,1024]{2,1,0:T(8,128)(2,1)} %bitcast.5), calls=%async_computation.2 | async-start | bytes 2097152 | tf_op jit(solution)/shard_map/all_to_all | solution.py:223
  158.0 22.3 %copy-start.1 = (s32[128,2]{0,1:T(2,128)S(1)}, s32[128,2]{0,1:T(2,128)}, u32[]{:S(2)}) copy-start(s32[128,2]{0,1:T(2,128)} %param.11) | copy-start | bytes 3076
Sparse Core Ops, SparseCore 0:
  10.1 147.8 all-gather.1

commit v7 on v6

--- a/solution.py
+++ b/solution.py
@@ -12,6 +12,7 @@
 LANES = 128
 DEVICES_A_STEP = 4
 PARTS = 4
+EARLY = 4
 SCALE = 128.0
 VMEM_BYTES = 48 * 1024 * 1024
 ROWS_ROWS = (((1,), (1,)), ((), ()))
@@ -55,12 +56,14 @@
     return out
 
 
-def pack_kernel(groups, capacity, dest_hbm, ids_hbm, codes_hbm, grads_hbm, row_hbm, *scratch):
+def pack_kernel(groups, capacity, dest_hbm, ids_hbm, codes_hbm, grads_hbm, inputs_hbm, row_hbm, early_hbm, *scratch):
     dest_ref, ids_ref, codes_ref, grads_ref, row_ref, sems = scratch
     pairs = ((dest_hbm, dest_ref), (ids_hbm, ids_ref), (codes_hbm, codes_ref), (grads_hbm, grads_ref))
     copies = [pltpu.make_async_copy(a, b, sems.at[i]) for i, (a, b) in enumerate(pairs)]
     for copy in copies:
         copy.start()
+    sends = [pltpu.make_async_copy(inputs_hbm.at[: early_hbm.shape[0]], early_hbm, sems.at[len(copies)])]
+    sends[0].start()
     slot_count = row_ref.shape[0]
     tokens, width = grads_ref.shape
     copies[0].wait()
@@ -77,11 +80,10 @@
     row_ref[:, width:] = notes.astype(BF16)
     copies[3].wait()
     height = slot_count // PARTS
-    sends = []
     for part in range(PARTS):
         lines = slice(part * height, (part + 1) * height)
         row_ref[lines, :width] = jnp.dot(pick[lines], grads_ref[...], preferred_element_type=F32).astype(BF16)
-        sends.append(pltpu.make_async_copy(row_ref.at[lines], row_hbm.at[lines], sems.at[len(copies) + part]))
+        sends.append(pltpu.make_async_copy(row_ref.at[lines], row_hbm.at[lines], sems.at[len(copies) + 1 + part]))
         sends[-1].start()
     for send in sends:
         send.wait()
@@ -98,7 +100,8 @@
     return out
 
 
-def score_kernel(per, row_ref, dec_ref, score_ref, ids_ref, codes_ref):
+def score_kernel(per, row_ref, dec_ref, input_ref, score_ref, ids_ref, codes_ref, late_ref):
+    late_ref[...] = input_ref[input_ref.shape[0] - late_ref.shape[0] :, :]
     width = dec_ref.shape[1]
     scores = lax.dot_general(row_ref[:, :width], dec_ref[...], ROWS_ROWS, preferred_element_type=F32)
     notes = row_ref[:, width:].astype(F32)
@@ -138,7 +141,7 @@
     out_ref[...] = jnp.dot(code, row_ref[:, :width], preferred_element_type=F32).astype(BF16)
 
 
-def enc_kernel(per, capacity, tokens, pre_ref, note_ref, input_ref, out_ref, mark_ref, turned_ref, total_ref):
+def enc_kernel(per, capacity, tokens, pre_ref, note_ref, early_ref, late_ref, out_ref, mark_ref, turned_ref, total_ref):
     step = pl.program_id(0)
 
     @pl.when(step == 0)
@@ -150,12 +153,15 @@
     slots = note_ref.shape[0]
     number = note_ref[:, 2 * per : 2 * per + 1].astype(F32).astype(jnp.int32)
     device = lax.broadcasted_iota(jnp.int32, (slots, 1), 0) // capacity
-    place = jnp.where(number > 0, device * tokens + number - 1, -1)
-    line = lax.broadcasted_iota(jnp.int32, (slots, input_ref.shape[0]), 1)
-    hot = (line == place).astype(F32).astype(BF16)
     here = turned_ref[pl.ds(pl.multiple_of(step * slots, slots), slots), :]
-    wide = lax.dot_general(here, hot, DEPTH_FIRST, preferred_element_type=F32).astype(BF16)
-    total_ref[...] += jnp.dot(wide, input_ref[...], preferred_element_type=F32)
+    first = early_ref.shape[0] * capacity // slots
+    for ref, start, count in ((early_ref, 0, first), (late_ref, first, tokens - first)):
+        token = number - 1 - start
+        place = jnp.where((token >= 0) & (token < count), device * count + token, -1)
+        line = lax.broadcasted_iota(jnp.int32, (slots, ref.shape[0]), 1)
+        hot = (line == place).astype(F32).astype(BF16)
+        wide = lax.dot_general(here, hot, DEPTH_FIRST, preferred_element_type=F32).astype(BF16)
+        total_ref[...] += jnp.dot(wide, ref[...], preferred_element_type=F32)
 
     @pl.when(step == pl.num_programs(0) - 1)
     def _():
@@ -180,36 +186,43 @@
     shape = jax.ShapeDtypeStruct
     mac = 2 * slots * width
 
-    every = lax.all_gather(inputs, "feat", axis=0, tiled=True)
-    send_rows = call(
+    early_count = tokens * EARLY // 8
+    send_rows, early = call(
         functools.partial(pack_kernel, groups, capacity),
-        shape((slots, width + LANES), BF16),
+        (shape((slots, width + LANES), BF16), shape((early_count, width), BF16)),
         mac * tokens,
         2 * slots * width + 2 * tokens * width,
-        (dest, jnp.transpose(local_ids, (1, 2, 0)), jnp.transpose(code_values, (1, 2, 0)), out_grad),
+        (dest, jnp.transpose(local_ids, (1, 2, 0)), jnp.transpose(code_values, (1, 2, 0)), out_grad, inputs),
         limit=None,
-        in_specs=[pl.BlockSpec(memory_space=pl.ANY)] * 4,
-        out_specs=pl.BlockSpec(memory_space=pl.ANY),
+        in_specs=[pl.BlockSpec(memory_space=pl.ANY)] * 5,
+        out_specs=(pl.BlockSpec(memory_space=pl.ANY), pl.BlockSpec(memory_space=pl.ANY)),
         scratch_shapes=[
             pltpu.VMEM((hops, tokens), jnp.int32),
             pltpu.VMEM((hops, per, tokens), jnp.int32),
             pltpu.VMEM((hops, per, tokens), F32),
             pltpu.VMEM((tokens, width), BF16),
             pltpu.VMEM((slots, width + LANES), BF16),
-            pltpu.SemaphoreType.DMA((4 + PARTS,)),
+            pltpu.SemaphoreType.DMA((5 + PARTS,)),
         ],
     )
+    early = lax.all_gather(early, "feat", axis=0, tiled=True)
     rows = lax.all_to_all(
         send_rows.reshape(groups, capacity, width + LANES), "feat", split_axis=0, concat_axis=0, tiled=True
     ).reshape(slots, width + LANES)
     held = slots * per // LANES
-    score, ids, codes = call(
+    score, ids, codes, late = call(
         functools.partial(score_kernel, per),
-        (shape((held, LANES), F32), shape((LANES, held), F32), shape((LANES, held), F32)),
+        (
+            shape((held, LANES), F32),
+            shape((LANES, held), F32),
+            shape((LANES, held), F32),
+            shape((tokens - early_count, width), BF16),
+        ),
         mac * features,
         2 * slots * width,
-        (rows, dec_rows),
-    )
+        (rows, dec_rows, inputs),
+    )
+    late = lax.all_gather(late, "feat", axis=0, tiled=True)
     parts = jnp.broadcast_to((score * SCALE).astype(jnp.float16), (slices, held, LANES))
     parts = lax.all_to_all(parts, "tok", split_axis=0, concat_axis=0, tiled=True)
     score = jnp.sum(parts.astype(F32), axis=0) * (1.0 / SCALE)
@@ -236,12 +249,13 @@
         (shape((features, width), BF16), shape((8, LANES), F32)),
         2 * groups * tokens * features * width,
         2 * groups * tokens * width,
-        (pre, rows, every),
+        (pre, rows, early, late),
         grid=(steps,),
         in_specs=[
             pl.BlockSpec((features, slots), lambda i: (0, 0)),
             pl.BlockSpec((slots // steps, LANES), lambda i: (i, width // LANES)),
-            pl.BlockSpec((groups * tokens // steps, width), lambda i: (i, 0)),
+            pl.BlockSpec((groups * early_count // steps, width), lambda i: (i, 0)),
+            pl.BlockSpec((groups * (tokens - early_count) // steps, width), lambda i: (i, 0)),
         ],
         out_specs=(
             pl.BlockSpec((features, width), lambda i: (0, 0)),

time: 191 us -> 241 us (1.26)
  waiting for transfers between devices: 42.1 us -> 87.9 us
  local copies, waits for them, and re-layouts: 0.11 us -> 4.29 us
  Pallas kernels: 19 us -> 21.9 us
    all_gather x1 -> x2, waiting for transfers between devices: 28.4 us -> 87.8 us  [the longest x1 87.8 us: shards(): late = lax.all_gather(late, 'feat', axis=0, tiled=True)]
    all_to_all x1, waiting for transfers between devices: 12.9 us -> 0.01 us  [shards(): lax.all_to_all(back.reshape(groups, capacity, width), 'feat', split_axis=...]
    unnamed x6 -> x10, local copies, waits for them, and re-layouts: 0.02 us -> 4.2 us
    pallas_call x6, Pallas kernels: 19 us -> 21.9 us  [call(): pl.pallas_call(body, out_shape=outs, in_specs=list(specs) + [pl.BlockSpec...]
  transfers between devices with their start and end apart: 2 -> 3, of which waited for: 2 -> 1; matrix products, arithmetic and copies ran while one was open for 0% -> 0% of each run, Pallas kernels for 9% -> 6%
where the time goes in v7:
time: 241 us; the launch traced here: 240 us
  blocking collectives  106 us (44%)
  waiting for transfers between devices  87.9 us (36%)
  Pallas kernels  21.9 us (9%)
  between operations  14.1 us (6%)
  starting transfers between devices  5.7 us (2%)
  local copies, waits for them, and re-layouts  4.29 us (2%)
    all_to_all x1, blocking collectives, shards(): lax.all_to_all(send_rows.reshape(groups, capacity, width + LANES), 'feat'...  89.1 us
    all_gather x1, waiting for transfers between devices, shards(): late = lax.all_gather(late, 'feat', axis=0, tiled=True)  87.8 us
    pallas_call x6, Pallas kernels, call(): pl.pallas_call(body, out_shape=outs, in_specs=list(specs) + [pl.BlockSpec...  21.9 us
    all_to_all x1, blocking collectives, shards(): lax.all_to_all(parts, 'tok', split_axis=0, concat_axis=0, tiled=True)  17 us
    all_to_all x1, starting transfers between devices, shards(): lax.all_to_all(back.reshape(groups, capacity, width), 'feat', split_axis=...  5.62 us
  transfers between devices with their start and end apart: 3, of which 1 were waited for; matrix products, arithmetic and copies ran while one was open for 0% of the time, Pallas kernels for 6%

profile of v7, /device:TPU:1, one launch (start us, length us, event | category | flops | bytes accessed | tf_op | source)
XLA Modules:
  0.0 240.1 jit_solution(14141612637560011668)
XLA Ops:
  7.2 0.0 copy-start.4
  7.2 0.0 all-gather.3.cloned.1.call-start
  7.2 5.2 %shard_map.94 = (bf16[512,1152]{1,0:T(8,128)(2,1)}, bf16[64,1024]{1,0:T(8,128)(2,1)}) custom-call(s32[2,128]{1,0:T(2,128)} %bitcast.11, s32[2,32,128]{2,1,0:T(8,128)} %bitcast.14, f32[2,32,128]{2,1,0:T(8,128)} %bitcast.15, bf16[128,1024]{1,0:T(8,128)(2,1)} %refs_3_.1, bf16[128,1024]{1,0:T(8,128)(2,1)} %refs_2_.2), custom_call_target="tpu_custom_call" | custom-call | flops 134217728 | bytes 1310720 | tf_op jit(solution)/shard_map/pallas_call | solution.py:29
  12.4 0.0 all-gather.3.cloned.1.call-update
  12.4 0.0 all-gather.5.cloned.1.call-start
  12.5 89.1 %all_to_all.15 = bf16[32,16,1152]{2,1,0:T(8,128)(2,1)S(1)} all-to-all(bf16[32,16,1152]{2,1,0:T(8,128)(2,1)} %bitcast.13), channel_id=1, replica_groups=mesh['feat'=32,'tok'=16] {'feat'}, dimensions={0} | all-to-all | bytes 2359296 | tf_op jit(solution)/shard_map/all_to_all | solution.py:209
  101.6 0.0 copy-start.1
  101.6 1.0 copy-done.1
  102.6 0.0 copy-start.2
  102.6 1.0 copy-done.2
  103.6 1.5 shard_map.95
  105.1 0.0 all-gather.5.cloned.1.call-update
  105.1 0.1 broadcast_in_dim.3
  105.2 17.0 %all_to_all.16 = f16[16,128,128]{2,1,0:T(8,128)(2,1)S(1)} all-to-all(f16[16,128,128]{2,1,0:T(8,128)(2,1)S(1)} %broadcast_in_dim.3), channel_id=1, replica_groups=mesh['feat'=32,'tok'=16] {'tok'}, dimensions={0} | all-to-all | bytes 1048576 | tf_op jit(solution)/shard_map/all_to_all | solution.py:227
  122.2 0.1 convert_reduce_fusion
  122.3 0.0 copy-done.4
  122.3 2.7 %shard_map.96 = (bf16[256,512]{1,0:T(8,128)(2,1)S(1)}, bf16[512,1024]{1,0:T(8,128)(2,1)}) custom-call(f32[128,128]{1,0:T(8,128)S(1)} %broadcast_multiply_fusion.refs_0_, f32[128,128]{1,0:T(8,128)S(1)} %get-tuple-element.15.refs_1_.refs_0_, bf16[256,1024]{1,0:T(8,128)(2,1)S(1)} %copy-done.4), custom_call_target="tpu_custom_call" | custom-call | flops 268435456 | bytes 1048576 | tf_op jit(solution)/shard_map/pallas_call | solution.py:29
  125.0 5.6 %all-to-all-start.2 = ((bf16[32,16,1024]{2,1,0:T(8,128)(2,1)}), bf16[32,16,1024]{2,1,0:T(8,128)(2,1)S(1)}, u32[]{:S(2)}, u32[]{:S(2)}) async-start(bf16[32,16,1024]{2,1,0:T(8,128)(2,1)} %bitcast.5), calls=%async_computation.2 | async-start | bytes 2097152 | tf_op jit(solution)/shard_map/all_to_all | solution.py:236
  130.6 2.2 shard_map.98
  132.9 0.0 all-gather.3.cloned.1.call-done.refs_2_
  132.9 87.8 %all-gather.5.cloned.1.call-done.refs_3_ = bf16[2048,1024]{1,0:T(8,128)(2,1)} async-done(((bf16[64,1024]{1,0:T(8,128)(2,1)}), bf16[2048,1024]{1,0:T(8,128)(2,1)}) %all-gather.5.cloned.1.call-update) | async-done | bytes 4194320 | tf_op jit(solution)/shard_map/all_gather | solution.py:225
  220.7 0.0 copy-start
  220.7 2.2 copy-done
  222.9 0.0 copy-start.3
  222.9 9.1 %shard_map.97 = (bf16[256,1024]{1,0:T(8,128)(2,1)}, f32[8,128]{1,0:T(8,128)S(1)}) custom-call(bf16[256,512]{1,0:T(8,128)(2,1)S(1)} %get-tuple-element.16.refs_0_, bf16[512,1152]{1,0:T(8,128)(2,1)S(1)} %bitcast.9, bf16[2048,1024]{1,0:T(8,128)(2,1)S(1)} %copy-done, bf16[2048,1024]{1,0:T(8,128)(2,1)} %all-gather.5.cloned.1.call-done.refs_3_), custom_call_target="tpu_custom_call" | custom-call | flops 2147483648 | bytes 8388608 | tf_op jit(solution)/shard_map/pallas_call | solution.py:29
  232.0 0.0 all-to-all-done.2
  232.0 0.0 copy-done.3
  232.0 1.2 shard_map.99
  (2 shorter events, 0.0 us)
Async XLA Ops:
  7.2 115.1 %copy-start.4 = (bf16[256,1024]{1,0:T(8,128)(2,1)S(1)}, bf16[256,1024]{1,0:T(8,128)(2,1)}, u32[]{:S(2)}) copy-start(bf16[256,1024]{1,0:T(8,128)(2,1)} %refs_2_.3) | copy-start | bytes 1572868
  7.2 125.7 %all-gather.3.cloned.1.call-start = ((), (), s32[]{:S(2)}) async-start(), calls=%async_computation.3 | async-start | bytes 4325376 | tf_op jit(solution)/shard_map/all_gather | solution.py:208
  12.4 208.3 %all-gather.5.cloned.1.call-start = ((), (), s32[]{:S(2)}) async-start(), calls=%async_computation.4 | async-start | bytes 4325376 | tf_op jit(solution)/shard_map/all_gather | solution.py:225
  101.6 1.0 copy-start.1
  102.6 1.0 copy-start.2
  125.0 107.0 %all-to-all-start.2 = ((bf16[32,16,1024]{2,1,0:T(8,128)(2,1)}), bf16[32,16,1024]{2,1,0:T(8,128)(2,1)S(1)}, u32[]{:S(2)}, u32[]{:S(2)}) async-start(bf16[32,16,1024]{2,1,0:T(8,128)(2,1)} %bitcast.5), calls=%async_computation.2 | async-start | bytes 2097152 | tf_op jit(solution)/shard_map/all_to_all | solution.py:236
  220.7 2.2 copy-start
  222.9 9.2 %copy-start.3 = (s32[128,2]{0,1:T(2,128)S(1)}, s32[128,2]{0,1:T(2,128)}, u32[]{:S(2)}) copy-start(s32[128,2]{0,1:T(2,128)} %param.11) | copy-start | bytes 3076
Sparse Core Ops, SparseCore 0:
  12.5 110.4 all-gather.2
  125.7 94.9 all-gather.4

commit v8 on v6

v8 whole, which is shorter than its diff:
```python
import functools

import jax
import jax.numpy as jnp
from jax import lax
from jax.experimental import pallas as pl
from jax.experimental.pallas import tpu as pltpu
from jax.sharding import PartitionSpec as P

F32 = jnp.float32
BF16 = jnp.bfloat16
LANES = 128
DEVICES_A_STEP = 8
PARTS = 4
SCALE = 128.0
VMEM_BYTES = 48 * 1024 * 1024
ROWS_ROWS = (((1,), (1,)), ((), ()))
DEPTH_FIRST = (((0,), (0,)), ((), ()))


def call(kernel, outs, flops, moved, operands, after=(), limit=VMEM_BYTES, **how):
    count = len(operands)

    def body(*refs):
        kernel(*refs[:count], *refs[count + len(after) :])

    specs = how.pop("in_specs", [pl.BlockSpec(memory_space=pltpu.VMEM)] * count)
    return pl.pallas_call(
        body,
        out_shape=outs,
        in_specs=list(specs) + [pl.BlockSpec(memory_space=pl.ANY)] * len(after),
        compiler_params=pltpu.CompilerParams(vmem_limit_bytes=limit),
        cost_estimate=pl.CostEstimate(flops=flops, bytes_accessed=moved, transcendentals=0),
        **how,
    )(*operands, *after)


def places(dest_ref, groups):
    tokens = dest_ref.shape[1]
    group_line = lax.broadcasted_iota(jnp.int32, (groups, tokens), 0)
    earlier = (
        lax.broadcasted_iota(jnp.int32, (tokens, tokens), 0)
        < lax.broadcasted_iota(jnp.int32, (tokens, tokens), 1)
    ).astype(F32).astype(BF16)
    taken = jnp.zeros((groups, 1), F32)
    out = []
    for hop in range(dest_ref.shape[0]):
        match = (group_line == dest_ref[hop : hop + 1, :]).astype(F32)
        before = jnp.dot(match.astype(BF16), earlier, preferred_element_type=F32) + taken
        out.append(jnp.sum(before * match, axis=0, keepdims=True).astype(jnp.int32))
        taken = taken + jnp.sum(match, axis=1, keepdims=True)
    return out


def one_hot(numbers, count):
    line = lax.broadcasted_iota(jnp.int32, (count, numbers.shape[1]), 0)
    return (line == numbers).astype(F32).astype(BF16)


def pick_matrices(dest_ref, groups, capacity):
    return [
        one_hot(dest_ref[hop : hop + 1, :] * capacity + place, groups * capacity)
        for hop, place in enumerate(places(dest_ref, groups))
    ]


def pack_kernel(groups, capacity, dest_hbm, ids_hbm, codes_hbm, grads_hbm, inputs_hbm, message_hbm, wide_hbm, *scratch):
    dest_ref, ids_ref, codes_ref, grads_ref, message_ref, wide_ref, sems = scratch
    tokens, width = grads_ref.shape
    pairs = (
        (dest_hbm, dest_ref),
        (ids_hbm, ids_ref),
        (codes_hbm, codes_ref),
        (grads_hbm, grads_ref),
    )
    blocks = width // LANES
    pairs += tuple(
        (inputs_hbm.at[:, block * LANES : (block + 1) * LANES], wide_ref.at[block * tokens : (block + 1) * tokens, :])
        for block in range(blocks)
    )
    copies = [pltpu.make_async_copy(a, b, sems.at[i]) for i, (a, b) in enumerate(pairs)]
    for copy in copies:
        copy.start()
    per = ids_ref.shape[1]
    copies[0].wait()
    ranks = places(dest_ref, groups)
    picks = [
        one_hot(dest_ref[hop : hop + 1, :] * capacity + rank, groups * capacity) for hop, rank in enumerate(ranks)
    ]
    pick = functools.reduce(jnp.add, picks)
    info = [line.astype(F32) for hop, rank in enumerate(ranks) for line in (dest_ref[hop : hop + 1, :], rank)]
    info.append(jnp.zeros((wide_ref.shape[0] - blocks * tokens - len(info), tokens), F32))
    wide_ref[blocks * tokens :, :] = jnp.concatenate(info, axis=0).astype(BF16)
    for copy in copies[4:]:
        copy.wait()
    sends = [pltpu.make_async_copy(wide_ref, wide_hbm, sems.at[len(copies)])]
    sends[0].start()
    notes = jnp.zeros((groups * capacity, LANES), F32)
    rest = jnp.zeros((LANES - 2 * per, tokens), F32)
    copies[1].wait()
    copies[2].wait()
    for hop, hop_pick in enumerate(picks):
        lines = jnp.concatenate([ids_ref[hop].astype(F32), codes_ref[hop], rest], axis=0).astype(BF16)
        notes = notes + lax.dot_general(hop_pick, lines, ROWS_ROWS, preferred_element_type=F32)
    half = capacity // 2
    notes = notes.reshape(groups, capacity, LANES)
    low = notes[:, :half, :].reshape(groups * half, LANES)
    high = pltpu.roll(notes[:, half:, :].reshape(groups * half, LANES), 2 * per, 1)
    message_ref[:, blocks * capacity :, :] = (low + high).astype(BF16).reshape(groups, half, LANES)
    copies[3].wait()
    some = groups // PARTS
    for part in range(PARTS):
        lines = slice(part * some * capacity, (part + 1) * some * capacity)
        here = slice(part * some, (part + 1) * some)
        rows = jnp.dot(pick[lines], grads_ref[...], preferred_element_type=F32).astype(BF16)
        for block in range(blocks):
            column = rows[:, block * LANES : (block + 1) * LANES]
            message_ref[here, block * capacity : (block + 1) * capacity, :] = column.reshape(some, capacity, LANES)
        sends.append(
            pltpu.make_async_copy(message_ref.at[here], message_hbm.at[here], sems.at[len(copies) + 1 + part])
        )
        sends[-1].start()
    for send in sends:
        send.wait()


def unpack(message_ref, capacity, line_ref):
    slots = line_ref.shape[0]
    for block in range(line_ref.shape[1] // LANES):
        column = message_ref[:, block * capacity : (block + 1) * capacity, :]
        line_ref[:, block * LANES : (block + 1) * LANES] = column.reshape(slots, LANES)


def fold(values, per):
    parts = LANES // per
    height = values.shape[0] // parts
    lane = lax.broadcasted_iota(jnp.int32, (height, LANES), 1)
    out = values[:height]
    for q in range(1, parts):
        turned = pltpu.roll(values[q * height : (q + 1) * height], q * per, 1)
        out = jnp.where(lane >= q * per, turned, out)
    return out


def score_kernel(per, capacity, message_ref, dec_ref, score_ref, ids_ref, codes_ref, line_ref):
    unpack(message_ref, capacity, line_ref)
    scores = lax.dot_general(line_ref[...], dec_ref[...], ROWS_ROWS, preferred_element_type=F32)
    groups, half = message_ref.shape[0], capacity // 2
    notes = message_ref[:, message_ref.shape[1] - half :, :].astype(F32)
    turned = pltpu.roll(notes.reshape(groups * half, LANES), LANES - 2 * per, 1).reshape(groups, half, LANES)
    notes = jnp.concatenate([notes, turned], axis=1).reshape(groups * capacity, LANES)
    ids = notes.astype(jnp.int32)
    low = ids & (LANES - 1)
    chosen = jnp.take_along_axis(scores[:, :LANES], low, axis=1)
    for part in range(1, dec_ref.shape[0] // LANES):
        here = jnp.take_along_axis(scores[:, part * LANES : (part + 1) * LANES], low, axis=1)
        chosen = jnp.where(ids >= part * LANES, here, chosen)
    score_ref[...] = fold(chosen, per)
    ids_ref[...] = fold(notes, per).T
    codes_ref[...] = fold(pltpu.roll(notes, LANES - per, 1), per).T


def spread(ids, values, features, per):
    held = ids.shape[1]
    feature_line = lax.broadcasted_iota(jnp.int32, (features, held), 0).astype(F32)
    blocks = []
    for q in range(LANES // per):
        block = jnp.zeros((features, held), F32)
        for j in range(q * per, (q + 1) * per):
            block = jnp.where(feature_line == ids[j : j + 1, :], values[j : j + 1, :], block)
        blocks.append(block)
    return jnp.concatenate(blocks, axis=1).astype(BF16)


def back_kernel(per, score_ref, ids_ref, enc_ref, pre_ref, back_ref):
    rounded = score_ref[...].astype(BF16).astype(F32).T
    pre = spread(ids_ref[...], rounded, enc_ref.shape[0], per)
    pre_ref[...] = pre
    back_ref[...] = lax.dot_general(pre, enc_ref[...], DEPTH_FIRST, preferred_element_type=F32).astype(BF16)


def dec_kernel(per, capacity, ids_ref, codes_ref, message_ref, out_ref, line_ref):
    unpack(message_ref, capacity, line_ref)
    code = spread(ids_ref[...], codes_ref[...], out_ref.shape[0], per)
    out_ref[...] = jnp.dot(code, line_ref[...], preferred_element_type=F32).astype(BF16)


def enc_kernel(capacity, tokens, pre_ref, wide_ref, out_ref, mark_ref, turned_ref, total_ref, line_ref):
    step = pl.program_id(0)

    @pl.when(step == 0)
    def _():
        turned_ref[...] = pre_ref[...].T
        total_ref[...] = jnp.zeros_like(total_ref)
        mark_ref[...] = jnp.zeros_like(mark_ref)

    devices, width = wide_ref.shape[0], total_ref.shape[1]
    blocks = width // LANES
    me = lax.axis_index("feat")
    slots = []
    for device in range(devices):
        for block in range(blocks):
            line_ref[device * tokens : (device + 1) * tokens, block * LANES : (block + 1) * LANES] = wide_ref[
                device, block * tokens : (block + 1) * tokens, :
            ]
        info = wide_ref[device, blocks * tokens :, :].astype(F32).astype(jnp.int32)
        slot = jnp.where(info[2:3] == me, info[3:4] + device * capacity, -1)
        slots.append(jnp.where(info[0:1] == me, info[1:2] + device * capacity, slot))
    count = devices * capacity
    hot = one_hot(jnp.concatenate(slots, axis=1), count)
    here = turned_ref[pl.ds(pl.multiple_of(step * count, count), count), :]
    spread_out = lax.dot_general(here, hot, DEPTH_FIRST, preferred_element_type=F32).astype(BF16)
    total_ref[...] += jnp.dot(spread_out, line_ref[...], preferred_element_type=F32)

    @pl.when(step == pl.num_programs(0) - 1)
    def _():
        out_ref[...] = total_ref[...].astype(BF16)


def merge_kernel(groups, capacity, dest_ref, back_ref, out_ref):
    picks = pick_matrices(dest_ref, groups, capacity)
    pick = functools.reduce(jnp.add, picks)
    out_ref[...] = lax.dot_general(pick, back_ref[...], DEPTH_FIRST, preferred_element_type=F32).astype(BF16)


def shards(enc_rows, dec_rows, inputs, out_grad, destinations, local_ids, code_values):
    groups = lax.axis_size("feat")
    slices = lax.axis_size("tok")
    tokens, hops = destinations.shape
    per = local_ids.shape[2]
    features, width = dec_rows.shape
    capacity = max(2, 2 * tokens * hops // groups)
    slots = groups * capacity
    dest = destinations.T
    shape = jax.ShapeDtypeStruct
    mac = 2 * slots * width

    lines = capacity * width // LANES + capacity * 2 * per // LANES
    wide_lines = tokens * width // LANES + 16
    message, wide = call(
        functools.partial(pack_kernel, groups, capacity),
        (shape((groups, lines, LANES), BF16), shape((wide_lines, LANES), BF16)),
        mac * tokens,
        2 * slots * width + 4 * tokens * width,
        (dest, jnp.transpose(local_ids, (1, 2, 0)), jnp.transpose(code_values, (1, 2, 0)), out_grad, inputs),
        limit=None,
        in_specs=[pl.BlockSpec(memory_space=pl.ANY)] * 5,
        out_specs=(pl.BlockSpec(memory_space=pl.ANY), pl.BlockSpec(memory_space=pl.ANY)),
        scratch_shapes=[
            pltpu.VMEM((hops, tokens), jnp.int32),
            pltpu.VMEM((hops, per, tokens), jnp.int32),
            pltpu.VMEM((hops, per, tokens), F32),
            pltpu.VMEM((tokens, width), BF16),
            pltpu.VMEM((groups, lines, LANES), BF16),
            pltpu.VMEM((wide_lines, LANES), BF16),
            pltpu.SemaphoreType.DMA((5 + width // LANES + PARTS,)),
        ],
    )
    wide = lax.all_gather(wide, "feat", axis=0)
    message = lax.all_to_all(message, "feat", split_axis=0, concat_axis=0, tiled=True)
    held = slots * per // LANES
    score, ids, codes = call(
        functools.partial(score_kernel, per, capacity),
        (shape((held, LANES), F32), shape((LANES, held), F32), shape((LANES, held), F32)),
        mac * features,
        2 * slots * width,
        (message, dec_rows),
        scratch_shapes=[pltpu.VMEM((slots, width), BF16)],
    )
    parts = jnp.broadcast_to((score * SCALE).astype(jnp.float16), (slices, held, LANES))
    parts = lax.all_to_all(parts, "tok", split_axis=0, concat_axis=0, tiled=True)
    score = jnp.sum(parts.astype(F32), axis=0) * (1.0 / SCALE)
    pre, back = call(
        functools.partial(back_kernel, per),
        (shape((features, slots), BF16), shape((slots, width), BF16)),
        mac * features,
        2 * slots * width,
        (score, ids, enc_rows),
    )
    returned = lax.all_to_all(
        back.reshape(groups, capacity, width), "feat", split_axis=0, concat_axis=0, tiled=True
    ).reshape(slots, width)
    dec_grad = call(
        functools.partial(dec_kernel, per, capacity),
        shape((features, width), BF16),
        mac * features,
        4 * slots * width,
        (ids, codes, message),
        scratch_shapes=[pltpu.VMEM((slots, width), BF16)],
    )
    steps = groups // DEVICES_A_STEP
    enc_grad, mark = call(
        functools.partial(enc_kernel, capacity, tokens),
        (shape((features, width), BF16), shape((8, LANES), F32)),
        2 * groups * tokens * features * width,
        2 * groups * tokens * width,
        (pre, wide),
        grid=(steps,),
        in_specs=[
            pl.BlockSpec((features, slots), lambda i: (0, 0)),
            pl.BlockSpec((DEVICES_A_STEP, wide_lines, LANES), lambda i: (i, 0, 0)),
        ],
        out_specs=(
            pl.BlockSpec((features, width), lambda i: (0, 0)),
            pl.BlockSpec((8, LANES), lambda i: (0, 0)),
        ),
        scratch_shapes=[
            pltpu.VMEM((slots, features), BF16),
            pltpu.VMEM((features, width), F32),
            pltpu.VMEM((DEVICES_A_STEP * tokens, width), BF16),
        ],
    )
    in_grad = call(
        functools.partial(merge_kernel, groups, capacity),
        shape((tokens, width), BF16),
        mac * tokens,
        4 * slots * width,
        (dest, returned),
        (mark,),
    )
    return (enc_grad, dec_grad, in_grad)


def solution(mesh):
    split = P("feat", "tok")
    return jax.shard_map(
        shards,
        mesh=mesh,
        in_specs=(split, split, split, split, P("feat", None), P("feat", None, None), P("feat", None, None)),
        out_specs=(split, split, split),
        check_vma=False,
    )
```

time: 191 us -> 187 us (0.979)
  waiting for transfers between devices: 42.1 us -> 45.3 us
  blocking collectives: 107 us -> 104 us
  Pallas kernels: 19 us -> 16.9 us
    all_gather x1, waiting for transfers between devices: 28.4 us -> 32.8 us  [shards(): wide = lax.all_gather(wide, 'feat', axis=0)]
    all_to_all x1, blocking collectives: 90.3 us -> 86.2 us  [shards(): lax.all_to_all(message, 'feat', split_axis=0, concat_axis=0, tiled=True)]
    pallas_call x6, Pallas kernels: 19 us -> 16.9 us  [call(): pl.pallas_call(body, out_shape=outs, in_specs=list(specs) + [pl.BlockSpec...]
  transfers between devices with their start and end apart: 2 -> 2, of which waited for: 2 -> 2; matrix products, arithmetic and copies ran while one was open for 0% -> 0% of each run, Pallas kernels for 9% -> 7%
where the time goes in v8:
time: 187 us; the launch traced here: 186 us
  blocking collectives  104 us (56%)
  waiting for transfers between devices  45.3 us (24%)
  Pallas kernels  16.9 us (9%)
  between operations  14.1 us (8%)
  starting transfers between devices  5.64 us (3%)
    all_to_all x1, blocking collectives, shards(): lax.all_to_all(message, 'feat', split_axis=0, concat_axis=0, tiled=True)  86.2 us
    all_gather x1, waiting for transfers between devices, shards(): wide = lax.all_gather(wide, 'feat', axis=0)  32.8 us
    all_to_all x1, blocking collectives, shards(): lax.all_to_all(parts, 'tok', split_axis=0, concat_axis=0, tiled=True)  17.4 us
    pallas_call x6, Pallas kernels, call(): pl.pallas_call(body, out_shape=outs, in_specs=list(specs) + [pl.BlockSpec...  16.9 us
    all_to_all x1, waiting for transfers between devices, shards(): lax.all_to_all(back.reshape(groups, capacity, width), 'feat', split_axis=...  12.4 us
    all_to_all x1, starting transfers between devices, shards(): lax.all_to_all(back.reshape(groups, capacity, width), 'feat', split_axis=...  5.61 us
  transfers between devices with their start and end apart: 2, of which 2 were waited for; matrix products, arithmetic and copies ran while one was open for 0% of the time, Pallas kernels for 7%

profile of v8, /device:TPU:1, one launch (start us, length us, event | category | flops | bytes accessed | tf_op | source)
XLA Modules:
  0.0 185.7 jit_solution(400389999589820877)
XLA Ops:
  7.2 0.0 all-gather.3.cloned.1.call-start
  7.2 2.7 %shard_map.94 = (bf16[32,136,128]{2,1,0:T(8,128)(2,1)}, bf16[1040,128]{1,0:T(8,128)(2,1)}) custom-call(s32[2,128]{1,0:T(2,128)} %bitcast.7, s32[2,32,128]{2,1,0:T(8,128)} %bitcast.10, f32[2,32,128]{2,1,0:T(8,128)} %bitcast.11, bf16[128,1024]{1,0:T(8,128)(2,1)} %refs_3_.1, bf16[128,1024]{1,0:T(8,128)(2,1)} %refs_4_.1), custom_call_target="tpu_custom_call" | custom-call | flops 134217728 | bytes 1572864 | tf_op jit(solution)/shard_map/pallas_call | solution.py:28
  10.0 0.0 all-gather.3.cloned.1.call-update
  10.0 0.0 copy-start
  10.0 86.2 %all_to_all.15.refs_0_.refs_2_ = bf16[32,136,128]{2,1,0:T(8,128)(2,1)S(1)} all-to-all(bf16[32,136,128]{2,1,0:T(8,128)(2,1)} %get-tuple-element.12), channel_id=1, replica_groups=mesh['feat'=32,'tok'=16] {'feat'}, dimensions={0} | all-to-all | bytes 2228224 | tf_op jit(solution)/shard_map/all_to_all | solution.py:260
  96.2 0.0 copy-done
  96.2 0.9 shard_map.95
  97.1 0.0 copy-start.2
  97.2 0.1 broadcast_in_dim.3
  97.3 17.4 %all_to_all.16 = f16[16,128,128]{2,1,0:T(8,128)(2,1)S(1)} all-to-all(f16[16,128,128]{2,1,0:T(8,128)(2,1)S(1)} %broadcast_in_dim.3), channel_id=1, replica_groups=mesh['feat'=32,'tok'=16] {'tok'}, dimensions={0} | all-to-all | bytes 1048576 | tf_op jit(solution)/shard_map/all_to_all | solution.py:271
  114.7 0.1 convert_reduce_fusion
  114.7 0.0 copy-done.2
  114.8 2.7 %shard_map.96 = (bf16[256,512]{1,0:T(8,128)(2,1)S(1)}, bf16[512,1024]{1,0:T(8,128)(2,1)}) custom-call(f32[128,128]{1,0:T(8,128)S(1)} %broadcast_multiply_fusion.refs_0_, f32[128,128]{1,0:T(8,128)S(1)} %get-tuple-element.14.refs_1_.refs_0_, bf16[256,1024]{1,0:T(8,128)(2,1)S(1)} %copy-done.2), custom_call_target="tpu_custom_call" | custom-call | flops 268435456 | bytes 1048576 | tf_op jit(solution)/shard_map/pallas_call | solution.py:28
  117.4 5.6 %all-to-all-start.2 = ((bf16[32,16,1024]{2,1,0:T(8,128)(2,1)}), bf16[32,16,1024]{2,1,0:T(8,128)(2,1)S(1)}, u32[]{:S(2)}, u32[]{:S(2)}) async-start(bf16[32,16,1024]{2,1,0:T(8,128)(2,1)} %bitcast.4), calls=%async_computation.2 | async-start | bytes 2097152 | tf_op jit(solution)/shard_map/all_to_all | solution.py:280
  123.0 2.3 %shard_map.98 = bf16[256,1024]{1,0:T(8,128)(2,1)} custom-call(f32[128,128]{1,0:T(8,128)S(1)} %get-tuple-element.14.refs_1_.refs_0_, f32[128,128]{1,0:T(8,128)S(1)} %get-tuple-element.18.refs_1_, bf16[32,136,128]{2,1,0:T(8,128)(2,1)S(1)} %all_to_all.15.refs_0_.refs_2_), custom_call_target="tpu_custom_call" | custom-call | flops 268435456 | bytes 2097152 | tf_op jit(solution)/shard_map/pallas_call | solution.py:28
  125.4 32.8 %all-gather.3.cloned.1.call-done = bf16[33280,128]{1,0:T(8,128)(2,1)} async-done(((bf16[1040,128]{1,0:T(8,128)(2,1)}), bf16[33280,128]{1,0:T(8,128)(2,1)}) %all-gather.3.cloned.1.call-update) | async-done | bytes 8519696 | tf_op jit(solution)/shard_map/all_gather | solution.py:259
  158.2 0.0 copy-start.1
  158.2 7.1 %shard_map.97 = (bf16[256,1024]{1,0:T(8,128)(2,1)}, f32[8,128]{1,0:T(8,128)S(1)}) custom-call(bf16[256,512]{1,0:T(8,128)(2,1)S(1)} %get-tuple-element.15.refs_0_, bf16[32,1040,128]{2,1,0:T(8,128)(2,1)} %bitcast.9), custom_call_target="tpu_custom_call" | custom-call | flops 2147483648 | bytes 8388608 | tf_op jit(solution)/shard_map/pallas_call | solution.py:28
  165.3 12.4 %all-to-all-done.2 = bf16[32,16,1024]{2,1,0:T(8,128)(2,1)S(1)} async-done(((bf16[32,16,1024]{2,1,0:T(8,128)(2,1)}), bf16[32,16,1024]{2,1,0:T(8,128)(2,1)S(1)}, u32[]{:S(2)}, u32[]{:S(2)}) %all-to-all-start.2) | async-done | bytes 1048608 | tf_op jit(solution)/shard_map/all_to_all | solution.py:280
  177.7 0.0 copy-done.1
  177.7 1.2 shard_map.99
  (2 shorter events, 0.0 us)
Async XLA Ops:
  7.2 151.0 %all-gather.3.cloned.1.call-start = ((), (), s32[]{:S(2)}) async-start(), calls=%async_computation.3 | async-start | bytes 8785920 | tf_op jit(solution)/shard_map/all_gather | solution.py:259
  10.0 86.3 %copy-start = (bf16[256,1024]{1,0:T(8,128)(2,1)S(1)}, bf16[256,1024]{1,0:T(8,128)(2,1)}, u32[]{:S(2)}) copy-start(bf16[256,1024]{1,0:T(8,128)(2,1)} %refs_1_.1) | copy-start | bytes 1572868
  97.1 17.6 %copy-start.2 = (bf16[256,1024]{1,0:T(8,128)(2,1)S(1)}, bf16[256,1024]{1,0:T(8,128)(2,1)}, u32[]{:S(2)}) copy-start(bf16[256,1024]{1,0:T(8,128)(2,1)} %refs_2_.1) | copy-start | bytes 1572868
  117.4 60.3 %all-to-all-start.2 = ((bf16[32,16,1024]{2,1,0:T(8,128)(2,1)}), bf16[32,16,1024]{2,1,0:T(8,128)(2,1)S(1)}, u32[]{:S(2)}, u32[]{:S(2)}) async-start(bf16[32,16,1024]{2,1,0:T(8,128)(2,1)} %bitcast.4), calls=%async_computation.2 | async-start | bytes 2097152 | tf_op jit(solution)/shard_map/all_to_all | solution.py:280
  158.2 19.5 %copy-start.1 = (s32[128,2]{0,1:T(2,128)S(1)}, s32[128,2]{0,1:T(2,128)}, u32[]{:S(2)}) copy-start(s32[128,2]{0,1:T(2,128)} %param.11) | copy-start | bytes 3076
Sparse Core Ops, SparseCore 0:
  10.7 147.4 all-gather.2

commit v9 on v8

--- a/solution.py
+++ b/solution.py
@@ -11,7 +11,6 @@
 BF16 = jnp.bfloat16
 LANES = 128
 DEVICES_A_STEP = 8
-PARTS = 4
 SCALE = 128.0
 VMEM_BYTES = 48 * 1024 * 1024
 ROWS_ROWS = (((1,), (1,)), ((), ()))
@@ -64,8 +63,8 @@
     ]
 
 
-def pack_kernel(groups, capacity, dest_hbm, ids_hbm, codes_hbm, grads_hbm, inputs_hbm, message_hbm, wide_hbm, *scratch):
-    dest_ref, ids_ref, codes_ref, grads_ref, message_ref, wide_ref, sems = scratch
+def pack_kernel(groups, capacity, dest_hbm, ids_hbm, codes_hbm, grads_hbm, inputs_hbm, message_ref, wide_hbm, *scratch):
+    dest_ref, ids_ref, codes_ref, grads_ref, wide_ref, sems = scratch
     tokens, width = grads_ref.shape
     pairs = (
         (dest_hbm, dest_ref),
@@ -93,8 +92,8 @@
     wide_ref[blocks * tokens :, :] = jnp.concatenate(info, axis=0).astype(BF16)
     for copy in copies[4:]:
         copy.wait()
-    sends = [pltpu.make_async_copy(wide_ref, wide_hbm, sems.at[len(copies)])]
-    sends[0].start()
+    send = pltpu.make_async_copy(wide_ref, wide_hbm, sems.at[len(copies)])
+    send.start()
     notes = jnp.zeros((groups * capacity, LANES), F32)
     rest = jnp.zeros((LANES - 2 * per, tokens), F32)
     copies[1].wait()
@@ -108,20 +107,11 @@
     high = pltpu.roll(notes[:, half:, :].reshape(groups * half, LANES), 2 * per, 1)
     message_ref[:, blocks * capacity :, :] = (low + high).astype(BF16).reshape(groups, half, LANES)
     copies[3].wait()
-    some = groups // PARTS
-    for part in range(PARTS):
-        lines = slice(part * some * capacity, (part + 1) * some * capacity)
-        here = slice(part * some, (part + 1) * some)
-        rows = jnp.dot(pick[lines], grads_ref[...], preferred_element_type=F32).astype(BF16)
-        for block in range(blocks):
-            column = rows[:, block * LANES : (block + 1) * LANES]
-            message_ref[here, block * capacity : (block + 1) * capacity, :] = column.reshape(some, capacity, LANES)
-        sends.append(
-            pltpu.make_async_copy(message_ref.at[here], message_hbm.at[here], sems.at[len(copies) + 1 + part])
-        )
-        sends[-1].start()
-    for send in sends:
-        send.wait()
+    rows = jnp.dot(pick, grads_ref[...], preferred_element_type=F32).astype(BF16)
+    for block in range(blocks):
+        column = rows[:, block * LANES : (block + 1) * LANES]
+        message_ref[:, block * capacity : (block + 1) * capacity, :] = column.reshape(groups, capacity, LANES)
+    send.wait()
 
 
 def unpack(message_ref, capacity, line_ref):
@@ -162,14 +152,18 @@
 
 def spread(ids, values, features, per):
     held = ids.shape[1]
-    feature_line = lax.broadcasted_iota(jnp.int32, (features, held), 0).astype(F32)
+    feature_line = lax.broadcasted_iota(jnp.int32, (features, held), 0).astype(F32).astype(BF16)
     blocks = []
     for q in range(LANES // per):
-        block = jnp.zeros((features, held), F32)
+        block = jnp.zeros((features, held), BF16)
         for j in range(q * per, (q + 1) * per):
-            block = jnp.where(feature_line == ids[j : j + 1, :], values[j : j + 1, :], block)
+            here, value = (
+                jnp.concatenate([jnp.broadcast_to(a[j : j + 1, :], (16, held)).astype(BF16)] * (features // 16), axis=0)
+                for a in (ids, values)
+            )
+            block = jnp.where(feature_line == here, value, block)
         blocks.append(block)
-    return jnp.concatenate(blocks, axis=1).astype(BF16)
+    return jnp.concatenate(blocks, axis=1)
 
 
 def back_kernel(per, score_ref, ids_ref, enc_ref, pre_ref, back_ref):
@@ -179,7 +173,8 @@
     back_ref[...] = lax.dot_general(pre, enc_ref[...], DEPTH_FIRST, preferred_element_type=F32).astype(BF16)
 
 
-def dec_kernel(per, capacity, ids_ref, codes_ref, message_ref, out_ref, line_ref):
+def dec_kernel(per, groups, capacity, ids_ref, codes_ref, message_ref, dest_ref, out_ref, pick_ref, line_ref):
+    pick_ref[...] = functools.reduce(jnp.add, pick_matrices(dest_ref, groups, capacity)).T
     unpack(message_ref, capacity, line_ref)
     code = spread(ids_ref[...], codes_ref[...], out_ref.shape[0], per)
     out_ref[...] = jnp.dot(code, line_ref[...], preferred_element_type=F32).astype(BF16)
@@ -217,10 +212,8 @@
         out_ref[...] = total_ref[...].astype(BF16)
 
 
-def merge_kernel(groups, capacity, dest_ref, back_ref, out_ref):
-    picks = pick_matrices(dest_ref, groups, capacity)
-    pick = functools.reduce(jnp.add, picks)
-    out_ref[...] = lax.dot_general(pick, back_ref[...], DEPTH_FIRST, preferred_element_type=F32).astype(BF16)
+def merge_kernel(pick_ref, back_ref, out_ref):
+    out_ref[...] = jnp.dot(pick_ref[...], back_ref[...], preferred_element_type=F32).astype(BF16)
 
 
 def shards(enc_rows, dec_rows, inputs, out_grad, destinations, local_ids, code_values):
@@ -245,15 +238,14 @@
         (dest, jnp.transpose(local_ids, (1, 2, 0)), jnp.transpose(code_values, (1, 2, 0)), out_grad, inputs),
         limit=None,
         in_specs=[pl.BlockSpec(memory_space=pl.ANY)] * 5,
-        out_specs=(pl.BlockSpec(memory_space=pl.ANY), pl.BlockSpec(memory_space=pl.ANY)),
+        out_specs=(pl.BlockSpec(memory_space=pltpu.VMEM), pl.BlockSpec(memory_space=pl.ANY)),
         scratch_shapes=[
             pltpu.VMEM((hops, tokens), jnp.int32),
             pltpu.VMEM((hops, per, tokens), jnp.int32),
             pltpu.VMEM((hops, per, tokens), F32),
             pltpu.VMEM((tokens, width), BF16),
-            pltpu.VMEM((groups, lines, LANES), BF16),
             pltpu.VMEM((wide_lines, LANES), BF16),
-            pltpu.SemaphoreType.DMA((5 + width // LANES + PARTS,)),
+            pltpu.SemaphoreType.DMA((5 + width // LANES,)),
         ],
     )
     wide = lax.all_gather(wide, "feat", axis=0)
@@ -280,12 +272,12 @@
     returned = lax.all_to_all(
         back.reshape(groups, capacity, width), "feat", split_axis=0, concat_axis=0, tiled=True
     ).reshape(slots, width)
-    dec_grad = call(
-        functools.partial(dec_kernel, per, capacity),
-        shape((features, width), BF16),
+    dec_grad, pick = call(
+        functools.partial(dec_kernel, per, groups, capacity),
+        (shape((features, width), BF16), shape((tokens, slots), BF16)),
         mac * features,
         4 * slots * width,
-        (ids, codes, message),
+        (ids, codes, message, dest),
         scratch_shapes=[pltpu.VMEM((slots, width), BF16)],
     )
     steps = groups // DEVICES_A_STEP
@@ -311,11 +303,11 @@
         ],
     )
     in_grad = call(
-        functools.partial(merge_kernel, groups, capacity),
+        merge_kernel,
         shape((tokens, width), BF16),
         mac * tokens,
         4 * slots * width,
-        (dest, returned),
+        (pick, returned),
         (mark,),
     )
     return (enc_grad, dec_grad, in_grad)

time: 187 us -> 187 us (level)
  waiting for transfers between devices: 45.3 us -> 47.3 us
    all_to_all x1, waiting for transfers between devices: 12.4 us -> 14.6 us  [shards(): lax.all_to_all(back.reshape(groups, capacity, width), 'feat', split_axis=...]
  transfers between devices with their start and end apart: 2 -> 2, of which waited for: 2 -> 2; matrix products, arithmetic and copies ran while one was open for 0% -> 0% of each run, Pallas kernels for 7% -> 6%
where the time goes in v9:
time: 187 us
  blocking collectives  104 us (56%)
  waiting for transfers between devices  47.3 us (25%)
  Pallas kernels  15.9 us (9%)
  between operations  14.1 us (8%)
  starting transfers between devices  5.76 us (3%)
    all_to_all x1, blocking collectives, shards(): lax.all_to_all(message, 'feat', split_axis=0, concat_axis=0, tiled=True)  86.5 us
    all_gather x1, waiting for transfers between devices, shards(): wide = lax.all_gather(wide, 'feat', axis=0)  32.7 us
    all_to_all x1, blocking collectives, shards(): lax.all_to_all(parts, 'tok', split_axis=0, concat_axis=0, tiled=True)  17.3 us
    pallas_call x6, Pallas kernels, call(): pl.pallas_call(body, out_shape=outs, in_specs=list(specs) + [pl.BlockSpec...  15.9 us
    all_to_all x1, waiting for transfers between devices, shards(): lax.all_to_all(back.reshape(groups, capacity, width), 'feat', split_axis=...  14.6 us
    all_to_all x1, starting transfers between devices, shards(): lax.all_to_all(back.reshape(groups, capacity, width), 'feat', split_axis=...  5.72 us
  transfers between devices with their start and end apart: 2, of which 2 were waited for; matrix products, arithmetic and copies ran while one was open for 0% of the time, Pallas kernels for 6%

profile of v9, /device:TPU:1, one launch (start us, length us, event | category | flops | bytes accessed | tf_op | source)
XLA Modules:
  0.0 187.0 jit_solution(12796473211975397414)
XLA Ops:
  7.2 0.0 all-gather.3.cloned.1.call-start
  7.2 2.9 %shard_map.94 = (bf16[32,136,128]{2,1,0:T(8,128)(2,1)}, bf16[1040,128]{1,0:T(8,128)(2,1)}) custom-call(s32[2,128]{1,0:T(2,128)} %bitcast.7, s32[2,32,128]{2,1,0:T(8,128)} %bitcast.10, f32[2,32,128]{2,1,0:T(8,128)} %bitcast.11, bf16[128,1024]{1,0:T(8,128)(2,1)} %refs_3_.1, bf16[128,1024]{1,0:T(8,128)(2,1)} %refs_4_.1), custom_call_target="tpu_custom_call" | custom-call | flops 134217728 | bytes 1572864 | tf_op jit(solution)/shard_map/pallas_call | solution.py:27
  10.1 0.0 all-gather.3.cloned.1.call-update
  10.1 0.0 copy-start
  10.2 86.5 %all_to_all.15.refs_0_.refs_2_ = bf16[32,136,128]{2,1,0:T(8,128)(2,1)S(1)} all-to-all(bf16[32,136,128]{2,1,0:T(8,128)(2,1)} %get-tuple-element.14), channel_id=1, replica_groups=mesh['feat'=32,'tok'=16] {'feat'}, dimensions={0} | all-to-all | bytes 2228224 | tf_op jit(solution)/shard_map/all_to_all | solution.py:252
  96.6 0.0 copy-done
  96.6 0.9 shard_map.95
  97.5 0.0 copy-start.2
  97.5 0.1 broadcast_in_dim.3
  97.7 17.3 %all_to_all.16 = f16[16,128,128]{2,1,0:T(8,128)(2,1)S(1)} all-to-all(f16[16,128,128]{2,1,0:T(8,128)(2,1)S(1)} %broadcast_in_dim.3), channel_id=1, replica_groups=mesh['feat'=32,'tok'=16] {'tok'}, dimensions={0} | all-to-all | bytes 1048576 | tf_op jit(solution)/shard_map/all_to_all | solution.py:263
  115.0 0.1 convert_reduce_fusion
  115.0 0.0 copy-done.2
  115.1 2.1 %shard_map.96 = (bf16[256,512]{1,0:T(8,128)(2,1)S(1)}, bf16[512,1024]{1,0:T(8,128)(2,1)}) custom-call(f32[128,128]{1,0:T(8,128)S(1)} %broadcast_multiply_fusion.refs_0_, f32[128,128]{1,0:T(8,128)S(1)} %get-tuple-element.16.refs_1_.refs_0_, bf16[256,1024]{1,0:T(8,128)(2,1)S(1)} %copy-done.2), custom_call_target="tpu_custom_call" | custom-call | flops 268435456 | bytes 1048576 | tf_op jit(solution)/shard_map/pallas_call | solution.py:27
  117.2 0.0 copy-start.1
  117.2 5.7 %all-to-all-start.2 = ((bf16[32,16,1024]{2,1,0:T(8,128)(2,1)}), bf16[32,16,1024]{2,1,0:T(8,128)(2,1)S(1)}, u32[]{:S(2)}, u32[]{:S(2)}) async-start(bf16[32,16,1024]{2,1,0:T(8,128)(2,1)} %bitcast.4), calls=%async_computation.2 | async-start | bytes 2097152 | tf_op jit(solution)/shard_map/all_to_all | solution.py:272
  122.9 0.0 copy-done.1
  122.9 1.9 %shard_map.98 = (bf16[256,1024]{1,0:T(8,128)(2,1)}, bf16[128,512]{1,0:T(8,128)(2,1)S(1)}) custom-call(f32[128,128]{1,0:T(8,128)S(1)} %get-tuple-element.16.refs_1_.refs_0_, f32[128,128]{1,0:T(8,128)S(1)} %get-tuple-element.20.refs_1_, bf16[32,136,128]{2,1,0:T(8,128)(2,1)S(1)} %all_to_all.15.refs_0_.refs_2_, s32[2,128]{1,0:T(2,128)S(1)} %bitcast.8), custom_call_target="tpu_custom_call" | custom-call | flops 268435456 | bytes 2097152 | tf_op jit(solution)/shard_map/pallas_call | solution.py:27
  124.8 32.7 %all-gather.3.cloned.1.call-done = bf16[33280,128]{1,0:T(8,128)(2,1)} async-done(((bf16[1040,128]{1,0:T(8,128)(2,1)}), bf16[33280,128]{1,0:T(8,128)(2,1)}) %all-gather.3.cloned.1.call-update) | async-done | bytes 8519696 | tf_op jit(solution)/shard_map/all_gather | solution.py:251
  157.5 7.1 %shard_map.97 = (bf16[256,1024]{1,0:T(8,128)(2,1)}, f32[8,128]{1,0:T(8,128)S(1)}) custom-call(bf16[256,512]{1,0:T(8,128)(2,1)S(1)} %get-tuple-element.17.refs_0_, bf16[32,1040,128]{2,1,0:T(8,128)(2,1)} %bitcast.9), custom_call_target="tpu_custom_call" | custom-call | flops 2147483648 | bytes 8388608 | tf_op jit(solution)/shard_map/pallas_call | solution.py:27
  164.5 14.6 %all-to-all-done.2 = bf16[32,16,1024]{2,1,0:T(8,128)(2,1)S(1)} async-done(((bf16[32,16,1024]{2,1,0:T(8,128)(2,1)}), bf16[32,16,1024]{2,1,0:T(8,128)(2,1)S(1)}, u32[]{:S(2)}, u32[]{:S(2)}) %all-to-all-start.2) | async-done | bytes 1048608 | tf_op jit(solution)/shard_map/all_to_all | solution.py:272
  179.1 1.0 shard_map.99
  (2 shorter events, 0.0 us)
Async XLA Ops:
  7.2 150.3 %all-gather.3.cloned.1.call-start = ((), (), s32[]{:S(2)}) async-start(), calls=%async_computation.3 | async-start | bytes 8785920 | tf_op jit(solution)/shard_map/all_gather | solution.py:251
  10.1 86.5 %copy-start = (bf16[256,1024]{1,0:T(8,128)(2,1)S(1)}, bf16[256,1024]{1,0:T(8,128)(2,1)}, u32[]{:S(2)}) copy-start(bf16[256,1024]{1,0:T(8,128)(2,1)} %refs_1_.1) | copy-start | bytes 1572868
  97.5 17.5 %copy-start.2 = (bf16[256,1024]{1,0:T(8,128)(2,1)S(1)}, bf16[256,1024]{1,0:T(8,128)(2,1)}, u32[]{:S(2)}) copy-start(bf16[256,1024]{1,0:T(8,128)(2,1)} %refs_2_.1) | copy-start | bytes 1572868
  117.2 5.7 %copy-start.1 = (s32[128,2]{0,1:T(2,128)S(1)}, s32[128,2]{0,1:T(2,128)}, u32[]{:S(2)}) copy-start(s32[128,2]{0,1:T(2,128)} %param.11) | copy-start | bytes 3076
  117.2 62.0 %all-to-all-start.2 = ((bf16[32,16,1024]{2,1,0:T(8,128)(2,1)}), bf16[32,16,1024]{2,1,0:T(8,128)(2,1)S(1)}, u32[]{:S(2)}, u32[]{:S(2)}) async-start(bf16[32,16,1024]{2,1,0:T(8,128)(2,1)} %bitcast.4), calls=%async_computation.2 | async-start | bytes 2097152 | tf_op jit(solution)/shard_map/all_to_all | solution.py:272
Sparse Core Ops, SparseCore 0:
  10.7 146.7 all-gather.2

commit v10 on v9

--- a/solution.py
+++ b/solution.py
@@ -166,11 +166,24 @@
     return jnp.concatenate(blocks, axis=1)
 
 
-def back_kernel(per, score_ref, ids_ref, enc_ref, pre_ref, back_ref):
-    rounded = score_ref[...].astype(BF16).astype(F32).T
-    pre = spread(ids_ref[...], rounded, enc_ref.shape[0], per)
-    pre_ref[...] = pre
-    back_ref[...] = lax.dot_general(pre, enc_ref[...], DEPTH_FIRST, preferred_element_type=F32).astype(BF16)
+def inverse_kernel(per, ids_ref, inverse_ref):
+    count, held = ids_ref.shape
+    lane = lax.broadcasted_iota(jnp.int32, (count, held), 0).astype(F32) + 1.0
+    inverse_ref[...] = spread(ids_ref[...], lane, inverse_ref.shape[1], per).astype(F32).T.astype(jnp.int32) - 1
+
+
+def back_kernel(score_ref, inverse_ref, enc_ref, pre_ref, back_ref):
+    held = score_ref.shape[0]
+    rounded = score_ref[...].astype(BF16).astype(F32)
+    slots, features = inverse_ref.shape
+    for q in range(slots // held):
+        for part in range(features // LANES):
+            lane = inverse_ref[q * held : (q + 1) * held, part * LANES : (part + 1) * LANES]
+            value = jnp.take_along_axis(rounded, jnp.maximum(lane, 0), axis=1)
+            pre_ref[q * held : (q + 1) * held, part * LANES : (part + 1) * LANES] = jnp.where(
+                lane >= 0, value, 0.0
+            ).astype(BF16)
+    back_ref[...] = jnp.dot(pre_ref[...], enc_ref[...], preferred_element_type=F32).astype(BF16)
 
 
 def dec_kernel(per, groups, capacity, ids_ref, codes_ref, message_ref, dest_ref, out_ref, pick_ref, line_ref):
@@ -180,12 +193,11 @@
     out_ref[...] = jnp.dot(code, line_ref[...], preferred_element_type=F32).astype(BF16)
 
 
-def enc_kernel(capacity, tokens, pre_ref, wide_ref, out_ref, mark_ref, turned_ref, total_ref, line_ref):
+def enc_kernel(capacity, tokens, pre_ref, wide_ref, out_ref, mark_ref, total_ref, line_ref):
     step = pl.program_id(0)
 
     @pl.when(step == 0)
     def _():
-        turned_ref[...] = pre_ref[...].T
         total_ref[...] = jnp.zeros_like(total_ref)
         mark_ref[...] = jnp.zeros_like(mark_ref)
 
@@ -203,8 +215,7 @@
         slots.append(jnp.where(info[0:1] == me, info[1:2] + device * capacity, slot))
     count = devices * capacity
     hot = one_hot(jnp.concatenate(slots, axis=1), count)
-    here = turned_ref[pl.ds(pl.multiple_of(step * count, count), count), :]
-    spread_out = lax.dot_general(here, hot, DEPTH_FIRST, preferred_element_type=F32).astype(BF16)
+    spread_out = lax.dot_general(pre_ref[...], hot, DEPTH_FIRST, preferred_element_type=F32).astype(BF16)
     total_ref[...] += jnp.dot(spread_out, line_ref[...], preferred_element_type=F32)
 
     @pl.when(step == pl.num_programs(0) - 1)
@@ -262,12 +273,19 @@
     parts = jnp.broadcast_to((score * SCALE).astype(jnp.float16), (slices, held, LANES))
     parts = lax.all_to_all(parts, "tok", split_axis=0, concat_axis=0, tiled=True)
     score = jnp.sum(parts.astype(F32), axis=0) * (1.0 / SCALE)
+    inverse = call(
+        functools.partial(inverse_kernel, per),
+        shape((slots, features), jnp.int32),
+        2 * slots * features * per,
+        4 * slots * features,
+        (ids,),
+    )
     pre, back = call(
-        functools.partial(back_kernel, per),
-        (shape((features, slots), BF16), shape((slots, width), BF16)),
+        back_kernel,
+        (shape((slots, features), BF16), shape((slots, width), BF16)),
         mac * features,
         2 * slots * width,
-        (score, ids, enc_rows),
+        (score, inverse, enc_rows),
     )
     returned = lax.all_to_all(
         back.reshape(groups, capacity, width), "feat", split_axis=0, concat_axis=0, tiled=True
@@ -289,7 +307,7 @@
         (pre, wide),
         grid=(steps,),
         in_specs=[
-            pl.BlockSpec((features, slots), lambda i: (0, 0)),
+            pl.BlockSpec((slots // steps, features), lambda i: (i, 0)),
             pl.BlockSpec((DEVICES_A_STEP, wide_lines, LANES), lambda i: (i, 0, 0)),
         ],
         out_specs=(
@@ -297,7 +315,6 @@
             pl.BlockSpec((8, LANES), lambda i: (0, 0)),
         ),
         scratch_shapes=[
-            pltpu.VMEM((slots, features), BF16),
             pltpu.VMEM((features, width), F32),
             pltpu.VMEM((DEVICES_A_STEP * tokens, width), BF16),
         ],

time: 187 us -> 187 us (level)
  blocking collectives: 104 us -> 86.5 us
  waiting for transfers between devices: 47.3 us -> 54.9 us
  starting transfers between devices: 5.76 us -> 12.8 us
    all_to_all x1 -> x0, blocking collectives: 17.3 us -> none  [shards(): lax.all_to_all(parts, 'tok', split_axis=0, concat_axis=0, tiled=True)]
    all_to_all x0 -> x1, waiting for transfers between devices: none -> 9.72 us  [shards(): lax.all_to_all(parts, 'tok', split_axis=0, concat_axis=0, tiled=True)]
    all_to_all x0 -> x1, starting transfers between devices: none -> 7.02 us  [shards(): lax.all_to_all(parts, 'tok', split_axis=0, concat_axis=0, tiled=True)]
    pallas_call x6 -> x7, Pallas kernels: 15.9 us -> 16.3 us  [call(): pl.pallas_call(body, out_shape=outs, in_specs=list(specs) + [pl.BlockSpec...]
  transfers between devices with their start and end apart: 2 -> 3, of which waited for: 2 -> 3; matrix products, arithmetic and copies ran while one was open for 0% -> 1% of each run, Pallas kernels for 6% -> 7%
where the time goes in v10:
time: 187 us; the launch traced here: 186 us
  blocking collectives  86.5 us (46%)
  waiting for transfers between devices  54.9 us (29%)
  Pallas kernels  16.3 us (9%)
  between operations  14.1 us (8%)
  starting transfers between devices  12.8 us (7%)
    all_to_all x1, blocking collectives, shards(): lax.all_to_all(message, 'feat', split_axis=0, concat_axis=0, tiled=True)  86.5 us
    all_gather x1, waiting for transfers between devices, shards(): wide = lax.all_gather(wide, 'feat', axis=0)  32 us
    pallas_call x7, Pallas kernels, call(): pl.pallas_call(body, out_shape=outs, in_specs=list(specs) + [pl.BlockSpec...  16.3 us
    all_to_all x1, waiting for transfers between devices, shards(): lax.all_to_all(back.reshape(groups, capacity, width), 'feat', split_axis=...  13.1 us
    all_to_all x1, waiting for transfers between devices, shards(): lax.all_to_all(parts, 'tok', split_axis=0, concat_axis=0, tiled=True)  9.72 us
    all_to_all x1, starting transfers between devices, shards(): lax.all_to_all(parts, 'tok', split_axis=0, concat_axis=0, tiled=True)  7.02 us
    all_to_all x1, starting transfers between devices, shards(): lax.all_to_all(back.reshape(groups, capacity, width), 'feat', split_axis=...  5.71 us
  transfers between devices with their start and end apart: 3, of which 3 were waited for; matrix products, arithmetic and copies ran while one was open for 1% of the time, Pallas kernels for 7%

profile of v10, /device:TPU:1, one launch (start us, length us, event | category | flops | bytes accessed | tf_op | source)
XLA Modules:
  0.0 185.5 jit_solution(15616115972333679247)
XLA Ops:
  7.2 0.0 all-gather.3.cloned.1.call-start
  7.2 2.9 %shard_map.94 = (bf16[32,136,128]{2,1,0:T(8,128)(2,1)}, bf16[1040,128]{1,0:T(8,128)(2,1)}) custom-call(s32[2,128]{1,0:T(2,128)} %bitcast.7, s32[2,32,128]{2,1,0:T(8,128)} %bitcast.10, f32[2,32,128]{2,1,0:T(8,128)} %bitcast.11, bf16[128,1024]{1,0:T(8,128)(2,1)} %refs_3_.1, bf16[128,1024]{1,0:T(8,128)(2,1)} %refs_4_.1), custom_call_target="tpu_custom_call" | custom-call | flops 134217728 | bytes 1572864 | tf_op jit(solution)/shard_map/pallas_call | solution.py:27
  10.1 0.0 all-gather.3.cloned.1.call-update
  10.1 0.0 copy-start
  10.2 86.5 %all_to_all.15.refs_0_.refs_2_ = bf16[32,136,128]{2,1,0:T(8,128)(2,1)S(1)} all-to-all(bf16[32,136,128]{2,1,0:T(8,128)(2,1)} %get-tuple-element.14), channel_id=1, replica_groups=mesh['feat'=32,'tok'=16] {'feat'}, dimensions={0} | all-to-all | bytes 2228224 | tf_op jit(solution)/shard_map/all_to_all | solution.py:263
  96.6 0.0 copy-done
  96.6 0.9 shard_map.95
  97.5 0.9 broadcast_in_dim.3
  98.4 0.0 copy-start.1
  98.4 7.0 %all-to-all-start.1 = ((f16[16,128,128]{2,1,0:T(8,128)(2,1)}), f16[16,128,128]{2,1,0:T(8,128)(2,1)S(1)}, u32[]{:S(2)}, u32[]{:S(2)}) async-start(f16[16,128,128]{2,1,0:T(8,128)(2,1)} %broadcast_in_dim.3), calls=%async_computation.1 | async-start | bytes 1048576 | tf_op jit(solution)/shard_map/all_to_all | solution.py:274
  105.5 0.8 shard_map.96.refs_1_
  106.2 9.7 %all-to-all-done.1 = f16[16,128,128]{2,1,0:T(8,128)(2,1)S(1)} async-done(((f16[16,128,128]{2,1,0:T(8,128)(2,1)}), f16[16,128,128]{2,1,0:T(8,128)(2,1)S(1)}, u32[]{:S(2)}, u32[]{:S(2)}) %all-to-all-start.1) | async-done | bytes 524320 | tf_op jit(solution)/shard_map/all_to_all | solution.py:274
  116.0 0.1 convert_reduce_fusion
  116.0 0.0 copy-done.1
  116.1 1.9 %shard_map.97 = (bf16[512,256]{1,0:T(8,128)(2,1)S(1)}, bf16[512,1024]{1,0:T(8,128)(2,1)}) custom-call(f32[128,128]{1,0:T(8,128)S(1)} %broadcast_multiply_fusion.refs_0_, s32[512,256]{1,0:T(8,128)S(1)} %shard_map.96.refs_1_, bf16[256,1024]{1,0:T(8,128)(2,1)S(1)} %copy-done.1), custom_call_target="tpu_custom_call" | custom-call | flops 268435456 | bytes 1048576 | tf_op jit(solution)/shard_map/pallas_call | solution.py:27
  117.9 0.0 copy-start.2
  117.9 5.7 %all-to-all-start.2 = ((bf16[32,16,1024]{2,1,0:T(8,128)(2,1)}), bf16[32,16,1024]{2,1,0:T(8,128)(2,1)S(1)}, u32[]{:S(2)}, u32[]{:S(2)}) async-start(bf16[32,16,1024]{2,1,0:T(8,128)(2,1)} %bitcast.4), calls=%async_computation.2 | async-start | bytes 2097152 | tf_op jit(solution)/shard_map/all_to_all | solution.py:290
  123.6 0.0 copy-done.2
  123.6 1.9 %shard_map.99 = (bf16[256,1024]{1,0:T(8,128)(2,1)}, bf16[128,512]{1,0:T(8,128)(2,1)S(1)}) custom-call(f32[128,128]{1,0:T(8,128)S(1)} %get-tuple-element.16.refs_0_, f32[128,128]{1,0:T(8,128)S(1)} %get-tuple-element.20.refs_1_, bf16[32,136,128]{2,1,0:T(8,128)(2,1)S(1)} %all_to_all.15.refs_0_.refs_2_, s32[2,128]{1,0:T(2,128)S(1)} %bitcast.8), custom_call_target="tpu_custom_call" | custom-call | flops 268435456 | bytes 2097152 | tf_op jit(solution)/shard_map/pallas_call | solution.py:27
  125.5 32.0 %all-gather.3.cloned.1.call-done = bf16[33280,128]{1,0:T(8,128)(2,1)} async-done(((bf16[1040,128]{1,0:T(8,128)(2,1)}), bf16[33280,128]{1,0:T(8,128)(2,1)}) %all-gather.3.cloned.1.call-update) | async-done | bytes 8519696 | tf_op jit(solution)/shard_map/all_gather | solution.py:262
  157.6 7.0 %shard_map.98 = (bf16[256,1024]{1,0:T(8,128)(2,1)}, f32[8,128]{1,0:T(8,128)S(1)}) custom-call(bf16[512,256]{1,0:T(8,128)(2,1)S(1)} %get-tuple-element.17.refs_0_, bf16[32,1040,128]{2,1,0:T(8,128)(2,1)} %bitcast.9), custom_call_target="tpu_custom_call" | custom-call | flops 2147483648 | bytes 8388608 | tf_op jit(solution)/shard_map/pallas_call | solution.py:27
  164.6 13.1 %all-to-all-done.2 = bf16[32,16,1024]{2,1,0:T(8,128)(2,1)S(1)} async-done(((bf16[32,16,1024]{2,1,0:T(8,128)(2,1)}), bf16[32,16,1024]{2,1,0:T(8,128)(2,1)S(1)}, u32[]{:S(2)}, u32[]{:S(2)}) %all-to-all-start.2) | async-done | bytes 1048608 | tf_op jit(solution)/shard_map/all_to_all | solution.py:290
  177.7 1.0 shard_map.100
  (2 shorter events, 0.0 us)
Async XLA Ops:
  7.2 150.4 %all-gather.3.cloned.1.call-start = ((), (), s32[]{:S(2)}) async-start(), calls=%async_computation.3 | async-start | bytes 8785920 | tf_op jit(solution)/shard_map/all_gather | solution.py:262
  10.1 86.5 %copy-start = (bf16[256,1024]{1,0:T(8,128)(2,1)S(1)}, bf16[256,1024]{1,0:T(8,128)(2,1)}, u32[]{:S(2)}) copy-start(bf16[256,1024]{1,0:T(8,128)(2,1)} %refs_1_.1) | copy-start | bytes 1572868
  98.4 17.6 %copy-start.1 = (bf16[256,1024]{1,0:T(8,128)(2,1)S(1)}, bf16[256,1024]{1,0:T(8,128)(2,1)}, u32[]{:S(2)}) copy-start(bf16[256,1024]{1,0:T(8,128)(2,1)} %refs_2_.1) | copy-start | bytes 1572868
  98.4 17.5 %all-to-all-start.1 = ((f16[16,128,128]{2,1,0:T(8,128)(2,1)}), f16[16,128,128]{2,1,0:T(8,128)(2,1)S(1)}, u32[]{:S(2)}, u32[]{:S(2)}) async-start(f16[16,128,128]{2,1,0:T(8,128)(2,1)} %broadcast_in_dim.3), calls=%async_computation.1 | async-start | bytes 1048576 | tf_op jit(solution)/shard_map/all_to_all | solution.py:274
  117.9 5.7 %copy-start.2 = (s32[128,2]{0,1:T(2,128)S(1)}, s32[128,2]{0,1:T(2,128)}, u32[]{:S(2)}) copy-start(s32[128,2]{0,1:T(2,128)} %param.11) | copy-start | bytes 3076
  117.9 59.8 %all-to-all-start.2 = ((bf16[32,16,1024]{2,1,0:T(8,128)(2,1)}), bf16[32,16,1024]{2,1,0:T(8,128)(2,1)S(1)}, u32[]{:S(2)}, u32[]{:S(2)}) async-start(bf16[32,16,1024]{2,1,0:T(8,128)(2,1)} %bitcast.4), calls=%async_computation.2 | async-start | bytes 2097152 | tf_op jit(solution)/shard_map/all_to_all | solution.py:290
Sparse Core Ops, SparseCore 0:
  10.7 146.8 all-gather.2
